TPU v7x, 32 devices: a whole 2x2x4 slice. The times are simulated.
32 devices in a mesh: rows: 8 (over y, x, core), blk: 4 (over z).
Axes of the slice: x: 2, y: 2, z: 4, core: 2. Of those that a mesh axis runs over, the one named last changes fastest.
Arguments:
- tokens: bfloat16 [8, 512, 2048], P('rows', 'blk'), may hold values from -6 to 6
- segment_ids: int32 [8, 512], P('rows'), may hold values from 0 to 3, as said below
- mixer_gain: bfloat16 [2048], P(('rows', 'blk')), may hold values from 0.5 to 1.5
- branch_weight: bfloat16 [2048, 2736], P(('rows', 'blk')), may hold values from -0.125 to 0.125
- input_weight: bfloat16 [2048, 2736], P(('rows', 'blk')), may hold values from -0.125 to 0.125
- output_weight: bfloat16 [2048, 2736], P(('rows', 'blk')), may hold values from -0.3125 to 0.3125
- conv_weight: float32 [4, 2736], P(None, 'blk'), may hold values from -3 to 3
- conv_bias: float32 [2736], P('blk'), may hold values from -2 to 2
- decay_gate: float32 [16, 171, 171], P('blk'), may hold values from -0.4375 to 0.4375
- decay_bias: float32 [2736], P('blk'), may hold values from -3 to 3
- input_gate: float32 [16, 171, 171], P('blk'), may hold values from -0.4375 to 0.4375
- input_bias: float32 [2736], P('blk'), may hold values from -3 to 3
- decay_param: float32 [2736], P('blk')
- mlp_gain: bfloat16 [2048], P(('rows', 'blk')), may hold values from 0.5 to 1.5
- hidden_gate: bfloat16 [6144, 2048], P(('rows', 'blk')), may hold values from -0.125 to 0.125
- hidden_up: bfloat16 [6144, 2048], P(('rows', 'blk')), may hold values from -0.125 to 0.125
- hidden_down: bfloat16 [6144, 2048], P(('rows', 'blk')), may hold values from -0.109375 to 0.109375
- cotangent: bfloat16 [8, 512, 2048], P('rows', 'blk'), may hold values from -6 to 6
Outputs:
- block_out: bfloat16 [8, 512, 2048], P('rows', 'blk')
- token_grad: float32 [8, 512, 2048], P('rows', 'blk')
- mixer_gain_grad: float32 [2048], P(('rows', 'blk'))
- branch_weight_grad: float32 [2048, 2736], P(('rows', 'blk'))
- input_weight_grad: float32 [2048, 2736], P(('rows', 'blk'))
- output_weight_grad: float32 [2048, 2736], P(('rows', 'blk'))
- conv_weight_grad: float32 [4, 2736], P(None, 'blk')
- conv_bias_grad: float32 [2736], P('blk')
- decay_gate_grad: float32 [16, 171, 171], P('blk')
- decay_bias_grad: float32 [2736], P('blk')
- input_gate_grad: float32 [16, 171, 171], P('blk')
- input_bias_grad: float32 [2736], P('blk')
- decay_param_grad: float32 [2736], P('blk')
- mlp_gain_grad: float32 [2048], P(('rows', 'blk'))
- hidden_gate_grad: float32 [6144, 2048], P(('rows', 'blk'))
- hidden_up_grad: float32 [6144, 2048], P(('rows', 'blk'))
- hidden_down_grad: float32 [6144, 2048], P(('rows', 'blk'))
Inputs may be any that keep to these rules, and one draw needn't show every extreme that they name: `segment_ids`: segment ids never fall along a row.
All inputs are finite; a program needn't handle non-finite values.
Results may differ from a plain program's by a relative error of at most 0.01.
Values may be sent and summed in bfloat16 or wider, within the bound.
No kernel may reach another device: no remote copies, remote signals or barrier semaphores. Data moves between devices by JAX's collectives and lax.ppermute only.
A program may use at most 832 MiB of HBM per device.

v0:
```python
import jax
import jax.numpy as jnp
from jax import lax
from jax.sharding import PartitionSpec as P

epsilon = 1e-06
scale_c = 8.0
highest = lax.Precision.HIGHEST


def rms_unit(values):
    return values * lax.rsqrt(jnp.mean(values * values, axis=-1, keepdims=True) + epsilon)


def gelu_tanh(values):
    return jax.nn.gelu(values, approximate=True)


def combine_affine(earlier, later):
    return (earlier[0] * later[0], later[0] * earlier[1] + later[1])


def norm_apply(vector, gain_vector):
    return rms_unit(vector) * gain_vector[None, :]


def gated_terms(signal, segments, params):
    conv_weight, conv_bias, decay_gate, decay_bias, input_gate, input_bias, decay_param = params
    length, channels = signal.shape
    tap_count = conv_weight.shape[0]
    conv_out = conv_bias[None, :] + conv_weight[0][None, :] * signal
    for offset in range(1, tap_count):
        shifted = jnp.concatenate(
            [jnp.zeros((offset, channels), jnp.float32), signal[:-offset]], axis=0
        )
        earlier_ids = jnp.concatenate(
            [jnp.full((offset,), -1, jnp.int32), segments[:-offset]], axis=0
        )
        matches = (earlier_ids == segments).astype(jnp.float32)
        conv_out = conv_out + conv_weight[offset][None, :] * shifted * matches[:, None]
    blocks = conv_out.reshape(length, decay_gate.shape[0], decay_gate.shape[1])
    decay_pre = (
        jnp.einsum("shc,hcd->shd", blocks, decay_gate, precision=highest).reshape(length, channels)
        + decay_bias[None, :]
    )
    input_pre = (
        jnp.einsum("shc,hcd->shd", blocks, input_gate, precision=highest).reshape(length, channels)
        + input_bias[None, :]
    )
    decay_rate = jax.nn.sigmoid(decay_pre)
    input_rate = jax.nn.sigmoid(input_pre)
    restart = jnp.concatenate(
        [jnp.ones((1,), jnp.float32), (segments[1:] != segments[:-1]).astype(jnp.float32)]
    )[:, None]
    log_decay = -scale_c * jax.nn.softplus(-decay_param)[None, :] * decay_rate
    scaled = restart + (1.0 - restart) * jnp.sqrt(-jnp.expm1(2.0 * log_decay))
    carried = (1.0 - restart) * jnp.exp(log_decay)
    return (carried, scaled * input_rate * conv_out)


def body(
    tokens,
    segment_ids,
    mixer_gain,
    branch_weight,
    input_weight,
    output_weight,
    conv_weight,
    conv_bias,
    decay_gate,
    decay_bias,
    input_gate,
    input_bias,
    decay_param,
    mlp_gain,
    hidden_gate,
    hidden_up,
    hidden_down,
    cotangent,
):
    residual_in = tokens[0].astype(jnp.float32)
    tok_count, model_width = residual_in.shape
    lru_width = branch_weight.shape[1]
    mixer_unit = rms_unit(residual_in)
    row_segments = segment_ids[0]
    out_grad = cotangent[0]
    lru_params = (
        conv_weight,
        conv_bias,
        decay_gate,
        decay_bias,
        input_gate,
        input_bias,
        decay_param,
    )

    def local_recurrence(signal, params):
        carried, driven = gated_terms(signal, row_segments, params)
        _, states = lax.associative_scan(combine_affine, (carried, driven), axis=0)
        return states

    branch_piece = lax.all_gather(branch_weight, ("rows", "blk"), axis=0, tiled=True)
    input_piece = lax.all_gather(input_weight, ("rows", "blk"), axis=0, tiled=True)
    mixer_piece = lax.all_gather(mixer_gain, ("rows", "blk"), axis=0, tiled=True)
    mlp_piece = lax.all_gather(mlp_gain, ("rows", "blk"), axis=0, tiled=True)
    normed = (mixer_unit * mixer_piece.astype(jnp.float32)[None, :]).astype(jnp.bfloat16)
    branch_sum = jnp.dot(normed, branch_piece, preferred_element_type=jnp.float32)
    input_sum = jnp.dot(normed, input_piece, preferred_element_type=jnp.float32)
    mixer_all = mixer_piece
    mlp_all = mlp_piece
    branch_pre, input_pre, mixer_all, mlp_all = (branch_sum, input_sum, mixer_all, mlp_all)
    mixer_gains = mixer_all.astype(jnp.float32)
    mlp_gains = mlp_all.astype(jnp.float32)
    mixer_normed = (mixer_unit * mixer_gains[None, :]).astype(jnp.bfloat16)
    channel_input = lax.all_to_all(
        input_pre.astype(jnp.bfloat16), "blk", split_axis=1, concat_axis=0, tiled=True
    )
    states, lru_pullback = jax.vjp(local_recurrence, channel_input.astype(jnp.float32), lru_params)
    state_tokens = lax.all_to_all(
        states.astype(jnp.bfloat16), "blk", split_axis=0, concat_axis=1, tiled=True
    )
    state_values = state_tokens.astype(jnp.float32)
    branch_act, branch_pullback = jax.vjp(gelu_tanh, branch_pre)
    mixed = (branch_act * state_values).astype(jnp.bfloat16)
    mixer_out = jnp.einsum(
        "tr,dr->td",
        mixed,
        lax.all_gather(output_weight, ("rows", "blk"), axis=0, tiled=True),
        preferred_element_type=jnp.float32,
    )
    residual_mid = residual_in + mixer_out
    mlp_normed = (rms_unit(residual_mid) * mlp_gains[None, :]).astype(jnp.bfloat16)

    def hidden_terms(pieces):
        gate_vals = jnp.einsum(
            "td,fd->tf", mlp_normed, pieces[0], preferred_element_type=jnp.float32
        )
        up_vals = jnp.einsum("td,fd->tf", mlp_normed, pieces[1], preferred_element_type=jnp.float32)
        return (gate_vals, up_vals)

    pieces = (
        lax.all_gather(hidden_gate, ("rows", "blk"), axis=0, tiled=True),
        lax.all_gather(hidden_up, ("rows", "blk"), axis=0, tiled=True),
        lax.all_gather(hidden_down, ("rows", "blk"), axis=0, tiled=True),
    )
    gate_vals, up_vals = hidden_terms(pieces)
    hidden_vals = (gelu_tanh(gate_vals) * up_vals).astype(jnp.bfloat16)
    summed = jnp.dot(hidden_vals, pieces[2], preferred_element_type=jnp.float32)
    block_out = (residual_mid + summed).astype(jnp.bfloat16)
    pieces = (
        lax.all_gather(hidden_gate, ("rows", "blk"), axis=0, tiled=True),
        lax.all_gather(hidden_up, ("rows", "blk"), axis=0, tiled=True),
        lax.all_gather(hidden_down, ("rows", "blk"), axis=0, tiled=True),
    )
    gate_piece, up_piece, down_piece = pieces
    gate_vals, up_vals = hidden_terms(pieces)
    gate_act, gate_pullback = jax.vjp(gelu_tanh, gate_vals)
    hidden_vals = (gate_act * up_vals).astype(jnp.bfloat16)
    hidden_grad = jnp.einsum("td,fd->tf", out_grad, down_piece, preferred_element_type=jnp.float32)
    gate_grad = gate_pullback(hidden_grad * up_vals)[0].astype(jnp.bfloat16)
    up_grad = (hidden_grad * gate_act).astype(jnp.bfloat16)
    normed_grad = jnp.dot(gate_grad, gate_piece, preferred_element_type=jnp.float32) + jnp.dot(
        up_grad, up_piece, preferred_element_type=jnp.float32
    )
    normed_grad, gate_grads, up_grads, hidden_all = (normed_grad, gate_grad, up_grad, hidden_vals)
    mlp_weight_grads = lax.psum_scatter(
        jnp.concatenate(
            [
                jnp.einsum("tf,td->fd", gate_grads, mlp_normed, preferred_element_type=jnp.float32),
                jnp.einsum("tf,td->fd", up_grads, mlp_normed, preferred_element_type=jnp.float32),
                jnp.einsum("tf,td->fd", hidden_all, out_grad, preferred_element_type=jnp.float32),
            ],
            axis=1,
        ),
        ("rows", "blk"),
        scatter_dimension=0,
        tiled=True,
    )
    _, mlp_norm_pullback = jax.vjp(norm_apply, residual_mid, mlp_gains)
    mid_part, mlp_gain_part = mlp_norm_pullback(normed_grad)
    mid_grad = out_grad.astype(jnp.float32) + mid_part
    mid_sent = mid_grad.astype(jnp.bfloat16)
    mixed_grad = jnp.dot(
        mid_sent,
        lax.all_gather(output_weight, ("rows", "blk"), axis=0, tiled=True),
        preferred_element_type=jnp.float32,
    )
    branch_grad = branch_pullback(mixed_grad * state_values)[0].astype(jnp.bfloat16)
    state_grad = (mixed_grad * branch_act).astype(jnp.bfloat16)
    channel_grad = lax.all_to_all(state_grad, "blk", split_axis=1, concat_axis=0, tiled=True)
    signal_grad, lru_grads = lru_pullback(channel_grad.astype(jnp.float32))
    input_grad_tokens = lax.all_to_all(
        signal_grad.astype(jnp.bfloat16), "blk", split_axis=0, concat_axis=1, tiled=True
    )
    pieces = lax.all_gather((branch_weight, input_weight), ("rows", "blk"), axis=0, tiled=True)
    mixer_normed_grad = jnp.einsum(
        "tr,dr->td", branch_grad, pieces[0], preferred_element_type=jnp.float32
    ) + jnp.einsum("tr,dr->td", input_grad_tokens, pieces[1], preferred_element_type=jnp.float32)
    _, mixer_norm_pullback = jax.vjp(norm_apply, residual_in, mixer_gains)
    token_part, mixer_gain_part = mixer_norm_pullback(mixer_normed_grad)
    token_grad = mid_grad + token_part
    mixer_weight_grads = lax.psum_scatter(
        jnp.concatenate(
            [
                jnp.einsum(
                    "td,tr->dr", mixer_normed, branch_grad, preferred_element_type=jnp.float32
                ),
                jnp.einsum(
                    "td,tr->dr", mixer_normed, input_grad_tokens, preferred_element_type=jnp.float32
                ),
                jnp.einsum("td,tr->dr", mid_sent, mixed, preferred_element_type=jnp.float32),
            ],
            axis=1,
        ),
        ("rows", "blk"),
        scatter_dimension=0,
        tiled=True,
    )
    branch_weight_grad = mixer_weight_grads[:, :lru_width]
    input_weight_grad = mixer_weight_grads[:, lru_width : 2 * lru_width]
    output_weight_grad = mixer_weight_grads[:, 2 * lru_width :]
    hidden_gate_grad = mlp_weight_grads[:, :model_width]
    hidden_up_grad = mlp_weight_grads[:, model_width : 2 * model_width]
    hidden_down_grad = mlp_weight_grads[:, 2 * model_width :]
    conv_w_sum, conv_b_sum, decay_g_sum, decay_b_sum, input_g_sum, input_b_sum, decay_p_sum = (
        lru_grads
    )
    (
        conv_weight_grad,
        conv_bias_grad,
        decay_gate_grad,
        decay_bias_grad,
        input_gate_grad,
        input_bias_grad,
        decay_param_grad,
    ) = lax.psum(
        (conv_w_sum, conv_b_sum, decay_g_sum, decay_b_sum, input_g_sum, input_b_sum, decay_p_sum),
        "rows",
    )
    mixer_gain_grad, mlp_gain_grad = (
        lax.psum_scatter(mixer_gain_part, ("rows", "blk"), scatter_dimension=0, tiled=True),
        lax.psum_scatter(mlp_gain_part, ("rows", "blk"), scatter_dimension=0, tiled=True),
    )
    return (
        block_out[None],
        token_grad[None],
        mixer_gain_grad,
        branch_weight_grad,
        input_weight_grad,
        output_weight_grad,
        conv_weight_grad,
        conv_bias_grad,
        decay_gate_grad,
        decay_bias_grad,
        input_gate_grad,
        input_bias_grad,
        decay_param_grad,
        mlp_gain_grad,
        hidden_gate_grad,
        hidden_up_grad,
        hidden_down_grad,
    )


def solution(mesh):
    return jax.shard_map(
        body,
        mesh=mesh,
        in_specs=(
            P("rows", "blk", None),
            P("rows", None),
            P(("rows", "blk")),
            P(("rows", "blk"), None),
            P(("rows", "blk"), None),
            P(("rows", "blk"), None),
            P(None, "blk"),
            P("blk"),
            P("blk", None, None),
            P("blk"),
            P("blk", None, None),
            P("blk"),
            P("blk"),
            P(("rows", "blk")),
            P(("rows", "blk"), None),
            P(("rows", "blk"), None),
            P(("rows", "blk"), None),
            P("rows", "blk", None),
        ),
        out_specs=(
            P("rows", "blk", None),
            P("rows", "blk", None),
            P(("rows", "blk")),
            P(("rows", "blk"), None),
            P(("rows", "blk"), None),
            P(("rows", "blk"), None),
            P(None, "blk"),
            P("blk"),
            P("blk", None, None),
            P("blk"),
            P("blk", None, None),
            P("blk"),
            P("blk"),
            P(("rows", "blk")),
            P(("rows", "blk"), None),
            P(("rows", "blk"), None),
            P(("rows", "blk"), None),
        ),
        check_vma=False,
    )
```

profile of v0, /device:TPU:0, one launch (start us, length us, event | category | flops | bytes accessed | tf_op | source)
XLA Modules:
  0.0 4342.0 jit_solution(1717380246642410880)
XLA Ops:
  11.7 43.0 all-reduce.104
  55.4 50.3 %all-gather.9.cloned.1.call-done = bf16[2048,2736]{1,0:T(8,128)(2,1)} async-done(((bf16[64,2736]{1,0:T(8,128)(2,1)}), bf16[2048,2736]{1,0:T(8,128)(2,1)}) %all-gather.9.cloned.1.call-update) | async-done | bytes 11206672 | tf_op jit(solution)/shard_map/all_gather | solution.py:103
  121.2 22.1 all-to-all-done
  164.6 27.8 slice.355
  192.4 28.5 slice.359
  221.0 28.5 slice.354
  250.2 27.6 slice.356
  277.8 27.5 slice.419
  305.3 27.8 slice.357
  649.6 25.2 pad.374
  674.9 28.0 pad.375
  711.5 38.3 all-to-all-done.1
  804.5 16.7 multiply_convert_fusion
  880.1 28.4 slice.420
  912.1 27.8 slice.421
  1281.4 26.5 pad.434
  1307.9 26.1 pad.378
  1334.0 26.2 pad.459
  1360.2 26.6 pad.435
  1386.7 26.1 pad.460
  1412.9 28.3 pad.436
  1514.1 50.3 %pad_maximum_fusion.1 = f32[2048,8208]{0,1:T(8,128)} fusion(f32[2048,2736]{0,1:T(8,128)} %fusion.58, f32[2048,2736]{0,1:T(8,128)} %fusion.47, f32[2048,2736]{0,1:T(8,128)S(1)} %copy-done.4), kind=kLoop, calls=%fused_computation.1 | loop fusion | flops 33619968 | bytes 134479872 | tf_op jit(solution)/shard_map/concatenate | solution.py:203
  1564.4 64.7 %copy.125 = f32[2048,8208]{1,0:T(8,128)} copy(f32[2048,8208]{0,1:T(8,128)} %pad_maximum_fusion.1) | data formatting | bytes 134479872
  1630.7 19.9 fusion.135
  1650.6 21.1 fusion.134
  1671.7 19.6 fusion.49
  1691.3 102.0 %pad_maximum_fusion = f32[6144,6144]{0,1:T(8,128)} fusion(f32[6144,2048]{0,1:T(8,128)} %fusion.49, f32[6144,2048]{0,1:T(8,128)} %fusion.135, f32[6144,2048]{0,1:T(8,128)} %fusion.134), kind=kLoop, calls=%fused_computation | loop fusion | flops 75497472 | bytes 301989888 | tf_op jit(solution)/shard_map/concatenate | solution.py:167
  1793.3 145.9 %copy.127 = f32[6144,6144]{1,0:T(8,128)} copy(f32[6144,6144]{0,1:T(8,128)} %pad_maximum_fusion) | data formatting | bytes 301989888
  1961.1 24.9 all-reduce.102
  1999.6 42.7 all-reduce.101
  2044.8 1014.8 %reduce-scatter.7.cloned.1.call-done = f32[64,8208]{1,0:T(8,128)} async-done(((f32[2048,8208]{1,0:T(8,128)}), f32[64,8208]{1,0:T(8,128)}) %reduce-scatter.7.cloned.1.call-update) | async-done | bytes 2101264
  3062.9 1267.6 %reduce-scatter.9.cloned.1.call-done = f32[192,6144]{1,0:T(8,128)} async-done(((f32[6144,6144]{1,0:T(8,128)}), f32[192,6144]{1,0:T(8,128)}) %reduce-scatter.9.cloned.1.call-update) | async-done | bytes 4718608
  (766 shorter events, 944.8 us)
Async XLA Ops:
  7.2 141.4 %copy-start = (f32[4,171,171]{2,0,1:T(4,128)S(1)}, f32[4,171,171]{2,0,1:T(4,128)}, u32[]{:S(2)}) copy-start(f32[4,171,171]{2,0,1:T(4,128)} %param.28) | copy-start | bytes 1403572
  7.2 98.5 %all-gather.9.cloned.1.call-start = ((), (), s32[]{:S(2)}) async-start(), calls=%async_computation.7 | async-start | bytes 11894784 | tf_op jit(solution)/shard_map/all_gather | solution.py:103
  7.9 745.6 %all-gather.7.cloned.1.call-start = ((), (), s32[]{:S(2)}) async-start(), calls=%async_computation.6 | async-start | bytes 11894784 | tf_op jit(solution)/shard_map/all_gather | solution.py:102
  8.7 46.0 %copy-start.13 = (bf16[1,128,2048]{2,1,0:T(8,128)(2,1)S(1)}, bf16[1,128,2048]{2,1,0:T(8,128)(2,1)}, u32[]{:S(2)}) copy-start(bf16[1,128,2048]{2,1,0:T(8,128)(2,1)} %param.18) | copy-start | bytes 1572868
  8.7 755.6 %all-gather.11.cloned.1.call-start = ((), (), s32[]{:S(2)}) async-start(), calls=%async_computation.8 | async-start | bytes 11894784 | tf_op jit(solution)/shard_map/all_gather | solution.py:128
  9.5 763.9 %all-gather.15.cloned.1.call-start = ((), (), s32[]{:S(2)}) async-start(), calls=%async_computation.10 | async-start | bytes 25952256 | tf_op jit(solution)/shard_map/all_gather | solution.py:143
  10.0 779.3 %all-gather.13.cloned.1.call-start = ((), (), s32[]{:S(2)}) async-start(), calls=%async_computation.9 | async-start | bytes 25952256 | tf_op jit(solution)/shard_map/all_gather | solution.py:142
  10.6 793.8 %all-gather.17.cloned.1.call-start = ((), (), s32[]{:S(2)}) async-start(), calls=%async_computation.11 | async-start | bytes 25952256 | tf_op jit(solution)/shard_map/all_gather | solution.py:144
  54.7 59.9 %copy-start.171 = (f32[2048]{0:T(1024)}, f32[2048]{0:T(1024)S(1)}, u32[]{:S(2)}) copy-start(f32[2048]{0:T(1024)S(1)} %convert_element_type.110) | copy-start | bytes 24580
  55.4 50.3 %copy-start.194 = (f32[128]{0:T(128)}, f32[128]{0:T(128)S(1)}, u32[]{:S(2)}) copy-start(f32[128]{0:T(128)S(1)} %fusion.81) | copy-start | bytes 1540
  115.6 27.7 all-to-all-start
  121.1 38.4 copy-start.174
  192.4 140.7 %copy-start.27 = (f32[256,684]{0,1:T(8,128)}, f32[256,684]{0,1:T(8,128)S(1)}, u32[]{:S(2)}) copy-start(f32[256,684]{0,1:T(8,128)S(1)} %slice.355) | copy-start | bytes 2101252
  192.4 57.0 %copy-start.29 = (f32[512,684]{0,1:T(8,128)S(1)}, f32[512,684]{0,1:T(8,128)}, u32[]{:S(2)}) copy-start(f32[512,684]{0,1:T(8,128)} %get-tuple-element.149) | copy-start | bytes 4202500
  221.0 112.2 %copy-start.44 = (f32[256,684]{0,1:T(8,128)}, f32[256,684]{0,1:T(8,128)S(1)}, u32[]{:S(2)}) copy-start(f32[256,684]{0,1:T(8,128)S(1)} %slice.359) | copy-start | bytes 2101252
  352.1 80.6 %copy-start.79 = (f32[128,684]{0,1:T(8,128)}, f32[128,684]{0,1:T(8,128)S(1)}, u32[]{:S(2)}) copy-start(f32[128,684]{0,1:T(8,128)S(1)} %slice.361) | copy-start | bytes 1050628
  368.5 64.1 %copy-start.113 = (f32[128,684]{0,1:T(8,128)}, f32[128,684]{0,1:T(8,128)S(1)}, u32[]{:S(2)}) copy-start(f32[128,684]{0,1:T(8,128)S(1)} %slice.365) | copy-start | bytes 1050628
  441.3 42.5 copy-start.81
  708.0 41.8 all-to-all-start.1
  773.1 69.8 %copy-start.17 = (f32[128,2048]{1,0:T(8,128)}, f32[128,2048]{1,0:T(8,128)S(1)}, u32[]{:S(2)}) copy-start(f32[128,2048]{1,0:T(8,128)S(1)} %get-tuple-element.233) | copy-start | bytes 3145732
  854.4 21.6 all-to-all-start.2
  1223.1 41.0 copy-start.160
  1236.5 40.9 copy-start.28
  1236.5 40.9 copy-start.45
  1236.5 40.9 copy-start.46
  1386.7 54.4 %copy-start.10 = (f32[512,684]{0,1:T(8,128)S(1)}, f32[512,684]{0,1:T(8,128)}, u32[]{:S(2)}) copy-start(f32[512,684]{0,1:T(8,128)} %copy-done.9) | copy-start | bytes 4202500
  1477.0 21.3 all-to-all-start.3
  1480.5 505.5 %all-reduce.107.cloned.1.call-start = ((), (), s32[]{:S(2)}) async-start(), calls=%async_computation.14 | async-start | bytes 2883584 | tf_op jit(solution)/shard_map/psum | solution.py:236
  1494.5 1565.1 %reduce-scatter.7.cloned.1.call-start = ((), (), s32[]{:S(2)}) async-start(), calls=%async_computation.12 | async-start | bytes 70287360
  1629.1 2701.4 %reduce-scatter.9.cloned.1.call-start = ((), (), s32[]{:S(2)}) async-start(), calls=%async_computation.13 | async-start | bytes 155713536
  1991.1 52.4 %copy-start.217 = (f32[128]{0:T(128)S(1)}, f32[128]{0:T(128)}, u32[]{:S(2)}) copy-start(f32[128]{0:T(128)} %copy-done.216) | copy-start | bytes 1540
  1991.1 52.4 %copy-start.36 = (f32[128,2048]{1,0:T(8,128)S(1)}, f32[128,2048]{1,0:T(8,128)}, u32[]{:S(2)}) copy-start(f32[128,2048]{1,0:T(8,128)} %fusion.38) | copy-start | bytes 3145732
  (205 other events, 1962.5 us)
Sparse Core Ops, SparseCore 0:
  10.9 94.7 all-gather.8
  108.5 99.3 all-gather.6
  210.8 89.6 all-gather.10
  303.2 153.0 all-gather.14
  459.0 152.8 all-gather.12
  614.6 165.3 all-gather.16
  1494.6 57.8 all-reduce.106
  1629.2 1430.3 reduce-scatter.6
  3066.0 1264.4 reduce-scatter.8
where the time goes:
time: 4350 us; the launch traced here: 4340 us
  waiting for transfers between devices  2410 us (55%)
  local copies, waits for them, and re-layouts  1280 us (29%)
  other arithmetic  261 us (6%)
  matrix products  246 us (6%)
  blocking collectives  111 us (3%)
    unnamed x11, waiting for transfers between devices  2290 us
    slice x64, local copies, waits for them, and re-layouts, local_recurrence(): _, states = lax.associative_scan(combine_affine, (carried, driven), axis=0)  529 us
    pad x70, local copies, waits for them, and re-layouts, local_recurrence(): _, states = lax.associative_scan(combine_affine, (carried, driven), axis=0)  484 us
    unnamed x468, local copies, waits for them, and re-layouts  238 us
    concatenate x1, other arithmetic, body(): jnp.concatenate([jnp.einsum('tf,td->fd', gate_grads, mlp_normed, preferre...  102 us
  transfers between devices with their start and end apart: 13, of which 7 were waited for; matrix products, arithmetic and copies ran while one was open for 26% of the time, Pallas kernels for 0%

commit v1 on v0

v1 whole, which is shorter than its diff:
```python
import functools

import jax
import jax.numpy as jnp
from jax import lax
from jax.experimental import pallas as pl
from jax.experimental.pallas import tpu as pltpu
from jax.sharding import PartitionSpec as P

epsilon = 1e-06
scale_c = 8.0
bf16 = jnp.bfloat16
f32 = jnp.float32
chunk = 64
vmem_limit = 48 * 1024 * 1024


def rms_scale(values):
    return lax.rsqrt(jnp.mean(values * values, axis=-1, keepdims=True) + epsilon)


def gelu_tanh(values):
    return jax.nn.gelu(values, approximate=True)


def mm(left, right, dims):
    return lax.dot_general(left, right, (dims, ((), ())), preferred_element_type=f32)


def tie(*values):
    return lax.optimization_barrier(values)


def flip(size, bit):
    return [(place, place ^ bit) for place in range(size)]


def bits_of(size):
    found, bit = [], 1
    while bit < size:
        found.append(bit)
        bit *= 2
    return found


def swap_blk(parts):
    return lax.all_to_all(parts, "blk", split_axis=0, concat_axis=0, tiled=True)


def gather_blk(part, size):
    return swap_blk(jnp.broadcast_to(part[None], (size,) + part.shape))


def halve(total, size, bit, left):
    axis = left.index(bit)
    left.remove(bit)
    mine = (lax.axis_index("rows") // bit) % 2
    away = lax.dynamic_index_in_dim(total, 1 - mine, axis, keepdims=False)
    keep = lax.dynamic_index_in_dim(total, mine, axis, keepdims=False)
    got = lax.ppermute(away.astype(bf16), "rows", flip(size, bit))
    return keep.astype(f32) + got.astype(f32), got


def by_bits(total, size):
    left = list(reversed(bits_of(size)))
    return total.reshape((2,) * len(left) + (total.shape[0] // size,) + total.shape[1:]), left


def sum_rows(value, size, wire=f32):
    for bit in bits_of(size):
        value = value + lax.ppermute(value.astype(wire), "rows", flip(size, bit)).astype(f32)
    return value


def sum_blk(value, size):
    for bit in bits_of(size):
        value = value + lax.ppermute(value, "blk", flip(size, bit))
    return value


def split_columns_kernel(
    width, wide, input_ref, branch_ref, output_ref, mixer_ref, mlp_ref, both_ref
):
    parts = both_ref.shape[0]
    both_ref[...] = jnp.zeros_like(both_ref)
    for part in range(parts):
        cut = slice(part * width, (part + 1) * width)
        both_ref[part, :, :width] = input_ref[:, cut]
        both_ref[part, :, wide : wide + width] = branch_ref[:, cut]
        both_ref[part, :, 2 * wide : 2 * wide + width] = output_ref[:, cut]
        both_ref[part, :, width : width + 1] = mixer_ref[...]
        both_ref[part, :, width + 1 : width + 2] = mlp_ref[...]


def join_columns_kernel(width, wide, parts_ref, *out_refs):
    for part in range(parts_ref.shape[0]):
        cut = slice(part * width, (part + 1) * width)
        for number, out_ref in enumerate(out_refs):
            begin = number * wide
            out_ref[:, cut] = parts_ref[part, :, begin : begin + width].astype(f32)


def mixer_norm_kernel(gain_ref, tokens_ref, out_ref):
    step = 32

    def rows_step(index, carry):
        here = pl.ds(pl.multiple_of(index * step, step), step)
        values = tokens_ref[here, :].astype(f32)
        out_ref[here, :] = (values * rms_scale(values) * gain_ref[...]).astype(bf16)
        return carry

    lax.fori_loop(0, tokens_ref.shape[0] // step, rows_step, 0)


def sum_parts(parts_ref, here):
    total = parts_ref[0, here, :].astype(f32)
    for part in range(1, parts_ref.shape[0]):
        total = total + parts_ref[part, here, :].astype(f32)
    return total


def mid_norm_kernel(gain_ref, tokens_ref, parts_ref, mid_ref, normed_ref):
    step = 32

    def rows_step(index, carry):
        here = pl.ds(pl.multiple_of(index * step, step), step)
        values = tokens_ref[here, :].astype(f32) + sum_parts(parts_ref, here)
        mid_ref[here, :] = values
        normed_ref[here, :] = (values * rms_scale(values) * gain_ref[...]).astype(bf16)
        return carry

    lax.fori_loop(0, tokens_ref.shape[0] // step, rows_step, 0)


def fold8(value):
    return value.reshape(value.shape[0] // 8, 8, value.shape[1]).sum(axis=0)


def norm_back(grad, values, gain):
    scale = rms_scale(values)
    product = grad * values
    factor = scale * scale * scale * jnp.mean(product * gain, axis=-1, keepdims=True)
    return scale * (grad * gain) - values * factor, product * scale


def mid_grad_kernel(gain_ref, mid_ref, cotangent_ref, parts_ref, grad_ref, sent_ref, sums_ref):
    step = 32
    sums_ref[...] = jnp.zeros_like(sums_ref)

    def rows_step(index, carry):
        here = pl.ds(pl.multiple_of(index * step, step), step)
        change, terms = norm_back(sum_parts(parts_ref, here), mid_ref[here, :], gain_ref[...])
        sums_ref[...] += fold8(terms)
        result = cotangent_ref[here, :].astype(f32) + change
        grad_ref[here, :] = result
        sent_ref[here, :] = result.astype(bf16)
        return carry

    lax.fori_loop(0, mid_ref.shape[0] // step, rows_step, 0)


def pack_grad_kernel(partial_ref, tokens_ref, sent_ref, sums_ref):
    step = 32
    sums_ref[...] = jnp.zeros_like(sums_ref)

    def rows_step(index, carry):
        here = pl.ds(pl.multiple_of(index * step, step), step)
        values = tokens_ref[here, :].astype(f32)
        grad = partial_ref[here, :]
        sums_ref[...] += fold8(values * rms_scale(values) * grad)
        sent_ref[here, :] = grad.astype(bf16)
        return carry

    lax.fori_loop(0, partial_ref.shape[0] // step, rows_step, 0)


def token_grad_kernel(gain_ref, tokens_ref, mid_grad_ref, parts_ref, grad_ref):
    step = 32

    def rows_step(index, carry):
        here = pl.ds(pl.multiple_of(index * step, step), step)
        values = tokens_ref[here, :].astype(f32)
        change, _ = norm_back(sum_parts(parts_ref, here), values, gain_ref[...])
        grad_ref[here, :] = mid_grad_ref[here, :] + change
        return carry

    lax.fori_loop(0, tokens_ref.shape[0] // step, rows_step, 0)


def local_kernel(kernel, name, operands, outs, scratch=()):
    return pl.pallas_call(
        kernel,
        out_shape=[jax.ShapeDtypeStruct(shape, kind) for shape, kind in outs],
        in_specs=[pl.BlockSpec(memory_space=pltpu.VMEM)] * len(operands),
        out_specs=[pl.BlockSpec(memory_space=pltpu.VMEM)] * len(outs),
        scratch_shapes=list(scratch),
        compiler_params=pltpu.CompilerParams(vmem_limit_bytes=vmem_limit),
        name=name,
    )(*operands)


def round_up(value):
    return -(-value // 128) * 128


def column_tiles(width, wide, block):
    tiles = []
    for start in range(0, wide, 256):
        stop = min(start + 256, wide)
        low = (start // block) * block
        high = ((min(stop, width) - 1) // block + 1) * block
        tiles.append((start, stop, low // 128 * 128, min(round_up(high), wide)))
    return tiles


def split_bf16(value):
    high = value.astype(bf16)
    return high, (value - high.astype(f32)).astype(bf16)


def one_minus_exp(value):
    series = 1.0 + value * (1.0 / 8.0)
    for term in (7.0, 6.0, 5.0, 4.0, 3.0, 2.0):
        series = 1.0 + value * (1.0 / term) * series
    return jnp.where(value > -0.3, -value * series, 1.0 - jnp.exp(value))


def shift_down(tile, count, fill):
    moved = pltpu.roll(tile, count, 0)
    row = lax.broadcasted_iota(jnp.int32, tile.shape, 0)
    return jnp.where(row < count, fill, moved)


def shift_up(tile, count, fill):
    moved = pltpu.roll(tile, tile.shape[0] - count, 0)
    row = lax.broadcasted_iota(jnp.int32, tile.shape, 0)
    return jnp.where(row >= tile.shape[0] - count, fill, moved)


def blocked_product(first, second, weights, tiles, store, length, turned=False):
    step = 256

    def rows_step(index, carry):
        rows = pl.ds(pl.multiple_of(index * step, step), step)
        for start, stop, low, high in tiles:
            total = None
            for (high_ref, low_ref), (w_high, w_low) in zip((first, second), weights):
                if high_ref is None:
                    continue
                a_high = high_ref[rows, low:high]
                a_low = low_ref[rows, low:high]
                cut = (slice(start, stop), slice(low, high))
                cut = cut if turned else cut[::-1]
                b_high, b_low = w_high[cut], w_low[cut]
                dims = ((1,), (1,)) if turned else ((1,), (0,))
                part = mm(a_high, b_high, dims) + mm(a_high, b_low, dims) + mm(a_low, b_high, dims)
                total = part if total is None else total + part
            store(rows, slice(start, stop), total)
        return carry

    lax.fori_loop(0, length // step, rows_step, 0)


def recur_forward_kernel(
    tiles,
    signal_ref,
    masks_ref,
    vectors_ref,
    decay_high,
    decay_low,
    input_high,
    input_low,
    states_ref,
    values_ref,
    conv_ref,
    decay_rate_ref,
    input_rate_ref,
    padded,
    conv_high,
    conv_low,
):
    length, width = signal_ref.shape
    count = length // chunk
    padded[0:8, :] = jnp.zeros((8, width), f32)

    def pad_step(index, carry):
        begin = pl.multiple_of(index * chunk, chunk)
        here = pl.ds(begin, chunk)
        padded[pl.ds(begin + 8, chunk), :] = signal_ref[here, :].astype(f32)
        return carry

    lax.fori_loop(0, count, pad_step, 0)

    def conv_step(index, carry):
        begin = pl.multiple_of(index * chunk, chunk)
        rows = pl.ds(begin, chunk)
        window = padded[pl.ds(begin, chunk + 8), :]
        total = vectors_ref[4:5, :] + vectors_ref[0:1, :] * window[8:, :]
        for tap in range(1, 4):
            total = total + vectors_ref[tap : tap + 1, :] * (
                window[8 - tap : 8 - tap + chunk, :] * masks_ref[rows, tap : tap + 1]
            )
        conv_ref[rows, :] = total
        high, low = split_bf16(total)
        conv_high[rows, :] = high
        conv_low[rows, :] = low
        return carry

    lax.fori_loop(0, count, conv_step, 0)

    def store_decay(rows, columns, value):
        decay_rate_ref[rows, columns] = jax.nn.sigmoid(value + vectors_ref[5:6, columns])

    def store_input(rows, columns, value):
        input_rate_ref[rows, columns] = jax.nn.sigmoid(value + vectors_ref[6:7, columns])

    nothing = (None, None)
    blocked_product(
        (conv_high, conv_low), nothing, ((decay_high, decay_low), nothing), tiles, store_decay, length
    )
    blocked_product(
        (conv_high, conv_low), nothing, ((input_high, input_low), nothing), tiles, store_input, length
    )

    def scan_step(index, state):
        begin = pl.multiple_of(index * 8, 8)
        rows = pl.ds(begin, 8)
        restart = masks_ref[rows, 4:5]
        keep = 1.0 - restart
        log_decay = -vectors_ref[7:8, :] * decay_rate_ref[rows, :]
        mult = restart + keep * jnp.sqrt(one_minus_exp(2.0 * log_decay))
        carried = keep * jnp.exp(log_decay)
        total = mult * input_rate_ref[rows, :] * conv_ref[rows, :]
        for count_rows in (1, 2, 4):
            total = total + carried * shift_down(total, count_rows, 0.0)
            carried = carried * shift_down(carried, count_rows, 1.0)
        total = total + carried * state
        states_ref[rows, :] = total
        return total[7:8, :]

    lax.fori_loop(0, length // 8, scan_step, jnp.zeros((1, width), f32), unroll=4)

    def values_step(index, carry):
        begin = pl.multiple_of(index * chunk, chunk)
        here = pl.ds(begin, chunk)
        values_ref[here, :] = states_ref[pl.ds(begin, chunk), :].astype(bf16)
        return carry

    lax.fori_loop(0, count, values_step, 0)


def recur_backward_kernel(
    tiles,
    grad_ref,
    signal_ref,
    masks_ref,
    vectors_ref,
    decay_high,
    decay_low,
    input_high,
    input_low,
    states_ref,
    conv_ref,
    decay_rate_ref,
    input_rate_ref,
    signal_grad_ref,
    decay_pre_ref,
    input_pre_ref,
    sums_ref,
    padded,
    grads,
    earlier,
    decay_pre_high,
    decay_pre_low,
    input_pre_high,
    input_pre_low,
):
    length, width = signal_ref.shape
    count = length // chunk
    padded[0:8, :] = jnp.zeros((8, width), f32)
    earlier[0:8, :] = jnp.zeros((8, width), f32)

    def pad_step(index, carry):
        begin = pl.multiple_of(index * chunk, chunk)
        here = pl.ds(begin, chunk)
        padded[pl.ds(begin + 8, chunk), :] = signal_ref[here, :].astype(f32)
        earlier[pl.ds(begin + 8, chunk), :] = states_ref[pl.ds(begin, chunk), :]
        grads[pl.ds(begin, chunk), :] = grad_ref[here, :].astype(f32)
        return carry

    lax.fori_loop(0, count, pad_step, 0)
    grads[length:, :] = jnp.zeros((8, width), f32)
    sums_ref[...] = jnp.zeros_like(sums_ref)

    def scan_step(index, later):
        begin = pl.multiple_of(length - 8 - index * 8, 8)
        rows = pl.ds(begin, 8)
        restart = masks_ref[rows, 4:5]
        keep = 1.0 - restart
        decay_rate = decay_rate_ref[rows, :]
        input_rate = input_rate_ref[rows, :]
        conv_out = conv_ref[rows, :]
        log_decay = -vectors_ref[7:8, :] * decay_rate
        decay = jnp.exp(log_decay)
        root = jnp.sqrt(one_minus_exp(2.0 * log_decay))
        mult = restart + keep * root
        carried = keep * decay
        flow = grads[rows, :]
        reach = shift_up(carried, 1, 1.0)
        for count_rows in (1, 2, 4):
            flow = flow + reach * shift_up(flow, count_rows, 0.0)
            reach = reach * shift_up(reach, count_rows, 1.0)
        flow = flow + reach * later
        window = earlier[pl.ds(begin, 16), :]
        before = window[7:15, :]
        flow_rate = flow * input_rate
        mult_grad = flow_rate * conv_out
        log_grad = keep * (flow * before * decay - mult_grad * decay * decay / root)
        rate_log = decay_rate * log_grad
        decay_pre = -vectors_ref[7:8, :] * rate_log * (1.0 - decay_rate)
        input_pre = mult_grad * mult * (1.0 - input_rate)
        grads[rows, :] = flow_rate * mult
        decay_pre_ref[rows, :] = decay_pre
        input_pre_ref[rows, :] = input_pre
        sums_ref[0:8, :] += rate_log
        sums_ref[8:16, :] += decay_pre
        sums_ref[16:24, :] += input_pre
        return carried[0:1, :] * flow[0:1, :]

    lax.fori_loop(0, length // 8, scan_step, jnp.zeros((1, width), f32), unroll=4)

    def split_step(index, carry):
        rows = pl.ds(pl.multiple_of(index * chunk, chunk), chunk)
        decay_pre_high[rows, :], decay_pre_low[rows, :] = split_bf16(decay_pre_ref[rows, :])
        input_pre_high[rows, :], input_pre_low[rows, :] = split_bf16(input_pre_ref[rows, :])
        return carry

    lax.fori_loop(0, count, split_step, 0)

    def store(rows, columns, value):
        grads[rows, columns] += value

    blocked_product(
        (decay_pre_high, decay_pre_low),
        (input_pre_high, input_pre_low),
        ((decay_high, decay_low), (input_high, input_low)),
        tiles,
        store,
        length,
        True,
    )

    def conv_step(index, carry):
        begin = pl.multiple_of(index * chunk, chunk)
        rows = pl.ds(begin, chunk)
        grad_window = grads[pl.ds(begin, chunk + 8), :]
        mask_window = masks_ref[pl.ds(begin, chunk + 8), :]
        signal_window = padded[pl.ds(begin, chunk + 8), :]
        here = grad_window[:chunk, :]
        result = vectors_ref[0:1, :] * here
        sums_ref[24:32, :] += fold8(here)
        sums_ref[32:40, :] += fold8(here * signal_window[8:, :])
        for tap in range(1, 4):
            masked = grad_window * mask_window[:, tap : tap + 1]
            result = result + vectors_ref[tap : tap + 1, :] * masked[tap : tap + chunk, :]
            sums_ref[32 + 8 * tap : 40 + 8 * tap, :] += fold8(
                masked[:chunk, :] * signal_window[8 - tap : 8 - tap + chunk, :]
            )
        here = pl.ds(begin, chunk)
        signal_grad_ref[here, :] = result.astype(bf16)
        return carry

    lax.fori_loop(0, count, conv_step, 0)


def recur_forward(signal, masks, vectors, weights, tiles):
    length, width = signal.shape
    whole = ((length, width), f32)
    return local_kernel(
        functools.partial(recur_forward_kernel, tiles),
        "recur_forward",
        (signal, masks, vectors, *weights),
        [whole, ((length, width), bf16), whole, whole, whole],
        [
            pltpu.VMEM((length + 8, width), f32),
            pltpu.VMEM((length, width), bf16),
            pltpu.VMEM((length, width), bf16),
        ],
    )


def recur_backward(state_grad, signal, masks, vectors, weights, saved, tiles):
    length, width = signal.shape
    whole = ((length, width), f32)
    pair = pltpu.VMEM((length, width), bf16)
    padded = pltpu.VMEM((length + 8, width), f32)
    return local_kernel(
        functools.partial(recur_backward_kernel, tiles),
        "recur_backward",
        (state_grad, signal, masks, vectors, *weights, *saved),
        [((length, width), bf16), whole, whole, ((64, width), f32)],
        [padded] * 3 + [pair] * 4,
    )


def dense_kernel(decay_ref, input_ref, decay_high, decay_low, input_high, input_low):
    heads, block, _ = decay_ref.shape
    for ref, high, low in (
        (decay_ref, decay_high, decay_low),
        (input_ref, input_high, input_low),
    ):
        high[...] = jnp.zeros_like(high)
        low[...] = jnp.zeros_like(low)
        for head in range(heads):
            cut = slice(head * block, (head + 1) * block)
            high[cut, cut], low[cut, cut] = split_bf16(ref[head])


def diagonal_blocks(left, right, heads, block):
    dense = lax.dot_general(
        left,
        right,
        (((0,), (0,)), ((), ())),
        precision=lax.Precision.HIGH,
        preferred_element_type=f32,
    )
    cuts = [slice(head * block, (head + 1) * block) for head in range(heads)]
    return jnp.stack([dense[cut, cut] for cut in cuts])


def unit_grads_kernel(*refs):
    count = (len(refs) - 1) // 2
    out_ref = refs[-1]
    for number in range(count):
        left_ref, right_ref = refs[number], refs[count + number]
        value = mm(left_ref[...], right_ref[...], ((0,), (0,))).astype(bf16)
        out_ref[:, number] = value.reshape(out_ref.shape[0], *out_ref.shape[2:])


def unit_grads(lefts, rights, parts):
    length, total = lefts[0].shape
    units = total // parts
    model_width = rights[0].shape[1]
    group = 1
    while group * units % 128:
        group *= 2
    count = len(lefts)
    return pl.pallas_call(
        unit_grads_kernel,
        grid=(parts // group,),
        out_shape=jax.ShapeDtypeStruct((parts, count, units, model_width), bf16),
        in_specs=[pl.BlockSpec((length, group * units), lambda i: (0, i))] * count
        + [pl.BlockSpec((length, model_width), lambda i: (0, 0))] * count,
        out_specs=pl.BlockSpec((group, count, units, model_width), lambda i: (i, 0, 0, 0)),
        compiler_params=pltpu.CompilerParams(vmem_limit_bytes=vmem_limit),
        cost_estimate=pl.CostEstimate(flops=1024, bytes_accessed=1024, transcendentals=0),
        name="unit_grads",
    )(*lefts, *rights)


def body(
    sizes,
    tokens,
    segment_ids,
    mixer_gain,
    branch_weight,
    input_weight,
    output_weight,
    conv_weight,
    conv_bias,
    decay_gate,
    decay_bias,
    input_gate,
    input_bias,
    decay_param,
    mlp_gain,
    hidden_gate,
    hidden_up,
    hidden_down,
    cotangent,
):
    n_rows, n_blk = sizes
    own_tokens, own_grad = tokens[0], cotangent[0]
    segments = segment_ids[0]
    tok_count, model_width = own_tokens.shape
    width = conv_weight.shape[1]
    wide = round_up(width + 2)
    heads, block, _ = decay_gate.shape
    tiles = column_tiles(width, wide, block)
    row, blk = lax.axis_index("rows"), lax.axis_index("blk")
    square = (tok_count, model_width)
    shard = branch_weight.shape[0]
    units = hidden_gate.shape[0]

    (column_parts,) = local_kernel(
        functools.partial(split_columns_kernel, width, wide),
        "split_columns",
        (input_weight, branch_weight, output_weight, mixer_gain[:, None], mlp_gain[:, None]),
        [((n_blk, shard, 3 * wide), bf16)],
    )
    columns = swap_blk(column_parts).reshape(n_blk * shard, 3 * wide)
    columns, token_own = tie(columns, own_tokens)
    both_columns = lax.all_gather(columns[:, : 2 * wide], "rows", axis=0, tiled=True)
    output_columns = lax.all_gather(columns[:, 2 * wide :], "rows", axis=0, tiled=True)
    tokens_all = gather_blk(token_own, n_blk).reshape(n_blk * tok_count, model_width)
    tokens_all, hidden_gate, hidden_up, hidden_down = tie(
        tokens_all, hidden_gate, hidden_up, hidden_down
    )
    gate_units = lax.all_gather(hidden_gate, "rows", axis=0, tiled=True)
    up_units = lax.all_gather(hidden_up, "rows", axis=0, tiled=True)
    down_units = lax.all_gather(hidden_down, "rows", axis=0, tiled=True)

    gains = both_columns[:, width : width + 2].astype(f32).T
    mixer_gains, mlp_gains = gains[0:1], gains[1:2]

    masks = [jnp.ones_like(segments, dtype=f32)]
    for tap in range(1, 4):
        masks.append(
            jnp.concatenate(
                [jnp.zeros((tap,), f32), (segments[tap:] == segments[:-tap]).astype(f32)]
            )
        )
    masks.append(1.0 - masks[1])
    masks = jnp.pad(jnp.stack(masks, axis=1), ((0, 8), (0, 3)))
    vectors = jnp.concatenate(
        [
            conv_weight,
            conv_bias[None],
            decay_bias[None],
            input_bias[None],
            scale_c * jax.nn.softplus(-decay_param)[None],
        ],
        axis=0,
    )
    vectors = jnp.pad(vectors, ((0, 0), (0, wide - width)), constant_values=1.0)
    weights = local_kernel(
        dense_kernel, "dense_gates", (decay_gate, input_gate), [((wide, wide), bf16)] * 4
    )
    (mixer_normed,) = local_kernel(
        mixer_norm_kernel,
        "mixer_norm",
        (mixer_gains, tokens_all),
        [((n_blk * tok_count, model_width), bf16)],
    )
    mixer_normed, grad_own = tie(mixer_normed, own_grad)
    out_grad = gather_blk(grad_own, n_blk).reshape(n_blk * tok_count, model_width)
    both_pre = mm(mixer_normed, both_columns, ((1,), (0,)))
    signal, branch_pre = both_pre[:, :wide].astype(bf16), both_pre[:, wide:]
    states, state_values, conv_out, decay_rate, input_rate = recur_forward(
        signal, masks, vectors, weights, tiles
    )
    branch_act, branch_pullback = jax.vjp(gelu_tanh, branch_pre)
    mixed = (branch_act * state_values.astype(f32)).astype(bf16)
    mixed, out_grad = tie(mixed, out_grad)

    def scatter_blk(partial):
        return swap_blk(partial.astype(bf16).reshape(n_blk, tok_count, model_width))

    mid_parts = scatter_blk(mm(mixed, output_columns, ((1,), (1,))))
    residual_mid, own_normed = local_kernel(
        mid_norm_kernel,
        "mid_norm",
        (mlp_gains, own_tokens, mid_parts),
        [(square, f32), (square, bf16)],
    )

    mlp_normed = gather_blk(own_normed, n_blk).reshape(n_blk * tok_count, model_width)
    gate_vals = mm(mlp_normed, gate_units, ((1,), (1,)))
    up_vals = mm(mlp_normed, up_units, ((1,), (1,)))
    gate_act, gate_pullback = jax.vjp(gelu_tanh, gate_vals)
    hidden_vals = (gate_act * up_vals).astype(bf16)
    hidden_grad = mm(out_grad, down_units, ((1,), (1,)))
    gate_grad = gate_pullback(hidden_grad * up_vals)[0].astype(bf16)
    up_grad = (hidden_grad * gate_act).astype(bf16)

    normed_partial = (
        mm(gate_grad, gate_units, ((1,), (0,))) + mm(up_grad, up_units, ((1,), (0,)))
    ).astype(bf16)
    normed_partial, gate_grad, up_grad, hidden_vals = tie(
        normed_partial, gate_grad, up_grad, hidden_vals
    )
    normed_parts = scatter_blk(normed_partial)
    unit_sums = unit_grads(
        (gate_grad, up_grad, hidden_vals), (mlp_normed, mlp_normed, out_grad), n_rows
    )
    out_partial = mm(hidden_vals, down_units, ((1,), (0,))).astype(bf16)
    normed_parts, _, out_partial = tie(normed_parts, unit_sums, out_partial)
    unit_sums = lax.psum_scatter(
        unit_sums.reshape(n_rows * 3 * units, model_width),
        "rows",
        scatter_dimension=0,
        tiled=True,
    )

    mid_grad, own_sent, mlp_gain_part = local_kernel(
        mid_grad_kernel,
        "mid_grad",
        (mlp_gains, residual_mid, own_grad, normed_parts),
        [(square, f32), (square, bf16), ((8, model_width), f32)],
    )
    mid_sent = gather_blk(own_sent, n_blk).reshape(n_blk * tok_count, model_width)

    mid_sent, out_partial = tie(mid_sent, out_partial)
    out_parts = scatter_blk(out_partial)
    mixed_grad = mm(mid_sent, output_columns, ((1,), (0,)))
    state_grad = (mixed_grad * branch_act).astype(bf16)
    branch_grad = branch_pullback(mixed_grad * state_values.astype(f32))[0].astype(bf16)

    def column_grads(left, right):
        partial = mm(left, right, ((0,), (0,))).astype(bf16)
        return partial.reshape(n_rows, 1, n_blk * shard, -1)

    early_sum = jnp.concatenate(
        [column_grads(mid_sent, mixed), column_grads(mixer_normed, branch_grad)], axis=1
    )
    signal_grad, decay_pre_grad, input_pre_grad, sums = recur_backward(
        state_grad,
        signal,
        masks,
        vectors,
        weights,
        (states, conv_out, decay_rate, input_rate),
        tiles,
    )
    signal_grad, out_parts = tie(signal_grad, out_parts)
    both_grad = jnp.concatenate([signal_grad, branch_grad], axis=1)
    partial = mm(both_grad, both_columns, ((1,), (1,)))
    token_sent, mixer_gain_part = local_kernel(
        pack_grad_kernel,
        "pack_grad",
        (partial, tokens_all),
        [((n_blk * tok_count, model_width), bf16), ((8, model_width), f32)],
    )
    token_parts = scatter_blk(token_sent)
    early_sum, unit_sums = tie(early_sum, unit_sums)
    early_sum = lax.psum_scatter(
        early_sum.reshape(n_rows * 2 * n_blk * shard, wide),
        "rows",
        scatter_dimension=0,
        tiled=True,
    ).reshape(2, n_blk * shard, wide)
    late_sum, late_left = by_bits(column_grads(mixer_normed, signal_grad)[:, 0], n_rows)
    gate_sums = jnp.stack(
        [
            diagonal_blocks(conv_out, decay_pre_grad, heads, block),
            diagonal_blocks(conv_out, input_pre_grad, heads, block),
        ]
    )
    vector_sums = sums.reshape(8, 8, wide).sum(axis=1)
    gain_sums = jnp.stack([mixer_gain_part.sum(axis=0), mlp_gain_part.sum(axis=0)])

    def add_from(value, bit, axis="rows", size=n_rows, wire=f32):
        return value + lax.ppermute(value.astype(wire), axis, flip(size, bit)).astype(f32)

    for bit in bits_of(n_rows):
        late_sum, _ = halve(late_sum, n_rows, bit, late_left)
        gate_sums = add_from(gate_sums, bit, wire=bf16)
        vector_sums = add_from(vector_sums, bit)
        gain_sums = add_from(gain_sums, bit)
        late_sum, gate_sums, vector_sums, gain_sums = tie(
            late_sum, gate_sums, vector_sums, gain_sums
        )
    for bit in bits_of(n_blk):
        gain_sums = add_from(gain_sums, bit, "blk", n_blk)
    vector_sums = vector_sums[:, :width]

    def join_columns(total):
        count = total.shape[0]
        parts = total.reshape(count, n_blk, shard, wide).transpose(1, 2, 0, 3)
        return local_kernel(
            functools.partial(join_columns_kernel, width, wide),
            "join_columns",
            (swap_blk(parts.reshape(n_blk, shard, count * wide)),),
            [((shard, n_blk * width), f32)] * count,
        )

    output_weight_grad, branch_weight_grad, input_weight_grad = join_columns(
        jnp.concatenate([early_sum, late_sum.astype(bf16)], axis=0)
    )
    block_out = (residual_mid + out_parts.astype(f32).sum(axis=0)).astype(bf16)

    (token_grad,) = local_kernel(
        token_grad_kernel,
        "token_grad",
        (mixer_gains, own_tokens, mid_grad, token_parts),
        [(square, f32)],
    )
    gain_sums = lax.dynamic_slice_in_dim(
        gain_sums, (row * n_blk + blk) * mixer_gain.shape[0], mixer_gain.shape[0], axis=1
    )

    return (
        block_out[None],
        token_grad[None],
        gain_sums[0],
        branch_weight_grad,
        input_weight_grad,
        output_weight_grad,
        vector_sums[4:8],
        vector_sums[3],
        gate_sums[0],
        vector_sums[1],
        gate_sums[1],
        vector_sums[2],
        scale_c * jax.nn.sigmoid(-decay_param) * vector_sums[0],
        gain_sums[1],
        unit_sums[:units].astype(f32),
        unit_sums[units : 2 * units].astype(f32),
        unit_sums[2 * units :].astype(f32),
    )


def solution(mesh):
    by_all = P(("rows", "blk"))
    by_all_rows = P(("rows", "blk"), None)
    tokens_spec = P("rows", "blk", None)
    by_blk = P("blk")
    by_blk_heads = P("blk", None, None)
    taps = P(None, "blk")
    recurrence = (taps, by_blk, by_blk_heads, by_blk, by_blk_heads, by_blk, by_blk)
    return jax.shard_map(
        functools.partial(body, (mesh.shape["rows"], mesh.shape["blk"])),
        mesh=mesh,
        in_specs=(tokens_spec, P("rows", None), by_all)
        + (by_all_rows,) * 3
        + recurrence
        + (by_all,)
        + (by_all_rows,) * 3
        + (tokens_spec,),
        out_specs=(tokens_spec, tokens_spec, by_all)
        + (by_all_rows,) * 3
        + recurrence
        + (by_all,)
        + (by_all_rows,) * 3,
        check_vma=False,
    )
```

time: 4350 us -> 649 us (0.15)
  waiting for transfers between devices: 2410 us -> 178 us
  local copies, waits for them, and re-layouts: 1280 us -> 39.7 us
  other arithmetic: 261 us -> 32.7 us
  matrix products: 246 us -> 82.8 us
  blocking collectives: 111 us -> 186 us
  Pallas kernels: 0 us -> 62.9 us
    unnamed x11 -> x7, waiting for transfers between devices: 2290 us -> 1.14 us
    slice x68 -> x8, local copies, waits for them, and re-layouts: 537 us -> 4.66 us  [the longest x1 2.12 us: body(): columns[:, :2 * wide]]
    pad x70 -> x2, local copies, waits for them, and re-layouts: 484 us -> 0.03 us  [the longest x1 0.02 us: body(): masks = jnp.pad(jnp.stack(masks, axis=1), ((0, 8), (0, 3)))]
    unnamed x468 -> x114, local copies, waits for them, and re-layouts: 238 us -> 21.5 us
    all_to_all x0 -> x4, blocking collectives: none -> 186 us  [swap_blk(): return lax.all_to_all(parts, 'blk', split_axis=0, concat_axis=0, tiled=True)]
    dot_general x24 -> x15, matrix products: 246 us -> 82.8 us  [the longest x13 75.9 us: mm(): lax.dot_general(left, right, (dims, ((), ())), preferred_element_type=f32)]
    concatenate x11 -> x3, other arithmetic: 157 us -> 3.4 us  [the longest x1 3.25 us: body(): jnp.concatenate([column_grads(mid_sent, mixed), column_grads(mixer_normed...]
    unnamed x2 -> x0, blocking collectives: 85.7 us -> none
  transfers between devices with their start and end apart: 13 -> 27, of which waited for: 7 -> 10; matrix products, arithmetic and copies ran while one was open for 26% -> 17% of each run, Pallas kernels for 0% -> 7%
where the time goes in v1:
time: 649 us; the launch traced here: 640 us
  blocking collectives  186 us (29%)
  waiting for transfers between devices  178 us (27%)
  matrix products  82.8 us (13%)
  Pallas kernels  62.9 us (10%)
  starting transfers between devices  43.7 us (7%)
  local copies, waits for them, and re-layouts  39.7 us (6%)
  other arithmetic  32.7 us (5%)
  between operations  15.5 us (2%)
    all_to_all x4, blocking collectives, swap_blk(): return lax.all_to_all(parts, 'blk', split_axis=0, concat_axis=0, tiled=True)  186 us
    all_to_all x6, waiting for transfers between devices, swap_blk(): return lax.all_to_all(parts, 'blk', split_axis=0, concat_axis=0, tiled=True)  109 us
    dot_general x13, matrix products, mm(): lax.dot_general(left, right, (dims, ((), ())), preferred_element_type=f32)  75.9 us
    ppermute x11, waiting for transfers between devices, add_from(): lax.ppermute(value.astype(wire), axis, flip(size, bit)).astype(f32)  62.3 us
    pallas_call x10, Pallas kernels, local_kernel(): pl.pallas_call(kernel, out_shape=[jax.ShapeDtypeStruct(shape, kind) for s...  46.9 us
    all_to_all x6, starting transfers between devices, swap_blk(): return lax.all_to_all(parts, 'blk', split_axis=0, concat_axis=0, tiled=True)  26.2 us
    unnamed x114, local copies, waits for them, and re-layouts  21.5 us
    pallas_call x1, Pallas kernels, unit_grads(): pl.pallas_call(unit_grads_kernel, grid=(parts // group,), out_shape=jax.S...  16 us
  transfers between devices with their start and end apart: 27, of which 10 were waited for; matrix products, arithmetic and copies ran while one was open for 17% of the time, Pallas kernels for 7%

profile of v1, /device:TPU:0, one launch (start us, length us, event | category | flops | bytes accessed | tf_op | source)
XLA Modules:
  0.0 640.4 jit_solution(14462688828519752730)
XLA Ops:
  12.1 34.7 %all_to_all.50 = bf16[4,64,2304]{2,1,0:T(8,128)(2,1)S(1)} all-to-all(bf16[4,64,2304]{2,1,0:T(8,128)(2,1)S(1)} %split_columns.1), channel_id=1, replica_groups=mesh['rows'=8,'blk'=4] {'blk'}, dimensions={0} | all-to-all | bytes 2359296 | tf_op jit(solution)/shard_map/all_to_all | solution.py:47
  51.5 50.3 %all_to_all.51 = bf16[4,128,2048]{2,1,0:T(8,128)(2,1)S(1)} all-to-all(bf16[4,128,2048]{2,1,0:T(8,128)(2,1)S(1)} %broadcast_in_dim.48), channel_id=1, replica_groups=mesh['rows'=8,'blk'=4] {'blk'}, dimensions={0} | all-to-all | bytes 4194304 | tf_op jit(solution)/shard_map/all_to_all | solution.py:47
  108.8 4.6 all-to-all-start.2
  118.0 7.5 %fusion.30 = f32[512,1536]{1,0:T(8,128)S(1)} fusion(bf16[512,2048]{1,0:T(8,128)(2,1)S(1)} %copy-done.14, bf16[2048,1536]{0,1:T(8,128)(2,1)} %all-gather.6.cloned.1.call-done), kind=kOutput, calls=%fused_computation.92 | convolution fusion | flops 3221225472 | bytes 11534336 | tf_op jit(solution)/shard_map/dot_general | solution.py:27
  125.7 13.8 %recur_forward.1 = (f32[512,768]{1,0:T(8,128)}, bf16[512,768]{1,0:T(8,128)(2,1)S(1)}, f32[512,768]{1,0:T(8,128)}, f32[512,768]{1,0:T(8,128)}, f32[512,768]{1,0:T(8,128)}) custom-call(bf16[512,768]{1,0:T(8,128)(2,1)S(1)} %slice.189.signal_ref, f32[520,8]{1,0:T(8,128)S(1)} %pad.12.masks_ref, f32[8,768]{1,0:T(8,128)S(1)} %pad.13.vectors_ref, ...), custom_call_target="tpu_custom_call" | custom-call | tf_op jit(solution)/shard_map/recur_forward/pallas_call | solution.py:191
  141.9 18.8 %all-to-all-done.2 = bf16[4,128,2048]{2,1,0:T(8,128)(2,1)} async-done(((bf16[4,128,2048]{2,1,0:T(8,128)(2,1)}), bf16[4,128,2048]{2,1,0:T(8,128)(2,1)}, u32[]{:S(2)}, u32[]{:S(2)}) %all-to-all-start.2) | async-done | bytes 2097184 | tf_op jit(solution)/shard_map/all_to_all | solution.py:47
  160.7 4.0 convolution_convert_fusion.4
  164.7 50.2 %all_to_all.52.parts_ref = bf16[4,128,2048]{2,1,0:T(8,128)(2,1)S(1)} all-to-all(bf16[4,128,2048]{2,1,0:T(8,128)(2,1)S(1)} %bitcast.120), channel_id=1, replica_groups=mesh['rows'=8,'blk'=4] {'blk'}, dimensions={0} | all-to-all | bytes 4194304 | tf_op jit(solution)/shard_map/all_to_all | solution.py:47
  218.2 4.5 all-to-all-start.4
  223.0 8.6 %fusion.31 = f32[512,1536]{1,0:T(8,128)} fusion(bf16[512,2048]{1,0:T(8,128)(2,1)} %bitcast.12.refs_5_, bf16[1536,2048]{1,0:T(8,128)(2,1)} %all-gather.10.cloned.1.call-done), kind=kOutput, calls=%fused_computation.93 | convolution fusion | flops 3221225472 | bytes 11534336 | tf_op jit(solution)/shard_map/dot_general | solution.py:27
  231.6 38.4 %all-to-all-done.4 = bf16[4,128,2048]{2,1,0:T(8,128)(2,1)} async-done(((bf16[4,128,2048]{2,1,0:T(8,128)(2,1)}), bf16[4,128,2048]{2,1,0:T(8,128)(2,1)}, u32[]{:S(2)}, u32[]{:S(2)}) %all-to-all-start.4) | async-done | bytes 2097184 | tf_op jit(solution)/shard_map/all_to_all | solution.py:47
  270.0 8.6 %fusion.32 = f32[512,1536]{1,0:T(8,128)} fusion(bf16[512,2048]{1,0:T(8,128)(2,1)} %bitcast.14.refs_3_.refs_4_, bf16[1536,2048]{1,0:T(8,128)(2,1)} %all-gather.14.cloned.1.call-done), kind=kOutput, calls=%fused_computation.94 | convolution fusion | flops 3221225472 | bytes 11534336 | tf_op jit(solution)/shard_map/dot_general | solution.py:27
  278.6 10.9 %multiply_convert_fusion = (bf16[512,1536]{1,0:T(8,128)(2,1)S(1)}, bf16[512,1536]{1,0:T(8,128)(2,1)S(1)}, bf16[512,1536]{1,0:T(8,128)(2,1)S(1)}) fusion(f32[512,1536]{1,0:T(8,128)} %fusion.32, f32[512,1536]{1,0:T(8,128)} %fusion.31, bf16[512,2048]{1,0:T(8,128)(2,1)} %bitcast.14.refs_3_.refs_4_, bf16[1536,2048]{1,0:T(8,128)(2,1)} %all-gather.12.cloned.1.call-done), kind=kOutput, calls=%fused_computation.16 | convolution fusion | flops 3241672704 | bytes 19398656 | tf_op jit(solution)/shard_map/dot_general | solution.py:27
  289.5 3.8 fusion.33
  293.4 4.8 add_convert_fusion
  298.2 16.0 %unit_grads.1 = bf16[8,3,192,2048]{3,2,1,0:T(8,128)(2,1)} custom-call(bf16[512,1536]{1,0:T(8,128)(2,1)S(1)} %get-tuple-element.92.refs_0_, bf16[512,1536]{1,0:T(8,128)(2,1)S(1)} %get-tuple-element.93.refs_1_, bf16[512,1536]{1,0:T(8,128)(2,1)S(1)} %get-tuple-element.94.refs_2_, bf16[512,2048]{1,0:T(8,128)(2,1)} %bitcast.14.refs_3_.refs_4_, ...), custom_call_target="tpu_custom_call" | custom-call | flops 1024 | bytes 1024 | tf_op jit(solution)/shard_map/unit_grads/pallas_call | solution.py:548
  314.2 4.5 all-to-all-start.5
  318.7 8.7 %convolution_convert_fusion.3 = bf16[512,2048]{1,0:T(8,128)(2,1)} fusion(bf16[512,1536]{1,0:T(8,128)(2,1)} %copy-done.17, bf16[1536,2048]{1,0:T(8,128)(2,1)} %all-gather.10.cloned.1.call-done), kind=kOutput, calls=%fused_computation.18 | convolution fusion | flops 3222274048 | bytes 9961472 | tf_op jit(solution)/shard_map/dot_general | solution.py:27
  327.4 38.9 %all-to-all-done.5.parts_ref = bf16[4,128,2048]{2,1,0:T(8,128)(2,1)} async-done(((bf16[4,128,2048]{2,1,0:T(8,128)(2,1)}), bf16[4,128,2048]{2,1,0:T(8,128)(2,1)}, u32[]{:S(2)}, u32[]{:S(2)}) %all-to-all-start.5) | async-done | bytes 2097184 | tf_op jit(solution)/shard_map/all_to_all | solution.py:47
  371.4 50.5 %all_to_all.53 = bf16[4,128,2048]{2,1,0:T(8,128)(2,1)S(1)} all-to-all(bf16[4,128,2048]{2,1,0:T(8,128)(2,1)S(1)} %broadcast_in_dim.54), channel_id=1, replica_groups=mesh['rows'=8,'blk'=4] {'blk'}, dimensions={0} | all-to-all | bytes 4194304 | tf_op jit(solution)/shard_map/all_to_all | solution.py:47
  434.1 5.4 reduce-scatter.3.cloned.1.call-done
  439.5 4.6 all-to-all-start.7
  449.0 17.5 %recur_backward.1 = (bf16[512,768]{1,0:T(8,128)(2,1)S(1)}, f32[512,768]{1,0:T(8,128)}, f32[512,768]{1,0:T(8,128)}, f32[64,768]{1,0:T(8,128)S(1)}) custom-call(bf16[512,768]{1,0:T(8,128)(2,1)S(1)} %copy-done.22, bf16[512,768]{1,0:T(8,128)(2,1)S(1)} %slice.189.signal_ref, f32[520,8]{1,0:T(8,128)S(1)} %copy-done.10, f32[8,768]{1,0:T(8,128)S(1)} %pad.13.vectors_ref, ...), custom_call_target="tpu_custom_call" | custom-call | tf_op jit(solution)/shard_map/recur_backward/pallas_call | solution.py:191
  466.6 4.4 fusion.35
  479.9 12.6 %all-to-all-done.7 = bf16[4,128,2048]{2,1,0:T(8,128)(2,1)} async-done(((bf16[4,128,2048]{2,1,0:T(8,128)(2,1)}), bf16[4,128,2048]{2,1,0:T(8,128)(2,1)}, u32[]{:S(2)}, u32[]{:S(2)}) %all-to-all-start.7) | async-done | bytes 2097184 | tf_op jit(solution)/shard_map/all_to_all | solution.py:47
  498.8 8.1 %fusion.15.partial_ref = f32[512,2048]{1,0:T(8,128)} fusion(bf16[2048,1536]{0,1:T(8,128)(2,1)} %all-gather.6.cloned.1.call-done, bf16[512,768]{1,0:T(8,128)(2,1)S(1)} %copy-done.55, bf16[512,768]{1,0:T(8,128)(2,1)S(1)} %copy-done.27), kind=kOutput, calls=%fused_computation.34 | convolution fusion | flops 3224371200 | bytes 12058624 | tf_op jit(solution)/shard_map/dot_general | solution.py:27
  506.9 4.4 pack_grad.1
  529.0 28.5 %collective-permute-done.7 = f32[2,2048]{1,0:T(2,128)S(1)} collective-permute-done((f32[2,2048]{1,0:T(2,128)S(1)}, f32[2,2048]{1,0:T(2,128)S(1)}, u32[]{:S(2)}, u32[]{:S(2)}) %collective-permute-start.7) | collective-permute-done | bytes 16416 | tf_op jit(solution)/shard_map/ppermute | solution.py:753
  569.6 18.0 %collective-permute-done.11 = f32[2,2048]{1,0:T(2,128)S(1)} collective-permute-done((f32[2,2048]{1,0:T(2,128)S(1)}, f32[2,2048]{1,0:T(2,128)S(1)}, u32[]{:S(2)}, u32[]{:S(2)}) %collective-permute-start.11) | collective-permute-done | bytes 16416 | tf_op jit(solution)/shard_map/ppermute | solution.py:753
  592.9 4.4 all-to-all-start.9
  603.9 11.9 %collective-permute-done.12 = f32[2,2048]{1,0:T(2,128)S(1)} collective-permute-done((f32[2,2048]{1,0:T(2,128)S(1)}, f32[2,2048]{1,0:T(2,128)S(1)}, u32[]{:S(2)}, u32[]{:S(2)}) %collective-permute-start.12) | collective-permute-done | bytes 16416 | tf_op jit(solution)/shard_map/ppermute | solution.py:753
  615.8 4.8 collective-permute-start.13
  (252 shorter events, 118.5 us)
Async XLA Ops:
  7.2 95.7 %all-gather.6.cloned.1.call-start = ((), (), s32[]{:S(2)}) async-start(), calls=%async_computation.12 | async-start | bytes 7077888 | tf_op jit(solution)/shard_map/all_gather | solution.py:603
  50.3 110.4 %all-gather.8.cloned.1.call-start = ((), (), s32[]{:S(2)}) async-start(), calls=%async_computation.13 | async-start | bytes 3538944 | tf_op jit(solution)/shard_map/all_gather | solution.py:604
  51.2 171.8 %all-gather.10.cloned.1.call-start = ((), (), s32[]{:S(2)}) async-start(), calls=%async_computation.14 | async-start | bytes 7077888 | tf_op jit(solution)/shard_map/all_gather | solution.py:611
  101.8 129.8 %all-gather.14.cloned.1.call-start = ((), (), s32[]{:S(2)}) async-start(), calls=%async_computation.16 | async-start | bytes 7077888 | tf_op jit(solution)/shard_map/all_gather | solution.py:609
  102.3 176.3 %all-gather.12.cloned.1.call-start = ((), (), s32[]{:S(2)}) async-start(), calls=%async_computation.15 | async-start | bytes 7077888 | tf_op jit(solution)/shard_map/all_gather | solution.py:610
  108.8 51.9 %all-to-all-start.2 = ((bf16[4,128,2048]{2,1,0:T(8,128)(2,1)}), bf16[4,128,2048]{2,1,0:T(8,128)(2,1)}, u32[]{:S(2)}, u32[]{:S(2)}) async-start(bf16[4,128,2048]{2,1,0:T(8,128)(2,1)} %broadcast_in_dim.52), calls=%async_computation.2 | async-start | bytes 4194304 | tf_op jit(solution)/shard_map/all_to_all | solution.py:47
  218.2 51.8 %all-to-all-start.4 = ((bf16[4,128,2048]{2,1,0:T(8,128)(2,1)}), bf16[4,128,2048]{2,1,0:T(8,128)(2,1)}, u32[]{:S(2)}, u32[]{:S(2)}) async-start(bf16[4,128,2048]{2,1,0:T(8,128)(2,1)} %broadcast_in_dim.53), calls=%async_computation.4 | async-start | bytes 4194304 | tf_op jit(solution)/shard_map/all_to_all | solution.py:47
  222.7 216.8 %reduce-scatter.3.cloned.1.call-start = ((), (), s32[]{:S(2)}) async-start(), calls=%async_computation.17 | async-start | bytes 21233664 | tf_op jit(solution)/shard_map/reduce_scatter | solution.py:688
  314.2 52.1 %all-to-all-start.5 = ((bf16[4,128,2048]{2,1,0:T(8,128)(2,1)}), bf16[4,128,2048]{2,1,0:T(8,128)(2,1)}, u32[]{:S(2)}, u32[]{:S(2)}) async-start(bf16[4,128,2048]{2,1,0:T(8,128)(2,1)} %bitcast.117), calls=%async_computation.5 | async-start | bytes 4194304 | tf_op jit(solution)/shard_map/all_to_all | solution.py:47
  318.6 271.9 %reduce-scatter.5.cloned.1.call-start = ((), (), s32[]{:S(2)}) async-start(), calls=%async_computation.18 | async-start | bytes 7077888 | tf_op jit(solution)/shard_map/reduce_scatter | solution.py:736
  371.1 50.8 %copy-start.18 = (f32[128,2048]{1,0:T(8,128)}, f32[128,2048]{1,0:T(8,128)S(1)}, u32[]{:S(2)}) copy-start(f32[128,2048]{1,0:T(8,128)S(1)} %get-tuple-element.106.mid_grad_ref) | copy-start | bytes 3145732
  371.3 50.5 %copy-start.44 = (bf16[512,768]{1,0:T(8,128)(2,1)S(1)}, bf16[512,768]{1,0:T(8,128)(2,1)}, u32[]{:S(2)}) copy-start(bf16[512,768]{1,0:T(8,128)(2,1)} %fusion.7) | copy-start | bytes 2359300
  439.5 53.0 %all-to-all-start.7 = ((bf16[4,128,2048]{2,1,0:T(8,128)(2,1)}), bf16[4,128,2048]{2,1,0:T(8,128)(2,1)}, u32[]{:S(2)}, u32[]{:S(2)}) async-start(bf16[4,128,2048]{2,1,0:T(8,128)(2,1)} %bitcast.116), calls=%async_computation.7 | async-start | bytes 4194304 | tf_op jit(solution)/shard_map/all_to_all | solution.py:47
  466.5 13.4 %collective-permute-start.2 = (f32[8,768]{1,0:T(8,128)S(1)}, f32[8,768]{1,0:T(8,128)S(1)}, u32[]{:S(2)}, u32[]{:S(2)}) collective-permute-start(f32[8,768]{1,0:T(8,128)S(1)} %bitcast_reduce_fusion), channel_id=1, source_target_pairs={{0,4},{4,0},{8,12},{12,8},{16,20},{20,16},{24,28},{28,24},{1,5},{5... | collective-permute-start | bytes 73736 | tf_op jit(solution)/shard_map/ppermute | solution.py:753
  479.6 33.4 %collective-permute-start.1 = (bf16[2,4,171,171]{3,1,2,0:T(4,128)(2,1)}, bf16[2,4,171,171]{3,1,2,0:T(4,128)(2,1)}, u32[]{:S(2)}, u32[]{:S(2)}) collective-permute-start(bf16[2,4,171,171]{3,1,2,0:T(4,128)(2,1)} %fusion.19), channel_id=1, source_target_pairs={{0,4},{4,0},{8,12},{12,8},{16,20},{20,16},{24,28},{28,24},{1,5},{5... | collective-permute-start | bytes 1403576 | tf_op jit(solution)/shard_map/ppermute | solution.py:753
  498.6 20.9 %collective-permute-start = (bf16[2,2,1,256,768]{4,3,0,2,1:T(8,128)(2,1)}, bf16[2,2,1,256,768]{4,3,0,2,1:T(8,128)(2,1)}, u32[]{:S(2)}, u32[]{:S(2)}) collective-permute-start(bf16[2,2,1,256,768]{4,3,0,2,1:T(8,128)(2,1)} %bitcast.99), channel_id=1, source_target_pairs={{0,4},{4,0},{8,12},{12,8},{16,20},{20,16},{24,28},{28,24},{1,5},{5... | collective-permute-start | bytes 4718600 | tf_op jit(solution)/shard_map/ppermute | solution.py:60
  512.6 6.9 %collective-permute-start.3 = (f32[2,2048]{1,0:T(2,128)S(1)}, f32[2,2048]{1,0:T(2,128)S(1)}, u32[]{:S(2)}, u32[]{:S(2)}) collective-permute-start(f32[2,2048]{1,0:T(2,128)S(1)} %pad_maximum_fusion.2), channel_id=1, source_target_pairs={{0,4},{4,0},{8,12},{12,8},{16,20},{20,16},{24,28},{28,24},{1,5},{5... | collective-permute-start | bytes 49160 | tf_op jit(solution)/shard_map/ppermute | solution.py:753
  515.9 77.0 %all-to-all-start.8 = ((bf16[4,128,2048]{2,1,0:T(8,128)(2,1)}), bf16[4,128,2048]{2,1,0:T(8,128)(2,1)S(1)}, u32[]{:S(2)}, u32[]{:S(2)}) async-start(bf16[4,128,2048]{2,1,0:T(8,128)(2,1)} %bitcast.107), calls=%async_computation.8 | async-start | bytes 4194304 | tf_op jit(solution)/shard_map/all_to_all | solution.py:47
  521.9 37.5 %collective-permute-start.4 = (bf16[2,1,256,768]{3,2,1,0:T(8,128)(2,1)S(1)}, bf16[2,1,256,768]{3,2,1,0:T(8,128)(2,1)}, u32[]{:S(2)}, u32[]{:S(2)}) collective-permute-start(bf16[2,1,256,768]{3,2,1,0:T(8,128)(2,1)S(1)} %fusion.20), channel_id=1, source_target_pairs={{0,8},{4,12},{8,0},{12,4},{16,24},{20,28},{24,16},{28,20},{1,9},{5... | collective-permute-start | bytes 2359304 | tf_op jit(solution)/shard_map/ppermute | solution.py:60
  525.3 32.2 %collective-permute-start.5 = (bf16[2,4,171,171]{3,1,2,0:T(4,128)(2,1)}, bf16[2,4,171,171]{3,1,2,0:T(4,128)(2,1)}, u32[]{:S(2)}, u32[]{:S(2)}) collective-permute-start(bf16[2,4,171,171]{3,1,2,0:T(4,128)(2,1)} %convert_element_type.176), channel_id=1, source_target_pairs={{0,8},{4,12},{8,0},{12,4},{16,24},{20,28},{24,16},{28,20},{1,9},{5... | collective-permute-start | bytes 1403576 | tf_op jit(solution)/shard_map/ppermute | solution.py:753
  527.0 30.6 %collective-permute-start.6 = (f32[8,768]{1,0:T(8,128)S(1)}, f32[8,768]{1,0:T(8,128)S(1)}, u32[]{:S(2)}, u32[]{:S(2)}) collective-permute-start(f32[8,768]{1,0:T(8,128)S(1)} %add.132), channel_id=1, source_target_pairs={{0,8},{4,12},{8,0},{12,4},{16,24},{20,28},{24,16},{28,20},{1,9},{5... | collective-permute-start | bytes 73736 | tf_op jit(solution)/shard_map/ppermute | solution.py:753
  527.3 30.2 %collective-permute-start.7 = (f32[2,2048]{1,0:T(2,128)S(1)}, f32[2,2048]{1,0:T(2,128)S(1)}, u32[]{:S(2)}, u32[]{:S(2)}) collective-permute-start(f32[2,2048]{1,0:T(2,128)S(1)} %fusion.26), channel_id=1, source_target_pairs={{0,8},{4,12},{8,0},{12,4},{16,24},{20,28},{24,16},{28,20},{1,9},{5... | collective-permute-start | bytes 49160 | tf_op jit(solution)/shard_map/ppermute | solution.py:753
  529.0 30.5 %copy-start.33 = (f32[2,2,1,256,768]{4,3,0,2,1:T(8,128)S(1)}, f32[2,2,1,256,768]{4,3,0,2,1:T(8,128)}, u32[]{:S(2)}) copy-start(f32[2,2,1,256,768]{4,3,0,2,1:T(8,128)} %copy-done.32) | copy-start | bytes 9437188
  561.3 26.5 %collective-permute-start.8 = (bf16[1,256,768]{2,1,0:T(8,128)(2,1)S(1)}, bf16[1,256,768]{2,1,0:T(8,128)(2,1)S(1)}, u32[]{:S(2)}, u32[]{:S(2)}) collective-permute-start(bf16[1,256,768]{2,1,0:T(8,128)(2,1)S(1)} %fusion.22), channel_id=1, source_target_pairs={{0,16},{4,20},{8,24},{12,28},{16,0},{20,4},{24,8},{28,12},{1,17},{... | collective-permute-start | bytes 1179656 | tf_op jit(solution)/shard_map/ppermute | solution.py:60
  564.2 23.7 %collective-permute-start.9 = (bf16[2,4,171,171]{3,1,2,0:T(4,128)(2,1)}, bf16[2,4,171,171]{3,1,2,0:T(4,128)(2,1)}, u32[]{:S(2)}, u32[]{:S(2)}) collective-permute-start(bf16[2,4,171,171]{3,1,2,0:T(4,128)(2,1)} %convert_element_type.181), channel_id=1, source_target_pairs={{0,16},{4,20},{8,24},{12,28},{16,0},{20,4},{24,8},{28,12},{1,17},{... | collective-permute-start | bytes 1403576 | tf_op jit(solution)/shard_map/ppermute | solution.py:753
  564.5 23.4 %copy-start.31 = (f32[2,4,171,171]{3,1,2,0:T(4,128)S(1)}, f32[2,4,171,171]{3,1,2,0:T(4,128)}, u32[]{:S(2)}) copy-start(f32[2,4,171,171]{3,1,2,0:T(4,128)} %copy-done.30) | copy-start | bytes 2807140
  564.5 23.0 %collective-permute-start.11 = (f32[2,2048]{1,0:T(2,128)S(1)}, f32[2,2048]{1,0:T(2,128)S(1)}, u32[]{:S(2)}, u32[]{:S(2)}) collective-permute-start(f32[2,2048]{1,0:T(2,128)S(1)} %add.140), channel_id=1, source_target_pairs={{0,16},{4,20},{8,24},{12,28},{16,0},{20,4},{24,8},{28,12},{1,17},{... | collective-permute-start | bytes 49160 | tf_op jit(solution)/shard_map/ppermute | solution.py:753
  566.3 21.6 %collective-permute-start.10 = (f32[8,768]{1,0:T(8,128)S(1)}, f32[8,768]{1,0:T(8,128)S(1)}, u32[]{:S(2)}, u32[]{:S(2)}) collective-permute-start(f32[8,768]{1,0:T(8,128)S(1)} %add.139), channel_id=1, source_target_pairs={{0,16},{4,20},{8,24},{12,28},{16,0},{20,4},{24,8},{28,12},{1,17},{... | collective-permute-start | bytes 73736 | tf_op jit(solution)/shard_map/ppermute | solution.py:753
  592.9 37.4 %all-to-all-start.9 = ((bf16[4,64,2304]{2,1,0:T(8,128)(2,1)}), bf16[4,64,2304]{2,1,0:T(8,128)(2,1)}, u32[]{:S(2)}, u32[]{:S(2)}) async-start(bf16[4,64,2304]{2,1,0:T(8,128)(2,1)} %bitcast.112), calls=%async_computation.11 | async-start | bytes 2359296 | tf_op jit(solution)/shard_map/all_to_all | solution.py:47
  599.9 26.2 %copy-start.19 = (f32[128,2048]{1,0:T(8,128)S(1)}, f32[128,2048]{1,0:T(8,128)}, u32[]{:S(2)}) copy-start(f32[128,2048]{1,0:T(8,128)} %copy-done.18) | copy-start | bytes 3145732
  599.9 15.9 %collective-permute-start.12 = (f32[2,2048]{1,0:T(2,128)S(1)}, f32[2,2048]{1,0:T(2,128)S(1)}, u32[]{:S(2)}, u32[]{:S(2)}) collective-permute-start(f32[2,2048]{1,0:T(2,128)S(1)} %add.147), channel_id=1, source_target_pairs={{0,1},{1,0},{2,3},{3,2},{4,5},{5,4},{6,7},{7,6},{8,9},{9,8},{10,11... | collective-permute-start | bytes 49160 | tf_op jit(solution)/shard_map/ppermute | solution.py:753
  615.8 9.7 %collective-permute-start.13 = (f32[2,2048]{1,0:T(2,128)S(1)}, f32[2,2048]{1,0:T(2,128)S(1)}, u32[]{:S(2)}, u32[]{:S(2)}) collective-permute-start(f32[2,2048]{1,0:T(2,128)S(1)} %add.148), channel_id=1, source_target_pairs={{0,2},{1,3},{2,0},{3,1},{4,6},{5,7},{6,4},{7,5},{8,10},{9,11},{10,... | collective-permute-start | bytes 49160 | tf_op jit(solution)/shard_map/ppermute | solution.py:753
  (51 other events, 235.1 us)
Sparse Core Ops, SparseCore 0:
  50.4 45.7 all-gather.5
  98.7 32.3 all-gather.7
  133.0 45.5 all-gather.9
  180.3 45.5 all-gather.13
  227.6 45.5 all-gather.11
  314.3 125.1 reduce-scatter.2
  442.9 61.7 reduce-scatter.4

commit v2 on v1

--- a/solution.py
+++ b/solution.py
@@ -12,7 +12,8 @@
 bf16 = jnp.bfloat16
 f32 = jnp.float32
 chunk = 64
-vmem_limit = 48 * 1024 * 1024
+gain_rows = 16
+vmem_limit = 60 * 1024 * 1024
 
 
 def rms_scale(values):
@@ -23,8 +24,22 @@
     return jax.nn.gelu(values, approximate=True)
 
 
+def gelu_parts(values):
+    slope, cubic = 0.7978845608028654, 0.044715
+    square = values * values
+    bend = jnp.tanh(slope * values * (1.0 + cubic * square))
+    lift = 0.5 + 0.5 * bend
+    turn = 0.5 * values * (1.0 - bend * bend) * (slope * (1.0 + 3.0 * cubic * square))
+    return values * lift, lift + turn
+
+
 def mm(left, right, dims):
     return lax.dot_general(left, right, (dims, ((), ())), preferred_element_type=f32)
+
+
+def split_bf16(value):
+    high = value.astype(bf16)
+    return high, (value - high.astype(f32)).astype(bf16)
 
 
 def tie(*values):
@@ -47,34 +62,28 @@
     return lax.all_to_all(parts, "blk", split_axis=0, concat_axis=0, tiled=True)
 
 
-def gather_blk(part, size):
-    return swap_blk(jnp.broadcast_to(part[None], (size,) + part.shape))
-
-
-def halve(total, size, bit, left):
-    axis = left.index(bit)
-    left.remove(bit)
-    mine = (lax.axis_index("rows") // bit) % 2
-    away = lax.dynamic_index_in_dim(total, 1 - mine, axis, keepdims=False)
-    keep = lax.dynamic_index_in_dim(total, mine, axis, keepdims=False)
-    got = lax.ppermute(away.astype(bf16), "rows", flip(size, bit))
-    return keep.astype(f32) + got.astype(f32), got
-
-
-def by_bits(total, size):
-    left = list(reversed(bits_of(size)))
-    return total.reshape((2,) * len(left) + (total.shape[0] // size,) + total.shape[1:]), left
-
-
-def sum_rows(value, size, wire=f32):
+def ring_blk(part, size):
+    me, rows = lax.axis_index("blk"), part.shape[0]
+    whole = jnp.zeros((size * rows,) + part.shape[1:], part.dtype)
+    whole = lax.dynamic_update_slice_in_dim(whole, part, me * rows, axis=0)
+    for step in range(1, size):
+        part = lax.ppermute(part, "blk", [(place, (place + 1) % size) for place in range(size)])
+        place = (me - step) % size
+        whole = lax.dynamic_update_slice_in_dim(whole, part, place * rows, axis=0)
+    return whole
+
+
+def for_all(part, size):
+    return jnp.broadcast_to(part[None], (size,) + part.shape)
+
+
+def add_from(value, size, bit, wire=f32):
+    return value + lax.ppermute(value.astype(wire), "rows", flip(size, bit)).astype(f32)
+
+
+def sum_rows(value, size):
     for bit in bits_of(size):
-        value = value + lax.ppermute(value.astype(wire), "rows", flip(size, bit)).astype(f32)
-    return value
-
-
-def sum_blk(value, size):
-    for bit in bits_of(size):
-        value = value + lax.ppermute(value, "blk", flip(size, bit))
+        value = add_from(value, size, bit)
     return value
 
 
@@ -92,21 +101,25 @@
         both_ref[part, :, width + 1 : width + 2] = mlp_ref[...]
 
 
-def join_columns_kernel(width, wide, parts_ref, *out_refs):
+def join_columns_kernel(width, parts_ref, *out_refs):
     for part in range(parts_ref.shape[0]):
         cut = slice(part * width, (part + 1) * width)
         for number, out_ref in enumerate(out_refs):
-            begin = number * wide
-            out_ref[:, cut] = parts_ref[part, :, begin : begin + width].astype(f32)
-
-
-def mixer_norm_kernel(gain_ref, tokens_ref, out_ref):
-    step = 32
+            out_ref[:, cut] = parts_ref[part, number, :, :width].astype(f32)
+
+
+def mixer_in_kernel(width, tokens_ref, columns_ref, normed_ref, pre_ref, gains_ref):
+    step = 256
+    begin = width // 128 * 128
+    turned = columns_ref[:, begin : begin + 128].astype(f32).T
+    gains_ref[...] = turned[width - begin : width - begin + 2, :]
+    gain = gains_ref[0:1, :]
 
     def rows_step(index, carry):
         here = pl.ds(pl.multiple_of(index * step, step), step)
         values = tokens_ref[here, :].astype(f32)
-        out_ref[here, :] = (values * rms_scale(values) * gain_ref[...]).astype(bf16)
+        normed_ref[here, :] = (values * rms_scale(values) * gain).astype(bf16)
+        pre_ref[here, :] = mm(normed_ref[here, :], columns_ref[...], ((1,), (0,)))
         return carry
 
     lax.fori_loop(0, tokens_ref.shape[0] // step, rows_step, 0)
@@ -126,7 +139,8 @@
         here = pl.ds(pl.multiple_of(index * step, step), step)
         values = tokens_ref[here, :].astype(f32) + sum_parts(parts_ref, here)
         mid_ref[here, :] = values
-        normed_ref[here, :] = (values * rms_scale(values) * gain_ref[...]).astype(bf16)
+        normed = (values * rms_scale(values) * gain_ref[...]).astype(bf16)
+        normed_ref[here, :] = normed
         return carry
 
     lax.fori_loop(0, tokens_ref.shape[0] // step, rows_step, 0)
@@ -153,29 +167,19 @@
         sums_ref[...] += fold8(terms)
         result = cotangent_ref[here, :].astype(f32) + change
         grad_ref[here, :] = result
-        sent_ref[here, :] = result.astype(bf16)
+        sent = result.astype(bf16)
+        sent_ref[here, :] = sent
         return carry
 
     lax.fori_loop(0, mid_ref.shape[0] // step, rows_step, 0)
 
 
-def pack_grad_kernel(partial_ref, tokens_ref, sent_ref, sums_ref):
+def token_grad_kernel(gain_ref, tokens_ref, mid_grad_ref, parts_ref, grad_ref, gains_ref):
     step = 32
-    sums_ref[...] = jnp.zeros_like(sums_ref)
-
-    def rows_step(index, carry):
-        here = pl.ds(pl.multiple_of(index * step, step), step)
-        values = tokens_ref[here, :].astype(f32)
-        grad = partial_ref[here, :]
-        sums_ref[...] += fold8(values * rms_scale(values) * grad)
-        sent_ref[here, :] = grad.astype(bf16)
-        return carry
-
-    lax.fori_loop(0, partial_ref.shape[0] // step, rows_step, 0)
-
-
-def token_grad_kernel(gain_ref, tokens_ref, mid_grad_ref, parts_ref, grad_ref):
-    step = 32
+    rows = tokens_ref.shape[0]
+    terms = sum_parts(parts_ref, slice(rows, rows + gain_rows))
+    gains_ref[0:1, :] = terms[0:1, :] + terms[1:2, :]
+    gains_ref[1:2, :] = terms[2:3, :] + terms[3:4, :]
 
     def rows_step(index, carry):
         here = pl.ds(pl.multiple_of(index * step, step), step)
@@ -185,6 +189,10 @@
         return carry
 
     lax.fori_loop(0, tokens_ref.shape[0] // step, rows_step, 0)
+
+
+def vmem_specs(count):
+    return [pl.BlockSpec(memory_space=pltpu.VMEM)] * count
 
 
 def local_kernel(kernel, name, operands, outs, scratch=()):
@@ -211,11 +219,6 @@
         high = ((min(stop, width) - 1) // block + 1) * block
         tiles.append((start, stop, low // 128 * 128, min(round_up(high), wide)))
     return tiles
-
-
-def split_bf16(value):
-    high = value.astype(bf16)
-    return high, (value - high.astype(f32)).astype(bf16)
 
 
 def one_minus_exp(value):
@@ -349,24 +352,40 @@
     lax.fori_loop(0, count, values_step, 0)
 
 
-def recur_backward_kernel(
+def mixer_backward_kernel(
     tiles,
-    grad_ref,
-    signal_ref,
+    state_grad_ref,
+    branch_grad_ref,
     masks_ref,
     vectors_ref,
+    mlp_ref,
+    signal_any,
+    states_any,
+    conv_any,
+    decay_rate_any,
+    input_rate_any,
+    decay_high_any,
+    decay_low_any,
+    input_high_any,
+    input_low_any,
+    both_any,
+    tokens_any,
+    both_grad_ref,
+    decay_pre_ref,
+    input_pre_ref,
+    sums_ref,
+    token_ref,
+    signal_ref,
+    states_ref,
+    conv_ref,
+    decay_rate_ref,
+    input_rate_ref,
     decay_high,
     decay_low,
     input_high,
     input_low,
-    states_ref,
-    conv_ref,
-    decay_rate_ref,
-    input_rate_ref,
-    signal_grad_ref,
-    decay_pre_ref,
-    input_pre_ref,
-    sums_ref,
+    both_ref,
+    tokens_ref,
     padded,
     grads,
     earlier,
@@ -374,23 +393,47 @@
     decay_pre_low,
     input_pre_high,
     input_pre_low,
+    gain_sums,
+    arrived,
 ):
-    length, width = signal_ref.shape
+    fetched = [
+        (signal_any, signal_ref),
+        (states_any, states_ref),
+        (conv_any, conv_ref),
+        (decay_rate_any, decay_rate_ref),
+        (input_rate_any, input_rate_ref),
+        (decay_high_any, decay_high),
+        (decay_low_any, decay_low),
+        (input_high_any, input_high),
+        (input_low_any, input_low),
+        (both_any, both_ref),
+    ]
+    copies = [
+        pltpu.make_async_copy(source, target, arrived.at[number])
+        for number, (source, target) in enumerate(fetched)
+    ]
+    for copy in copies:
+        copy.start()
+    length, width = grads.shape[0] - 8, grads.shape[1]
     count = length // chunk
     padded[0:8, :] = jnp.zeros((8, width), f32)
     earlier[0:8, :] = jnp.zeros((8, width), f32)
+    grads[length:, :] = jnp.zeros((8, width), f32)
+    sums_ref[...] = jnp.zeros_like(sums_ref)
+
+    for copy in copies[:5]:
+        copy.wait()
 
     def pad_step(index, carry):
         begin = pl.multiple_of(index * chunk, chunk)
         here = pl.ds(begin, chunk)
         padded[pl.ds(begin + 8, chunk), :] = signal_ref[here, :].astype(f32)
-        earlier[pl.ds(begin + 8, chunk), :] = states_ref[pl.ds(begin, chunk), :]
-        grads[pl.ds(begin, chunk), :] = grad_ref[here, :].astype(f32)
+        earlier[pl.ds(begin + 8, chunk), :] = states_ref[here, :]
+        grads[here, :] = state_grad_ref[here, :].astype(f32)
+        both_grad_ref[here, width:] = branch_grad_ref[here, :]
         return carry
 
     lax.fori_loop(0, count, pad_step, 0)
-    grads[length:, :] = jnp.zeros((8, width), f32)
-    sums_ref[...] = jnp.zeros_like(sums_ref)
 
     def scan_step(index, later):
         begin = pl.multiple_of(length - 8 - index * 8, 8)
@@ -429,6 +472,9 @@
 
     lax.fori_loop(0, length // 8, scan_step, jnp.zeros((1, width), f32), unroll=4)
 
+    for copy in copies[5:9]:
+        copy.wait()
+
     def split_step(index, carry):
         rows = pl.ds(pl.multiple_of(index * chunk, chunk), chunk)
         decay_pre_high[rows, :], decay_pre_low[rows, :] = split_bf16(decay_pre_ref[rows, :])
@@ -467,10 +513,34 @@
                 masked[:chunk, :] * signal_window[8 - tap : 8 - tap + chunk, :]
             )
         here = pl.ds(begin, chunk)
-        signal_grad_ref[here, :] = result.astype(bf16)
+        both_grad_ref[here, :width] = result.astype(bf16)
         return carry
 
     lax.fori_loop(0, count, conv_step, 0)
+    copies[9].wait()
+    parts, rows, model_width = token_ref.shape
+    rows = rows - gain_rows
+    gain_sums[...] = jnp.zeros_like(gain_sums)
+
+    def token_step(index, carry):
+        here = pl.ds(pl.multiple_of(index * rows, rows), rows)
+        copy = pltpu.make_async_copy(tokens_any.at[here, :], tokens_ref, arrived.at[len(fetched)])
+        copy.start()
+        grad = mm(both_grad_ref[here, :], both_ref[...], ((1,), (1,)))
+        copy.wait()
+        values = tokens_ref[...].astype(f32)
+        gain_sums[...] += fold8(values * rms_scale(values) * grad)
+        token_ref[index, :rows, :] = grad.astype(bf16)
+        return carry
+
+    lax.fori_loop(0, parts, token_step, 0)
+    terms = []
+    for total in (gain_sums[...], mlp_ref[...]):
+        terms += split_bf16(total.sum(axis=0, keepdims=True))
+    terms.append(jnp.zeros((gain_rows - len(terms), model_width), bf16))
+    terms = jnp.concatenate([term.astype(f32) for term in terms], axis=0).astype(bf16)
+    for part in range(parts):
+        token_ref[part, rows:, :] = terms
 
 
 def recur_forward(signal, masks, vectors, weights, tiles):
@@ -489,18 +559,74 @@
     )
 
 
-def recur_backward(state_grad, signal, masks, vectors, weights, saved, tiles):
-    length, width = signal.shape
-    whole = ((length, width), f32)
-    pair = pltpu.VMEM((length, width), bf16)
-    padded = pltpu.VMEM((length + 8, width), f32)
-    return local_kernel(
-        functools.partial(recur_backward_kernel, tiles),
-        "recur_backward",
-        (state_grad, signal, masks, vectors, *weights, *saved),
-        [((length, width), bf16), whole, whole, ((64, width), f32)],
-        [padded] * 3 + [pair] * 4,
-    )
+def mixer_backward(resident, fetched, parts, tiles):
+    length, wide = resident[0].shape
+    model_width = fetched[-1].shape[1]
+    whole = ((length, wide), f32)
+    outs = [
+        ((length, 2 * wide), bf16),
+        whole,
+        whole,
+        ((64, wide), f32),
+        ((parts, length // parts + gain_rows, model_width), bf16),
+    ]
+    padded = pltpu.VMEM((length + 8, wide), f32)
+    return pl.pallas_call(
+        functools.partial(mixer_backward_kernel, tiles),
+        out_shape=[jax.ShapeDtypeStruct(shape, kind) for shape, kind in outs],
+        in_specs=vmem_specs(len(resident)) + [pl.BlockSpec(memory_space=pl.ANY)] * len(fetched),
+        out_specs=vmem_specs(len(outs)),
+        scratch_shapes=[pltpu.VMEM(value.shape, value.dtype) for value in fetched[:-1]]
+        + [pltpu.VMEM((length // parts, model_width), bf16)]
+        + [padded] * 3
+        + [pltpu.VMEM((length, wide), bf16)] * 4
+        + [pltpu.VMEM((8, model_width), f32), pltpu.SemaphoreType.DMA((len(fetched),))],
+        compiler_params=pltpu.CompilerParams(vmem_limit_bytes=vmem_limit),
+        name="mixer_backward",
+    )(*resident, *fetched)
+
+
+def column_grads_kernel(count, *refs):
+    for number in range(count):
+        value = mm(refs[number][...], refs[count + number][...], ((0,), (0,)))
+        value = value.astype(bf16)
+        refs[-1][0, :, number] = value.reshape(refs[-1].shape[1], *refs[-1].shape[3:])
+
+
+def column_grads(lefts, rights, size, parts):
+    length, model_width = lefts[0].shape
+    wide = rights[0].shape[1]
+    each, count = model_width // size, len(lefts)
+    block = (1, parts, count, each // parts, wide)
+    total = pl.pallas_call(
+        functools.partial(column_grads_kernel, count),
+        grid=(size,),
+        in_specs=[pl.BlockSpec((length, each), lambda i: (0, i))] * count
+        + [pl.BlockSpec((length, wide), lambda i: (0, 0))] * count,
+        out_specs=pl.BlockSpec(block, lambda i: (i, 0, 0, 0, 0)),
+        out_shape=jax.ShapeDtypeStruct((size,) + block[1:], bf16),
+        compiler_params=pltpu.CompilerParams(vmem_limit_bytes=vmem_limit),
+        name="column_grads",
+    )(*lefts, *rights)
+    total = total.reshape(size * count * each, wide)
+    total = lax.psum_scatter(total, "rows", scatter_dimension=0, tiled=True)
+    return total.reshape(parts, count, each // parts, wide)
+
+
+def gate_grads_kernel(tiles, conv_ref, decay_pre_ref, input_pre_ref, gates_ref, dense, pairs):
+    heads, block = gates_ref.shape[1:3]
+    pairs[0], pairs[1] = split_bf16(conv_ref[...])
+    for gate, ref in enumerate((decay_pre_ref, input_pre_ref)):
+        pairs[2], pairs[3] = split_bf16(ref[...])
+        for start, stop, low, high in tiles:
+            total = None
+            for left, right in ((0, 2), (0, 3), (1, 2)):
+                part = mm(pairs[left, :, low:high], pairs[right, :, start:stop], ((0,), (0,)))
+                total = part if total is None else total + part
+            dense[low:high, start:stop] = total
+        for head in range(heads):
+            cut = slice(head * block, (head + 1) * block)
+            gates_ref[gate, head] = dense[cut, cut]
 
 
 def dense_kernel(decay_ref, input_ref, decay_high, decay_low, input_high, input_low):
@@ -516,46 +642,105 @@
             high[cut, cut], low[cut, cut] = split_bf16(ref[head])
 
 
-def diagonal_blocks(left, right, heads, block):
-    dense = lax.dot_general(
-        left,
-        right,
-        (((0,), (0,)), ((), ())),
-        precision=lax.Precision.HIGH,
-        preferred_element_type=f32,
-    )
-    cuts = [slice(head * block, (head + 1) * block) for head in range(heads)]
-    return jnp.stack([dense[cut, cut] for cut in cuts])
-
-
-def unit_grads_kernel(*refs):
-    count = (len(refs) - 1) // 2
-    out_ref = refs[-1]
-    for number in range(count):
-        left_ref, right_ref = refs[number], refs[count + number]
-        value = mm(left_ref[...], right_ref[...], ((0,), (0,))).astype(bf16)
-        out_ref[:, number] = value.reshape(out_ref.shape[0], *out_ref.shape[2:])
-
-
-def unit_grads(lefts, rights, parts):
-    length, total = lefts[0].shape
-    units = total // parts
-    model_width = rights[0].shape[1]
+def mlp_kernel(
+    normed_ref,
+    cotangent_ref,
+    hidden_grad_ref,
+    gate_ref,
+    up_ref,
+    down_ref,
+    normed_grad_ref,
+    out_ref,
+    units_any,
+    normed_total,
+    out_total,
+    gate_grads,
+    up_grads,
+    hidden_all,
+    units,
+    sent,
+):
+    step, steps = pl.program_id(0), pl.num_programs(0)
+    length = normed_ref.shape[0]
+    group = units.shape[1]
+    gate_units = lambda: gate_ref[...].reshape(down_ref.shape)
+    up_units = lambda: up_ref[...].reshape(down_ref.shape)
+
+    @pl.when(step == 0)
+    def _():
+        normed_total[...] = jnp.zeros_like(normed_total)
+        out_total[...] = jnp.zeros_like(out_total)
+
+    def rows_step(index, carry):
+        here = pl.ds(pl.multiple_of(index * 256, 256), 256)
+        normed = normed_ref[here, :]
+        gate_act, slope = gelu_parts(mm(normed, gate_units(), ((1,), (1,))))
+        up_vals = mm(normed, up_units(), ((1,), (1,)))
+        hidden_grad = hidden_grad_ref[here, :]
+        gate_grads[here, :] = (hidden_grad * up_vals * slope).astype(bf16)
+        up_grads[here, :] = (hidden_grad * gate_act).astype(bf16)
+        hidden_all[here, :] = (gate_act * up_vals).astype(bf16)
+        normed_total[here, :] += mm(gate_grads[here, :], gate_units(), ((1,), (0,))) + mm(
+            up_grads[here, :], up_units(), ((1,), (0,))
+        )
+        out_total[here, :] += mm(hidden_all[here, :], down_ref[...], ((1,), (0,)))
+        return carry
+
+    lax.fori_loop(0, length // 256, rows_step, 0)
+
+    def copy_of(number):
+        return pltpu.make_async_copy(
+            units.at[number], units_any.at[pl.ds(step * group, group), number], sent.at[number]
+        )
+
+    products = ((gate_grads, normed_ref), (up_grads, normed_ref), (hidden_all, cotangent_ref))
+    for number, (left, right) in enumerate(products):
+
+        @pl.when(step > 0)
+        def _():
+            copy_of(number).wait()
+
+        value = mm(left[...], right[...], ((0,), (0,))).astype(bf16)
+        units[number] = value.reshape(units.shape[1:])
+        copy_of(number).start()
+
+    @pl.when(step == steps - 1)
+    def _():
+        normed_grad_ref[...] = normed_total[...].astype(bf16)
+        out_ref[...] = out_total[...].astype(bf16)
+        for number in range(len(products)):
+            copy_of(number).wait()
+
+
+def mlp(normed, cotangent, hidden_grad, first_units, down_units):
+    length, model_width = normed.shape
+    parts, _, units, _ = first_units.shape
+    total = parts * units
     group = 1
-    while group * units % 128:
+    while group * units % 128 or (group < parts and 2 * group * units * length <= 768 * 512):
         group *= 2
-    count = len(lefts)
+    tile = group * units
+    first = lambda which: pl.BlockSpec(
+        (group, 1, units, model_width), lambda i: (i, which, 0, 0)
+    )
+    weights = [first(0), first(1), pl.BlockSpec((tile, model_width), lambda i: (i, 0))]
+    whole = jax.ShapeDtypeStruct((length, model_width), bf16)
     return pl.pallas_call(
-        unit_grads_kernel,
-        grid=(parts // group,),
-        out_shape=jax.ShapeDtypeStruct((parts, count, units, model_width), bf16),
-        in_specs=[pl.BlockSpec((length, group * units), lambda i: (0, i))] * count
-        + [pl.BlockSpec((length, model_width), lambda i: (0, 0))] * count,
-        out_specs=pl.BlockSpec((group, count, units, model_width), lambda i: (i, 0, 0, 0)),
+        mlp_kernel,
+        grid=(total // tile,),
+        out_shape=[
+            whole,
+            whole,
+            jax.ShapeDtypeStruct((parts, 3, units, model_width), bf16),
+        ],
+        in_specs=vmem_specs(2) + [pl.BlockSpec((length, tile), lambda i: (0, i))] + weights,
+        out_specs=vmem_specs(2) + [pl.BlockSpec(memory_space=pl.ANY)],
+        scratch_shapes=[pltpu.VMEM((length, model_width), f32)] * 2
+        + [pltpu.VMEM((length, tile), bf16)] * 3
+        + [pltpu.VMEM((3, group, units, model_width), bf16), pltpu.SemaphoreType.DMA((3,))],
         compiler_params=pltpu.CompilerParams(vmem_limit_bytes=vmem_limit),
-        cost_estimate=pl.CostEstimate(flops=1024, bytes_accessed=1024, transcendentals=0),
-        name="unit_grads",
-    )(*lefts, *rights)
+        name="mlp",
+    )(normed, cotangent, hidden_grad, first_units, first_units, down_units)
 
 
 def body(
@@ -602,16 +787,15 @@
     columns, token_own = tie(columns, own_tokens)
     both_columns = lax.all_gather(columns[:, : 2 * wide], "rows", axis=0, tiled=True)
     output_columns = lax.all_gather(columns[:, 2 * wide :], "rows", axis=0, tiled=True)
-    tokens_all = gather_blk(token_own, n_blk).reshape(n_blk * tok_count, model_width)
-    tokens_all, hidden_gate, hidden_up, hidden_down = tie(
-        tokens_all, hidden_gate, hidden_up, hidden_down
-    )
-    gate_units = lax.all_gather(hidden_gate, "rows", axis=0, tiled=True)
-    up_units = lax.all_gather(hidden_up, "rows", axis=0, tiled=True)
+    tokens_all = ring_blk(token_own, n_blk)
+    tokens_all, grad_own, hidden_gate, hidden_up, hidden_down = tie(
+        tokens_all, for_all(own_grad, n_blk), hidden_gate, hidden_up, hidden_down
+    )
+    out_grad = swap_blk(grad_own).reshape(n_blk * tok_count, model_width)
     down_units = lax.all_gather(hidden_down, "rows", axis=0, tiled=True)
-
-    gains = both_columns[:, width : width + 2].astype(f32).T
-    mixer_gains, mlp_gains = gains[0:1], gains[1:2]
+    first_units = lax.all_gather(
+        jnp.concatenate([hidden_gate, hidden_up], axis=0), "rows", axis=0, tiled=True
+    ).reshape(n_rows, 2, units, model_width)
 
     masks = [jnp.ones_like(segments, dtype=f32)]
     for tap in range(1, 4):
@@ -636,21 +820,22 @@
     weights = local_kernel(
         dense_kernel, "dense_gates", (decay_gate, input_gate), [((wide, wide), bf16)] * 4
     )
-    (mixer_normed,) = local_kernel(
-        mixer_norm_kernel,
-        "mixer_norm",
-        (mixer_gains, tokens_all),
-        [((n_blk * tok_count, model_width), bf16)],
-    )
-    mixer_normed, grad_own = tie(mixer_normed, own_grad)
-    out_grad = gather_blk(grad_own, n_blk).reshape(n_blk * tok_count, model_width)
-    both_pre = mm(mixer_normed, both_columns, ((1,), (0,)))
+    mixer_normed, both_pre, gains = local_kernel(
+        functools.partial(mixer_in_kernel, width),
+        "mixer_in",
+        (tokens_all, both_columns),
+        [
+            (tokens_all.shape, bf16),
+            ((n_blk * tok_count, 2 * wide), f32),
+            ((2, model_width), f32),
+        ],
+    )
+    mixer_gains, mlp_gains = gains[0:1], gains[1:2]
     signal, branch_pre = both_pre[:, :wide].astype(bf16), both_pre[:, wide:]
     states, state_values, conv_out, decay_rate, input_rate = recur_forward(
         signal, masks, vectors, weights, tiles
     )
-    branch_act, branch_pullback = jax.vjp(gelu_tanh, branch_pre)
-    mixed = (branch_act * state_values.astype(f32)).astype(bf16)
+    mixed = (gelu_tanh(branch_pre) * state_values.astype(f32)).astype(bf16)
     mixed, out_grad = tie(mixed, out_grad)
 
     def scatter_blk(partial):
@@ -664,27 +849,12 @@
         [(square, f32), (square, bf16)],
     )
 
-    mlp_normed = gather_blk(own_normed, n_blk).reshape(n_blk * tok_count, model_width)
-    gate_vals = mm(mlp_normed, gate_units, ((1,), (1,)))
-    up_vals = mm(mlp_normed, up_units, ((1,), (1,)))
-    gate_act, gate_pullback = jax.vjp(gelu_tanh, gate_vals)
-    hidden_vals = (gate_act * up_vals).astype(bf16)
+    mlp_normed = ring_blk(own_normed, n_blk)
     hidden_grad = mm(out_grad, down_units, ((1,), (1,)))
-    gate_grad = gate_pullback(hidden_grad * up_vals)[0].astype(bf16)
-    up_grad = (hidden_grad * gate_act).astype(bf16)
-
-    normed_partial = (
-        mm(gate_grad, gate_units, ((1,), (0,))) + mm(up_grad, up_units, ((1,), (0,)))
-    ).astype(bf16)
-    normed_partial, gate_grad, up_grad, hidden_vals = tie(
-        normed_partial, gate_grad, up_grad, hidden_vals
+    normed_partial, out_partial, unit_sums = mlp(
+        mlp_normed, out_grad, hidden_grad, first_units, down_units
     )
     normed_parts = scatter_blk(normed_partial)
-    unit_sums = unit_grads(
-        (gate_grad, up_grad, hidden_vals), (mlp_normed, mlp_normed, out_grad), n_rows
-    )
-    out_partial = mm(hidden_vals, down_units, ((1,), (0,))).astype(bf16)
-    normed_parts, _, out_partial = tie(normed_parts, unit_sums, out_partial)
     unit_sums = lax.psum_scatter(
         unit_sums.reshape(n_rows * 3 * units, model_width),
         "rows",
@@ -698,93 +868,71 @@
         (mlp_gains, residual_mid, own_grad, normed_parts),
         [(square, f32), (square, bf16), ((8, model_width), f32)],
     )
-    mid_sent = gather_blk(own_sent, n_blk).reshape(n_blk * tok_count, model_width)
+    mid_sent = ring_blk(own_sent, n_blk)
 
     mid_sent, out_partial = tie(mid_sent, out_partial)
     out_parts = scatter_blk(out_partial)
     mixed_grad = mm(mid_sent, output_columns, ((1,), (0,)))
+    branch_act, branch_slope = gelu_parts(branch_pre)
     state_grad = (mixed_grad * branch_act).astype(bf16)
-    branch_grad = branch_pullback(mixed_grad * state_values.astype(f32))[0].astype(bf16)
-
-    def column_grads(left, right):
-        partial = mm(left, right, ((0,), (0,))).astype(bf16)
-        return partial.reshape(n_rows, 1, n_blk * shard, -1)
-
-    early_sum = jnp.concatenate(
-        [column_grads(mid_sent, mixed), column_grads(mixer_normed, branch_grad)], axis=1
-    )
-    signal_grad, decay_pre_grad, input_pre_grad, sums = recur_backward(
-        state_grad,
-        signal,
-        masks,
-        vectors,
-        weights,
-        (states, conv_out, decay_rate, input_rate),
+    branch_grad = (mixed_grad * state_values.astype(f32) * branch_slope).astype(bf16)
+    early_sum = column_grads((mid_sent, mixer_normed), (mixed, branch_grad), n_rows, n_blk)
+    both_grad, decay_pre_grad, input_pre_grad, sums, token_sent = mixer_backward(
+        (state_grad, branch_grad, masks, vectors, mlp_gain_part),
+        (
+            signal,
+            states,
+            conv_out,
+            decay_rate,
+            input_rate,
+            *weights,
+            both_columns,
+            tokens_all,
+        ),
+        n_blk,
         tiles,
     )
-    signal_grad, out_parts = tie(signal_grad, out_parts)
-    both_grad = jnp.concatenate([signal_grad, branch_grad], axis=1)
-    partial = mm(both_grad, both_columns, ((1,), (1,)))
-    token_sent, mixer_gain_part = local_kernel(
-        pack_grad_kernel,
-        "pack_grad",
-        (partial, tokens_all),
-        [((n_blk * tok_count, model_width), bf16), ((8, model_width), f32)],
-    )
-    token_parts = scatter_blk(token_sent)
-    early_sum, unit_sums = tie(early_sum, unit_sums)
-    early_sum = lax.psum_scatter(
-        early_sum.reshape(n_rows * 2 * n_blk * shard, wide),
-        "rows",
-        scatter_dimension=0,
-        tiled=True,
-    ).reshape(2, n_blk * shard, wide)
-    late_sum, late_left = by_bits(column_grads(mixer_normed, signal_grad)[:, 0], n_rows)
-    gate_sums = jnp.stack(
-        [
-            diagonal_blocks(conv_out, decay_pre_grad, heads, block),
-            diagonal_blocks(conv_out, input_pre_grad, heads, block),
-        ]
-    )
+    token_sent, out_parts, unit_sums, both_grad, decay_pre_grad, input_pre_grad, sums = tie(
+        token_sent, out_parts, unit_sums, both_grad, decay_pre_grad, input_pre_grad, sums
+    )
+    token_parts = swap_blk(token_sent)
+    late_sum = column_grads((mixer_normed,), (both_grad[:, :wide],), n_rows, n_blk)
+    (gate_sums,) = local_kernel(
+        functools.partial(gate_grads_kernel, tiles),
+        "gate_grads",
+        (conv_out, decay_pre_grad, input_pre_grad),
+        [((2, heads, block, block), f32)],
+        [pltpu.VMEM((wide, wide), f32), pltpu.VMEM((4,) + signal.shape, bf16)],
+    )
+    gate_sums, token_parts = tie(gate_sums, token_parts)
+    gate_sums = [gate_sums[0], gate_sums[1]]
+    one_way = bits_of(n_rows)
+    other_way = one_way[:1] + one_way[:0:-1]
     vector_sums = sums.reshape(8, 8, wide).sum(axis=1)
-    gain_sums = jnp.stack([mixer_gain_part.sum(axis=0), mlp_gain_part.sum(axis=0)])
-
-    def add_from(value, bit, axis="rows", size=n_rows, wire=f32):
-        return value + lax.ppermute(value.astype(wire), axis, flip(size, bit)).astype(f32)
-
-    for bit in bits_of(n_rows):
-        late_sum, _ = halve(late_sum, n_rows, bit, late_left)
-        gate_sums = add_from(gate_sums, bit, wire=bf16)
-        vector_sums = add_from(vector_sums, bit)
-        gain_sums = add_from(gain_sums, bit)
-        late_sum, gate_sums, vector_sums, gain_sums = tie(
-            late_sum, gate_sums, vector_sums, gain_sums
-        )
-    for bit in bits_of(n_blk):
-        gain_sums = add_from(gain_sums, bit, "blk", n_blk)
+    for at, bit in enumerate(bits_of(n_rows)):
+        for number, order in enumerate((one_way, other_way)):
+            gate_sums[number] = add_from(gate_sums[number], n_rows, order[at], bf16)
+        vector_sums = add_from(vector_sums, n_rows, bit)
+        vector_sums, *gate_sums = tie(vector_sums, *gate_sums)
+    token_parts, early_sum = tie(token_parts, early_sum)
     vector_sums = vector_sums[:, :width]
-
-    def join_columns(total):
-        count = total.shape[0]
-        parts = total.reshape(count, n_blk, shard, wide).transpose(1, 2, 0, 3)
-        return local_kernel(
-            functools.partial(join_columns_kernel, width, wide),
-            "join_columns",
-            (swap_blk(parts.reshape(n_blk, shard, count * wide)),),
-            [((shard, n_blk * width), f32)] * count,
-        )
-
-    output_weight_grad, branch_weight_grad, input_weight_grad = join_columns(
-        jnp.concatenate([early_sum, late_sum.astype(bf16)], axis=0)
-    )
-    block_out = (residual_mid + out_parts.astype(f32).sum(axis=0)).astype(bf16)
-
-    (token_grad,) = local_kernel(
+    token_grad, gain_sums = local_kernel(
         token_grad_kernel,
         "token_grad",
         (mixer_gains, own_tokens, mid_grad, token_parts),
-        [(square, f32)],
-    )
+        [(square, f32), ((2, model_width), f32)],
+    )
+    gain_sums = sum_rows(gain_sums, n_rows)
+
+    column_sums = swap_blk(jnp.concatenate([early_sum, late_sum], axis=1))
+    output_weight_grad, branch_weight_grad, input_weight_grad = local_kernel(
+        functools.partial(join_columns_kernel, width),
+        "join_columns",
+        (column_sums,),
+        [((shard, n_blk * width), f32)] * 3,
+    )
+    block_out = (residual_mid + out_parts.astype(f32).sum(axis=0)).astype(bf16)
+
     gain_sums = lax.dynamic_slice_in_dim(
         gain_sums, (row * n_blk + blk) * mixer_gain.shape[0], mixer_gain.shape[0], axis=1
     )

time: 649 us -> 588 us (0.906)
  blocking collectives: 186 us -> 88.2 us
  Pallas kernels: 62.9 us -> 136 us
  matrix products: 82.8 us -> 17.5 us
  waiting for transfers between devices: 178 us -> 242 us
  other arithmetic: 32.7 us -> 16.9 us
  starting transfers between devices: 43.7 us -> 33.8 us
  local copies, waits for them, and re-layouts: 39.7 us -> 30.3 us
    all_to_all x4 -> x2, blocking collectives: 186 us -> 88.2 us  [swap_blk(): return lax.all_to_all(parts, 'blk', split_axis=0, concat_axis=0, tiled=True)]
    pallas_call x1 -> x4, Pallas kernels: 16 us -> 83.5 us  [the longest x1 37.9 us: mlp(): pl.pallas_call(mlp_kernel, grid=(total // tile,), out_shape=[whole, whole...]
    ppermute x14 -> x21, waiting for transfers between devices: 62.3 us -> 127 us  [the longest x9 112 us: ring_blk(): lax.ppermute(part, 'blk', [(place, (place + 1) % size) for place in range...]
    dot_general x13 -> x3, matrix products: 75.9 us -> 17.5 us  [mm(): lax.dot_general(left, right, (dims, ((), ())), preferred_element_type=f32)]
    unnamed x114 -> x68, local copies, waits for them, and re-layouts: 21.5 us -> 10.2 us
    add x14 -> x11, other arithmetic: 11.6 us -> 0.55 us  [add_from(): value + lax.ppermute(value.astype(wire), 'rows', flip(size, bit)).astype(...]
    dot_general x2 -> x0, matrix products: 6.83 us -> none  [diagonal_blocks(): lax.dot_general(left, right, (((0,), (0,)), ((), ())), precision=lax.Prec...]
    ppermute x14 -> x21, starting transfers between devices: 17.1 us -> 10.9 us  [the longest x12 10 us: add_from(): lax.ppermute(value.astype(wire), 'rows', flip(size, bit)).astype(f32)]
  transfers between devices with their start and end apart: 27 -> 33, of which waited for: 10 -> 19; matrix products, arithmetic and copies ran while one was open for 17% -> 10% of each run, Pallas kernels for 7% -> 16%
where the time goes in v2:
time: 588 us; the launch traced here: 579 us
  waiting for transfers between devices  242 us (41%)
  Pallas kernels  136 us (23%)
  blocking collectives  88.2 us (15%)
  starting transfers between devices  33.8 us (6%)
  local copies, waits for them, and re-layouts  30.3 us (5%)
  matrix products  17.5 us (3%)
  other arithmetic  16.9 us (3%)
  between operations  15.2 us (3%)
    ppermute x9, waiting for transfers between devices, ring_blk(): lax.ppermute(part, 'blk', [(place, (place + 1) % size) for place in range...  112 us
    all_to_all x5, waiting for transfers between devices, swap_blk(): return lax.all_to_all(parts, 'blk', split_axis=0, concat_axis=0, tiled=True)  107 us
    all_to_all x2, blocking collectives, swap_blk(): return lax.all_to_all(parts, 'blk', split_axis=0, concat_axis=0, tiled=True)  88.2 us
    pallas_call x9, Pallas kernels, local_kernel(): pl.pallas_call(kernel, out_shape=[jax.ShapeDtypeStruct(shape, kind) for s...  52.2 us
    pallas_call x1, Pallas kernels, mlp(): pl.pallas_call(mlp_kernel, grid=(total // tile,), out_shape=[whole, whole...  37.9 us
    pallas_call x1, Pallas kernels, mixer_backward(): pl.pallas_call(functools.partial(mixer_backward_kernel, tiles), out_shape...  28.2 us
    all_to_all x5, starting transfers between devices, swap_blk(): return lax.all_to_all(parts, 'blk', split_axis=0, concat_axis=0, tiled=True)  22.4 us
    dot_general x3, matrix products, mm(): lax.dot_general(left, right, (dims, ((), ())), preferred_element_type=f32)  17.5 us
  transfers between devices with their start and end apart: 33, of which 19 were waited for; matrix products, arithmetic and copies ran while one was open for 10% of the time, Pallas kernels for 16%

profile of v2, /device:TPU:0, one launch (start us, length us, event | category | flops | bytes accessed | tf_op | source)
XLA Modules:
  0.0 579.2 jit_solution(792301353051757098)
XLA Ops:
  12.6 34.9 %all_to_all.35 = bf16[4,64,2304]{2,1,0:T(8,128)(2,1)S(1)} all-to-all(bf16[4,64,2304]{2,1,0:T(8,128)(2,1)} %split_columns.1), channel_id=1, replica_groups=mesh['rows'=8,'blk'=4] {'blk'}, dimensions={0} | all-to-all | bytes 2359296 | tf_op jit(solution)/shard_map/all_to_all | solution.py:62
  49.5 14.1 %collective-permute-done = bf16[128,2048]{1,0:T(8,128)(2,1)S(1)} collective-permute-done((bf16[128,2048]{1,0:T(8,128)(2,1)S(1)}, bf16[128,2048]{1,0:T(8,128)(2,1)S(1)}, u32[]{:S(2)}, u32[]{:S(2)}) %collective-permute-start) | collective-permute-done | bytes 524320 | tf_op jit(solution)/shard_map/ppermute | solution.py:70
  63.7 13.5 %collective-permute-done.1 = bf16[128,2048]{1,0:T(8,128)(2,1)} collective-permute-done((bf16[128,2048]{1,0:T(8,128)(2,1)S(1)}, bf16[128,2048]{1,0:T(8,128)(2,1)}, u32[]{:S(2)}, u32[]{:S(2)}) %collective-permute-start.1) | collective-permute-done | bytes 524320 | tf_op jit(solution)/shard_map/ppermute | solution.py:70
  79.4 10.5 %collective-permute-done.2 = bf16[128,2048]{1,0:T(8,128)(2,1)S(1)} collective-permute-done((bf16[128,2048]{1,0:T(8,128)(2,1)}, bf16[128,2048]{1,0:T(8,128)(2,1)S(1)}, u32[]{:S(2)}, u32[]{:S(2)}) %collective-permute-start.2) | collective-permute-done | bytes 524320 | tf_op jit(solution)/shard_map/ppermute | solution.py:70
  102.0 4.3 dense_gates.1
  107.1 9.3 %mixer_in.1 = (bf16[512,2048]{1,0:T(8,128)(2,1)}, f32[512,1536]{1,0:T(8,128)}, f32[2,2048]{1,0:T(2,128)}) custom-call(bf16[512,2048]{1,0:T(8,128)(2,1)} %copy-done, bf16[2048,1536]{1,0:T(8,128)(2,1)} %all-gather.5.cloned.1.call-done.columns_ref.both_any), custom_call_target="tpu_custom_call" | custom-call | tf_op jit(solution)/shard_map/mixer_in/pallas_call | solution.py:199
  118.8 14.7 %recur_forward.1 = (f32[512,768]{1,0:T(8,128)}, bf16[512,768]{1,0:T(8,128)(2,1)}, f32[512,768]{1,0:T(8,128)}, f32[512,768]{1,0:T(8,128)}, f32[512,768]{1,0:T(8,128)}) custom-call(bf16[512,768]{1,0:T(8,128)(2,1)} %slice.137.signal_ref.signal_any, f32[520,8]{1,0:T(8,128)} %pad.12.masks_ref, f32[8,768]{1,0:T(8,128)} %pad.13.vectors_ref, ...), custom_call_target="tpu_custom_call" | custom-call | tf_op jit(solution)/shard_map/recur_forward/pallas_call | solution.py:199
  135.7 7.1 %all-to-all-done.1 = bf16[4,128,2048]{2,1,0:T(8,128)(2,1)S(1)} async-done(((bf16[4,128,2048]{2,1,0:T(8,128)(2,1)}), bf16[4,128,2048]{2,1,0:T(8,128)(2,1)S(1)}, u32[]{:S(2)}, u32[]{:S(2)}) %all-to-all-start.1) | async-done | bytes 2097184 | tf_op jit(solution)/shard_map/all_to_all | solution.py:62
  142.8 5.8 convolution_convert_fusion
  148.6 4.6 all-to-all-start.2
  153.9 47.1 %all-to-all-done.2.parts_ref = bf16[4,128,2048]{2,1,0:T(8,128)(2,1)} async-done(((bf16[4,128,2048]{2,1,0:T(8,128)(2,1)}), bf16[4,128,2048]{2,1,0:T(8,128)(2,1)}, u32[]{:S(2)}, u32[]{:S(2)}) %all-to-all-start.2) | async-done | bytes 2097184 | tf_op jit(solution)/shard_map/all_to_all | solution.py:62
  204.6 14.9 %collective-permute-done.3 = bf16[128,2048]{1,0:T(8,128)(2,1)S(1)} collective-permute-done((bf16[128,2048]{1,0:T(8,128)(2,1)}, bf16[128,2048]{1,0:T(8,128)(2,1)S(1)}, u32[]{:S(2)}, u32[]{:S(2)}) %collective-permute-start.3) | collective-permute-done | bytes 524320 | tf_op jit(solution)/shard_map/ppermute | solution.py:70
  219.7 8.0 %fusion.21.hidden_grad_ref = f32[512,1536]{1,0:T(8,128)} fusion(bf16[512,2048]{1,0:T(8,128)(2,1)S(1)} %bitcast.47, bf16[1536,2048]{1,0:T(8,128)(2,1)} %all-gather.9.cloned.1.call-done.down_ref), kind=kOutput, calls=%fused_computation.75 | convolution fusion | flops 3221225472 | bytes 11534336 | tf_op jit(solution)/shard_map/dot_general | solution.py:37
  227.6 5.7 collective-permute-done.4
  233.8 12.4 %collective-permute-done.5 = bf16[128,2048]{1,0:T(8,128)(2,1)S(1)} collective-permute-done((bf16[128,2048]{1,0:T(8,128)(2,1)S(1)}, bf16[128,2048]{1,0:T(8,128)(2,1)S(1)}, u32[]{:S(2)}, u32[]{:S(2)}) %collective-permute-start.5) | collective-permute-done | bytes 524320 | tf_op jit(solution)/shard_map/ppermute | solution.py:70
  249.4 37.9 %mlp.1 = (bf16[512,2048]{1,0:T(8,128)(2,1)}, bf16[512,2048]{1,0:T(8,128)(2,1)}, bf16[8,3,192,2048]{3,2,1,0:T(8,128)(2,1)}) custom-call(bf16[512,2048]{1,0:T(8,128)(2,1)} %copy-done.4, bf16[512,2048]{1,0:T(8,128)(2,1)} %bitcast.48, f32[512,1536]{1,0:T(8,128)} %fusion.21.hidden_grad_ref, bf16[8,2,192,2048]{3,2,1,0:T(8,128)(2,1)} %bitcast.42, ...), custom_call_target="tpu_custom_call" | custom-call | tf_op jit(solution)/shard_map/mlp/pallas_call | solution.py:728
  288.9 53.3 %all_to_all.36.parts_ref = bf16[4,128,2048]{2,1,0:T(8,128)(2,1)} all-to-all(bf16[4,128,2048]{2,1,0:T(8,128)(2,1)S(1)} %bitcast.58), channel_id=1, replica_groups=mesh['rows'=8,'blk'=4] {'blk'}, dimensions={0} | all-to-all | bytes 4194304 | tf_op jit(solution)/shard_map/all_to_all | solution.py:62
  342.2 4.3 mid_grad.1
  346.9 14.6 %collective-permute-done.6 = bf16[128,2048]{1,0:T(8,128)(2,1)S(1)} collective-permute-done((bf16[128,2048]{1,0:T(8,128)(2,1)}, bf16[128,2048]{1,0:T(8,128)(2,1)S(1)}, u32[]{:S(2)}, u32[]{:S(2)}) %collective-permute-start.6) | collective-permute-done | bytes 524320 | tf_op jit(solution)/shard_map/ppermute | solution.py:70
  361.6 13.9 %collective-permute-done.7 = bf16[128,2048]{1,0:T(8,128)(2,1)S(1)} collective-permute-done((bf16[128,2048]{1,0:T(8,128)(2,1)S(1)}, bf16[128,2048]{1,0:T(8,128)(2,1)S(1)}, u32[]{:S(2)}, u32[]{:S(2)}) %collective-permute-start.7) | collective-permute-done | bytes 524320 | tf_op jit(solution)/shard_map/ppermute | solution.py:70
  375.9 12.5 %collective-permute-done.8 = bf16[128,2048]{1,0:T(8,128)(2,1)S(1)} collective-permute-done((bf16[128,2048]{1,0:T(8,128)(2,1)S(1)}, bf16[128,2048]{1,0:T(8,128)(2,1)S(1)}, u32[]{:S(2)}, u32[]{:S(2)}) %collective-permute-start.8) | collective-permute-done | bytes 524320 | tf_op jit(solution)/shard_map/ppermute | solution.py:70
  392.2 9.8 %column_grads.2 = bf16[8,4,2,64,768]{4,3,2,1,0:T(8,128)(2,1)} custom-call(bf16[512,2048]{1,0:T(8,128)(2,1)} %copy-done.7, bf16[512,2048]{1,0:T(8,128)(2,1)} %get-tuple-element.118.refs_1_.refs_0_, bf16[512,768]{1,0:T(8,128)(2,1)} %copy-done.10, bf16[512,768]{1,0:T(8,128)(2,1)} %get-tuple-element.194.branch_grad_ref.refs_3_), custom_call_target="tpu_custom_call" | custom-call | tf_op jit(solution)/shard_map/column_grads/pallas_call | solution.py:601
  405.7 28.2 %mixer_backward.1 = (bf16[512,1536]{1,0:T(8,128)(2,1)}, f32[512,768]{1,0:T(8,128)}, f32[512,768]{1,0:T(8,128)}, f32[64,768]{1,0:T(8,128)}, bf16[4,144,2048]{2,1,0:T(8,128)(2,1)}) custom-call(bf16[512,768]{1,0:T(8,128)(2,1)} %get-tuple-element.195.state_grad_ref, bf16[512,768]{1,0:T(8,128)(2,1)} %get-tuple-element.194.branch_grad_ref.refs_3_, ...), custom_call_target="tpu_custom_call" | custom-call | tf_op jit(solution)/shard_map/mixer_backward/pallas_call | solution.py:574
  433.9 16.8 %all-to-all-done.4 = bf16[4,128,2048]{2,1,0:T(8,128)(2,1)S(1)} async-done(((bf16[4,128,2048]{2,1,0:T(8,128)(2,1)}), bf16[4,128,2048]{2,1,0:T(8,128)(2,1)S(1)}, u32[]{:S(2)}, u32[]{:S(2)}) %all-to-all-start.4) | async-done | bytes 2097184 | tf_op jit(solution)/shard_map/all_to_all | solution.py:62
  458.0 7.6 %column_grads.3 = bf16[8,4,1,64,768]{4,3,2,1,0:T(8,128)(2,1)} custom-call(bf16[512,2048]{1,0:T(8,128)(2,1)} %get-tuple-element.118.refs_1_.refs_0_, bf16[512,768]{1,0:T(8,128)(2,1)} %slice.101.refs_1_), custom_call_target="tpu_custom_call" | custom-call | tf_op jit(solution)/shard_map/column_grads/pallas_call | solution.py:601
  466.6 6.3 %gate_grads.1 = f32[2,4,171,171]{3,2,1,0:T(8,128)} custom-call(f32[512,768]{1,0:T(8,128)} %get-tuple-element.102.conv_any.conv_ref, f32[512,768]{1,0:T(8,128)} %get-tuple-element.114.decay_pre_ref, f32[512,768]{1,0:T(8,128)} %get-tuple-element.115.input_pre_ref), custom_call_target="tpu_custom_call" | custom-call | tf_op jit(solution)/shard_map/gate_grads/pallas_call | solution.py:199
  472.9 35.9 %all-to-all-done.5.parts_ref = bf16[4,144,2048]{2,1,0:T(8,128)(2,1)S(1)} async-done(((bf16[4,144,2048]{2,1,0:T(8,128)(2,1)}), bf16[4,144,2048]{2,1,0:T(8,128)(2,1)S(1)}, u32[]{:S(2)}, u32[]{:S(2)}) %all-to-all-start.5) | async-done | bytes 2359328 | tf_op jit(solution)/shard_map/all_to_all | solution.py:62
  512.5 4.0 slice_convert_fusion.1
  516.5 4.1 token_grad.1
  525.4 4.0 reduce-scatter.8.cloned.1.call-done
  531.6 6.8 %all-to-all-start.6 = ((bf16[4,3,64,768]{3,2,1,0:T(8,128)(2,1)}), bf16[4,3,64,768]{3,2,1,0:T(8,128)(2,1)S(1)}, u32[]{:S(2)}, u32[]{:S(2)}) async-start(bf16[4,3,64,768]{3,2,1,0:T(8,128)(2,1)} %pad_maximum_fusion.1), calls=%async_computation.9 | async-start | bytes 2359296 | tf_op jit(solution)/shard_map/all_to_all | solution.py:62
  543.4 7.7 %collective-permute-done.16 = bf16[4,171,171]{2,1,0:T(8,128)(2,1)S(1)} collective-permute-done((bf16[4,171,171]{2,1,0:T(8,128)(2,1)S(1)}, bf16[4,171,171]{2,1,0:T(8,128)(2,1)S(1)}, u32[]{:S(2)}, u32[]{:S(2)}) %collective-permute-start.16) | collective-permute-done | bytes 233960 | tf_op jit(solution)/shard_map/ppermute | solution.py:81
  (196 shorter events, 89.4 us)
Async XLA Ops:
  7.2 99.9 %all-gather.5.cloned.1.call-start = ((), (), s32[]{:S(2)}) async-start(), calls=%async_computation.10 | async-start | bytes 7077888 | tf_op jit(solution)/shard_map/all_gather | solution.py:788
  48.4 94.5 %all-gather.7.cloned.1.call-start = ((), (), s32[]{:S(2)}) async-start(), calls=%async_computation.11 | async-start | bytes 3538944 | tf_op jit(solution)/shard_map/all_gather | solution.py:789
  49.2 170.4 %all-gather.9.cloned.1.call-start = ((), (), s32[]{:S(2)}) async-start(), calls=%async_computation.12 | async-start | bytes 7077888 | tf_op jit(solution)/shard_map/all_gather | solution.py:795
  49.3 14.4 %collective-permute-start = (bf16[128,2048]{1,0:T(8,128)(2,1)S(1)}, bf16[128,2048]{1,0:T(8,128)(2,1)S(1)}, u32[]{:S(2)}, u32[]{:S(2)}) collective-permute-start(bf16[128,2048]{1,0:T(8,128)(2,1)S(1)} %bitcast.53), channel_id=1, source_target_pairs={{0,1},{1,2},{2,3},{3,0},{4,5},{5,6},{6,7},{7,4},{8,9},{9,10},{10,1... | collective-permute-start | bytes 1572872 | tf_op jit(solution)/shard_map/ppermute | solution.py:70
  63.7 13.5 %collective-permute-start.1 = (bf16[128,2048]{1,0:T(8,128)(2,1)S(1)}, bf16[128,2048]{1,0:T(8,128)(2,1)}, u32[]{:S(2)}, u32[]{:S(2)}) collective-permute-start(bf16[128,2048]{1,0:T(8,128)(2,1)S(1)} %collective-permute-done), channel_id=1, source_target_pairs={{0,1},{1,2},{2,3},{3,0},{4,5},{5,6},{6,7},{7,4},{8,9},{9,10},{10,1... | collective-permute-start | bytes 1572872 | tf_op jit(solution)/shard_map/ppermute | solution.py:70
  77.2 12.7 %collective-permute-start.2 = (bf16[128,2048]{1,0:T(8,128)(2,1)}, bf16[128,2048]{1,0:T(8,128)(2,1)S(1)}, u32[]{:S(2)}, u32[]{:S(2)}) collective-permute-start(bf16[128,2048]{1,0:T(8,128)(2,1)} %collective-permute-done.1), channel_id=1, source_target_pairs={{0,1},{1,2},{2,3},{3,0},{4,5},{5,6},{6,7},{7,4},{8,9},{9,10},{10,1... | collective-permute-start | bytes 1572872 | tf_op jit(solution)/shard_map/ppermute | solution.py:70
  91.7 157.7 %all-gather.11.cloned.1.call-start = ((), (), s32[]{:S(2)}) async-start(), calls=%async_computation.13 | async-start | bytes 14155776 | tf_op jit(solution)/shard_map/all_gather | solution.py:796
  94.6 48.2 %all-to-all-start.1 = ((bf16[4,128,2048]{2,1,0:T(8,128)(2,1)}), bf16[4,128,2048]{2,1,0:T(8,128)(2,1)S(1)}, u32[]{:S(2)}, u32[]{:S(2)}) async-start(bf16[4,128,2048]{2,1,0:T(8,128)(2,1)} %broadcast_in_dim.32), calls=%async_computation.1 | async-start | bytes 4194304 | tf_op jit(solution)/shard_map/all_to_all | solution.py:62
  148.6 52.4 %all-to-all-start.2 = ((bf16[4,128,2048]{2,1,0:T(8,128)(2,1)}), bf16[4,128,2048]{2,1,0:T(8,128)(2,1)}, u32[]{:S(2)}, u32[]{:S(2)}) async-start(bf16[4,128,2048]{2,1,0:T(8,128)(2,1)} %bitcast.59), calls=%async_computation.2 | async-start | bytes 4194304 | tf_op jit(solution)/shard_map/all_to_all | solution.py:62
  153.2 297.4 %reduce-scatter.4.cloned.1.call-start = ((), (), s32[]{:S(2)}) async-start(), calls=%async_computation.14 | async-start | bytes 21233664 | tf_op jit(solution)/shard_map/reduce_scatter | solution.py:858
  204.6 14.9 %collective-permute-start.3 = (bf16[128,2048]{1,0:T(8,128)(2,1)}, bf16[128,2048]{1,0:T(8,128)(2,1)S(1)}, u32[]{:S(2)}, u32[]{:S(2)}) collective-permute-start(bf16[128,2048]{1,0:T(8,128)(2,1)} %get-tuple-element.91), channel_id=1, source_target_pairs={{0,1},{1,2},{2,3},{3,0},{4,5},{5,6},{6,7},{7,4},{8,9},{9,10},{10,1... | collective-permute-start | bytes 1572872 | tf_op jit(solution)/shard_map/ppermute | solution.py:70
  219.5 13.9 %collective-permute-start.4 = (bf16[128,2048]{1,0:T(8,128)(2,1)S(1)}, bf16[128,2048]{1,0:T(8,128)(2,1)S(1)}, u32[]{:S(2)}, u32[]{:S(2)}) collective-permute-start(bf16[128,2048]{1,0:T(8,128)(2,1)S(1)} %collective-permute-done.3), channel_id=1, source_target_pairs={{0,1},{1,2},{2,3},{3,0},{4,5},{5,6},{6,7},{7,4},{8,9},{9,10},{10,1... | collective-permute-start | bytes 1572872 | tf_op jit(solution)/shard_map/ppermute | solution.py:70
  233.4 12.8 %collective-permute-start.5 = (bf16[128,2048]{1,0:T(8,128)(2,1)S(1)}, bf16[128,2048]{1,0:T(8,128)(2,1)S(1)}, u32[]{:S(2)}, u32[]{:S(2)}) collective-permute-start(bf16[128,2048]{1,0:T(8,128)(2,1)S(1)} %collective-permute-done.4), channel_id=1, source_target_pairs={{0,1},{1,2},{2,3},{3,0},{4,5},{5,6},{6,7},{7,4},{8,9},{9,10},{10,1... | collective-permute-start | bytes 1572872 | tf_op jit(solution)/shard_map/ppermute | solution.py:70
  287.3 229.1 %reduce-scatter.6.cloned.1.call-start = ((), (), s32[]{:S(2)}) async-start(), calls=%async_computation.15 | async-start | bytes 7077888 | tf_op jit(solution)/shard_map/reduce_scatter | solution.py:612
  346.6 15.0 %collective-permute-start.6 = (bf16[128,2048]{1,0:T(8,128)(2,1)}, bf16[128,2048]{1,0:T(8,128)(2,1)S(1)}, u32[]{:S(2)}, u32[]{:S(2)}) collective-permute-start(bf16[128,2048]{1,0:T(8,128)(2,1)} %get-tuple-element.97), channel_id=1, source_target_pairs={{0,1},{1,2},{2,3},{3,0},{4,5},{5,6},{6,7},{7,4},{8,9},{9,10},{10,1... | collective-permute-start | bytes 1572872 | tf_op jit(solution)/shard_map/ppermute | solution.py:70
  361.5 13.9 %collective-permute-start.7 = (bf16[128,2048]{1,0:T(8,128)(2,1)S(1)}, bf16[128,2048]{1,0:T(8,128)(2,1)S(1)}, u32[]{:S(2)}, u32[]{:S(2)}) collective-permute-start(bf16[128,2048]{1,0:T(8,128)(2,1)S(1)} %collective-permute-done.6), channel_id=1, source_target_pairs={{0,1},{1,2},{2,3},{3,0},{4,5},{5,6},{6,7},{7,4},{8,9},{9,10},{10,1... | collective-permute-start | bytes 1572872 | tf_op jit(solution)/shard_map/ppermute | solution.py:70
  375.4 12.9 %collective-permute-start.8 = (bf16[128,2048]{1,0:T(8,128)(2,1)S(1)}, bf16[128,2048]{1,0:T(8,128)(2,1)S(1)}, u32[]{:S(2)}, u32[]{:S(2)}) collective-permute-start(bf16[128,2048]{1,0:T(8,128)(2,1)S(1)} %collective-permute-done.7), channel_id=1, source_target_pairs={{0,1},{1,2},{2,3},{3,0},{4,5},{5,6},{6,7},{7,4},{8,9},{9,10},{10,1... | collective-permute-start | bytes 1572872 | tf_op jit(solution)/shard_map/ppermute | solution.py:70
  402.0 48.6 %all-to-all-start.4 = ((bf16[4,128,2048]{2,1,0:T(8,128)(2,1)}), bf16[4,128,2048]{2,1,0:T(8,128)(2,1)S(1)}, u32[]{:S(2)}, u32[]{:S(2)}) async-start(bf16[4,128,2048]{2,1,0:T(8,128)(2,1)} %bitcast.57), calls=%async_computation.4 | async-start | bytes 4194304 | tf_op jit(solution)/shard_map/all_to_all | solution.py:62
  452.0 56.9 %all-to-all-start.5 = ((bf16[4,144,2048]{2,1,0:T(8,128)(2,1)}), bf16[4,144,2048]{2,1,0:T(8,128)(2,1)S(1)}, u32[]{:S(2)}, u32[]{:S(2)}) async-start(bf16[4,144,2048]{2,1,0:T(8,128)(2,1)} %get-tuple-element.116), calls=%async_computation.6 | async-start | bytes 4718592 | tf_op jit(solution)/shard_map/all_to_all | solution.py:62
  455.6 73.9 %reduce-scatter.8.cloned.1.call-start = ((), (), s32[]{:S(2)}) async-start(), calls=%async_computation.16 | async-start | bytes 3538944 | tf_op jit(solution)/shard_map/reduce_scatter | solution.py:612
  466.5 55.5 %collective-permute-start.12 = (f32[8,768]{1,0:T(8,128)S(1)}, f32[8,768]{1,0:T(8,128)S(1)}, u32[]{:S(2)}, u32[]{:S(2)}) collective-permute-start(f32[8,768]{1,0:T(8,128)S(1)} %bitcast_reduce_fusion), channel_id=1, source_target_pairs={{0,4},{4,0},{8,12},{12,8},{16,20},{20,16},{24,28},{28,24},{1,5},{5... | collective-permute-start | bytes 73736 | tf_op jit(solution)/shard_map/ppermute | solution.py:81
  512.0 11.6 %collective-permute-start.13 = (bf16[4,171,171]{2,1,0:T(8,128)(2,1)}, bf16[4,171,171]{2,1,0:T(8,128)(2,1)S(1)}, u32[]{:S(2)}, u32[]{:S(2)}) collective-permute-start(bf16[4,171,171]{2,1,0:T(8,128)(2,1)} %get-tuple-element.202), channel_id=1, source_target_pairs={{0,4},{4,0},{8,12},{12,8},{16,20},{20,16},{24,28},{28,24},{1,5},{5... | collective-permute-start | bytes 701792 | tf_op jit(solution)/shard_map/ppermute | solution.py:81
  512.0 11.6 %collective-permute-start.14 = (bf16[4,171,171]{2,1,0:T(8,128)(2,1)}, bf16[4,171,171]{2,1,0:T(8,128)(2,1)S(1)}, u32[]{:S(2)}, u32[]{:S(2)}) collective-permute-start(bf16[4,171,171]{2,1,0:T(8,128)(2,1)} %get-tuple-element.201), channel_id=1, source_target_pairs={{0,4},{4,0},{8,12},{12,8},{16,20},{20,16},{24,28},{28,24},{1,5},{5... | collective-permute-start | bytes 701792 | tf_op jit(solution)/shard_map/ppermute | solution.py:81
  522.1 18.7 %collective-permute-start.10 = (f32[2,2048]{1,0:T(2,128)S(1)}, f32[2,2048]{1,0:T(2,128)S(1)}, u32[]{:S(2)}, u32[]{:S(2)}) collective-permute-start(f32[2,2048]{1,0:T(2,128)S(1)} %add.134), channel_id=1, source_target_pairs={{0,8},{4,12},{8,0},{12,4},{16,24},{20,28},{24,16},{28,20},{1,9},{5... | collective-permute-start | bytes 49160 | tf_op jit(solution)/shard_map/ppermute | solution.py:81
  523.8 19.5 %collective-permute-start.17 = (bf16[4,171,171]{2,1,0:T(8,128)(2,1)S(1)}, bf16[4,171,171]{2,1,0:T(8,128)(2,1)S(1)}, u32[]{:S(2)}, u32[]{:S(2)}) collective-permute-start(bf16[4,171,171]{2,1,0:T(8,128)(2,1)S(1)} %convert_element_type.107), channel_id=1, source_target_pairs={{0,16},{4,20},{8,24},{12,28},{16,0},{20,4},{24,8},{28,12},{1,17},{... | collective-permute-start | bytes 701792 | tf_op jit(solution)/shard_map/ppermute | solution.py:81
  524.3 18.9 %collective-permute-start.15 = (f32[8,768]{1,0:T(8,128)S(1)}, f32[8,768]{1,0:T(8,128)S(1)}, u32[]{:S(2)}, u32[]{:S(2)}) collective-permute-start(f32[8,768]{1,0:T(8,128)S(1)} %add.139), channel_id=1, source_target_pairs={{0,8},{4,12},{8,0},{12,4},{16,24},{20,28},{24,16},{28,20},{1,9},{5... | collective-permute-start | bytes 73736 | tf_op jit(solution)/shard_map/ppermute | solution.py:81
  531.6 36.4 %all-to-all-start.6 = ((bf16[4,3,64,768]{3,2,1,0:T(8,128)(2,1)}), bf16[4,3,64,768]{3,2,1,0:T(8,128)(2,1)S(1)}, u32[]{:S(2)}, u32[]{:S(2)}) async-start(bf16[4,3,64,768]{3,2,1,0:T(8,128)(2,1)} %pad_maximum_fusion.1), calls=%async_computation.9 | async-start | bytes 2359296 | tf_op jit(solution)/shard_map/all_to_all | solution.py:62
  540.8 12.2 %collective-permute-start.11 = (f32[2,2048]{1,0:T(2,128)S(1)}, f32[2,2048]{1,0:T(2,128)S(1)}, u32[]{:S(2)}, u32[]{:S(2)}) collective-permute-start(f32[2,2048]{1,0:T(2,128)S(1)} %add.135), channel_id=1, source_target_pairs={{0,16},{4,20},{8,24},{12,28},{16,0},{20,4},{24,8},{28,12},{1,17},{... | collective-permute-start | bytes 49160 | tf_op jit(solution)/shard_map/ppermute | solution.py:81
  541.5 9.6 %collective-permute-start.16 = (bf16[4,171,171]{2,1,0:T(8,128)(2,1)S(1)}, bf16[4,171,171]{2,1,0:T(8,128)(2,1)S(1)}, u32[]{:S(2)}, u32[]{:S(2)}) collective-permute-start(bf16[4,171,171]{2,1,0:T(8,128)(2,1)S(1)} %convert_element_type.105), channel_id=1, source_target_pairs={{0,8},{4,12},{8,0},{12,4},{16,24},{20,28},{24,16},{28,20},{1,9},{5... | collective-permute-start | bytes 701792 | tf_op jit(solution)/shard_map/ppermute | solution.py:81
  551.2 8.7 %collective-permute-start.20 = (bf16[4,171,171]{2,1,0:T(8,128)(2,1)S(1)}, bf16[4,171,171]{2,1,0:T(8,128)(2,1)S(1)}, u32[]{:S(2)}, u32[]{:S(2)}) collective-permute-start(bf16[4,171,171]{2,1,0:T(8,128)(2,1)S(1)} %convert_element_type.111), channel_id=1, source_target_pairs={{0,8},{4,12},{8,0},{12,4},{16,24},{20,28},{24,16},{28,20},{1,9},{5... | collective-permute-start | bytes 701792 | tf_op jit(solution)/shard_map/ppermute | solution.py:81
  553.1 4.1 collective-permute-start.18
  555.4 8.1 %collective-permute-start.19 = (bf16[4,171,171]{2,1,0:T(8,128)(2,1)S(1)}, bf16[4,171,171]{2,1,0:T(8,128)(2,1)S(1)}, u32[]{:S(2)}, u32[]{:S(2)}) collective-permute-start(bf16[4,171,171]{2,1,0:T(8,128)(2,1)S(1)} %convert_element_type.109), channel_id=1, source_target_pairs={{0,16},{4,20},{8,24},{12,28},{16,0},{20,4},{24,8},{28,12},{1,17},{... | collective-permute-start | bytes 701792 | tf_op jit(solution)/shard_map/ppermute | solution.py:81
  (33 other events, 296.7 us)
Sparse Core Ops, SparseCore 0:
  48.5 44.6 all-gather.4
  95.6 32.3 all-gather.6
  129.9 45.5 all-gather.8
  177.2 72.1 all-gather.10
  287.5 126.1 reduce-scatter.3
  416.9 61.7 reduce-scatter.5
  482.4 47.0 reduce-scatter.7

commit v3 on v2

--- a/solution.py
+++ b/solution.py
@@ -62,19 +62,58 @@
     return lax.all_to_all(parts, "blk", split_axis=0, concat_axis=0, tiled=True)
 
 
-def ring_blk(part, size):
+def ring_blk(part, size, beside=None):
     me, rows = lax.axis_index("blk"), part.shape[0]
     whole = jnp.zeros((size * rows,) + part.shape[1:], part.dtype)
     whole = lax.dynamic_update_slice_in_dim(whole, part, me * rows, axis=0)
     for step in range(1, size):
         part = lax.ppermute(part, "blk", [(place, (place + 1) % size) for place in range(size)])
+        if step == 1 and beside is not None:
+            part, beside = tie(part, beside)
         place = (me - step) % size
         whole = lax.dynamic_update_slice_in_dim(whole, part, place * rows, axis=0)
-    return whole
+    return whole if beside is None else (whole, beside)
+
+
+def ring_sum(partial, size):
+    me, rows = lax.axis_index("blk"), partial.shape[0] // size
+    pick = lambda place: lax.dynamic_slice_in_dim(partial, place % size * rows, rows, axis=0)
+    total = pick(me - 1 + size)
+    for step in range(1, size):
+        total = lax.ppermute(total, "blk", [(place, (place + 1) % size) for place in range(size)])
+        if step < size - 1:
+            total = (total.astype(f32) + pick(me - 1 - step + size).astype(f32)).astype(bf16)
+    return total, pick(me)
 
 
 def for_all(part, size):
     return jnp.broadcast_to(part[None], (size,) + part.shape)
+
+
+def halve(total, size, bit, left):
+    axis = left.index(bit)
+    left.remove(bit)
+    mine = (lax.axis_index("rows") // bit) % 2
+    away = lax.dynamic_index_in_dim(total, 1 - mine, axis, keepdims=False)
+    keep = lax.dynamic_index_in_dim(total, mine, axis, keepdims=False)
+    got = lax.ppermute(away, "rows", flip(size, bit))
+    return (keep.astype(f32) + got.astype(f32)).astype(bf16)
+
+
+def sum_columns(total, size):
+    left = list(reversed(bits_of(size)))
+    total = total.reshape((2,) * len(left) + total.shape[1:])
+    total = halve(total, size, 1, left)
+    half, order = total.shape[-1] // 2, bits_of(size)[1:]
+    found = []
+    for cut, bits in ((total[..., :half], order), (total[..., half:], order[::-1])):
+        rest = list(left)
+        found.append([cut, bits, rest])
+    for at in range(len(order)):
+        for piece in found:
+            piece[0] = halve(piece[0], size, piece[1][at], piece[2])
+        found[0][0], found[1][0] = tie(found[0][0], found[1][0])
+    return jnp.concatenate([found[0][0], found[1][0]], axis=-1)
 
 
 def add_from(value, size, bit, wire=f32):
@@ -108,7 +147,7 @@
             out_ref[:, cut] = parts_ref[part, number, :, :width].astype(f32)
 
 
-def mixer_in_kernel(width, tokens_ref, columns_ref, normed_ref, pre_ref, gains_ref):
+def mixer_in_kernel(width, tokens_ref, columns_ref, normed_ref, signal_ref, branch_ref, gains_ref):
     step = 256
     begin = width // 128 * 128
     turned = columns_ref[:, begin : begin + 128].astype(f32).T
@@ -119,7 +158,10 @@
         here = pl.ds(pl.multiple_of(index * step, step), step)
         values = tokens_ref[here, :].astype(f32)
         normed_ref[here, :] = (values * rms_scale(values) * gain).astype(bf16)
-        pre_ref[here, :] = mm(normed_ref[here, :], columns_ref[...], ((1,), (0,)))
+        value = mm(normed_ref[here, :], columns_ref[...], ((1,), (0,)))
+        wide = signal_ref.shape[1]
+        signal_ref[here, :] = value[:, :wide].astype(bf16)
+        branch_ref[here, :] = value[:, wide:]
         return carry
 
     lax.fori_loop(0, tokens_ref.shape[0] // step, rows_step, 0)
@@ -132,12 +174,13 @@
     return total
 
 
-def mid_norm_kernel(gain_ref, tokens_ref, parts_ref, mid_ref, normed_ref):
+def mid_norm_kernel(gain_ref, tokens_ref, one_ref, two_ref, mid_ref, normed_ref):
     step = 32
 
     def rows_step(index, carry):
         here = pl.ds(pl.multiple_of(index * step, step), step)
-        values = tokens_ref[here, :].astype(f32) + sum_parts(parts_ref, here)
+        values = tokens_ref[here, :].astype(f32) + one_ref[here, :].astype(f32)
+        values = values + two_ref[here, :].astype(f32)
         mid_ref[here, :] = values
         normed = (values * rms_scale(values) * gain_ref[...]).astype(bf16)
         normed_ref[here, :] = normed
@@ -157,13 +200,16 @@
     return scale * (grad * gain) - values * factor, product * scale
 
 
-def mid_grad_kernel(gain_ref, mid_ref, cotangent_ref, parts_ref, grad_ref, sent_ref, sums_ref):
+def mid_grad_kernel(
+    gain_ref, mid_ref, cotangent_ref, one_ref, two_ref, grad_ref, sent_ref, sums_ref
+):
     step = 32
     sums_ref[...] = jnp.zeros_like(sums_ref)
 
     def rows_step(index, carry):
         here = pl.ds(pl.multiple_of(index * step, step), step)
-        change, terms = norm_back(sum_parts(parts_ref, here), mid_ref[here, :], gain_ref[...])
+        grad = one_ref[here, :].astype(f32) + two_ref[here, :].astype(f32)
+        change, terms = norm_back(grad, mid_ref[here, :], gain_ref[...])
         sums_ref[...] += fold8(terms)
         result = cotangent_ref[here, :].astype(f32) + change
         grad_ref[here, :] = result
@@ -369,8 +415,9 @@
     input_high_any,
     input_low_any,
     both_any,
+    normed_any,
     tokens_any,
-    both_grad_ref,
+    late_ref,
     decay_pre_ref,
     input_pre_ref,
     sums_ref,
@@ -385,7 +432,9 @@
     input_high,
     input_low,
     both_ref,
+    normed_ref,
     tokens_ref,
+    both_grad_ref,
     padded,
     grads,
     earlier,
@@ -407,6 +456,7 @@
         (input_high_any, input_high),
         (input_low_any, input_low),
         (both_any, both_ref),
+        (normed_any, normed_ref),
     ]
     copies = [
         pltpu.make_async_copy(source, target, arrived.at[number])
@@ -518,6 +568,16 @@
 
     lax.fori_loop(0, count, conv_step, 0)
     copies[9].wait()
+    copies[10].wait()
+    each = late_ref.shape[1] * late_ref.shape[3]
+
+    def late_step(index, carry):
+        rows = pl.ds(pl.multiple_of(index * each, each), each)
+        value = mm(normed_ref[:, rows], both_grad_ref[:, :width], ((0,), (0,))).astype(bf16)
+        late_ref[index, :, 0] = value.reshape(late_ref.shape[1], *late_ref.shape[3:])
+        return carry
+
+    lax.fori_loop(0, late_ref.shape[0], late_step, 0)
     parts, rows, model_width = token_ref.shape
     rows = rows - gain_rows
     gain_sums[...] = jnp.zeros_like(gain_sums)
@@ -559,12 +619,12 @@
     )
 
 
-def mixer_backward(resident, fetched, parts, tiles):
+def mixer_backward(resident, fetched, size, parts, tiles):
     length, wide = resident[0].shape
     model_width = fetched[-1].shape[1]
     whole = ((length, wide), f32)
     outs = [
-        ((length, 2 * wide), bf16),
+        ((size, parts, 1, model_width // size // parts, wide), bf16),
         whole,
         whole,
         ((64, wide), f32),
@@ -578,6 +638,7 @@
         out_specs=vmem_specs(len(outs)),
         scratch_shapes=[pltpu.VMEM(value.shape, value.dtype) for value in fetched[:-1]]
         + [pltpu.VMEM((length // parts, model_width), bf16)]
+        + [pltpu.VMEM((length, 2 * wide), bf16)]
         + [padded] * 3
         + [pltpu.VMEM((length, wide), bf16)] * 4
         + [pltpu.VMEM((8, model_width), f32), pltpu.SemaphoreType.DMA((len(fetched),))],
@@ -608,9 +669,7 @@
         compiler_params=pltpu.CompilerParams(vmem_limit_bytes=vmem_limit),
         name="column_grads",
     )(*lefts, *rights)
-    total = total.reshape(size * count * each, wide)
-    total = lax.psum_scatter(total, "rows", scatter_dimension=0, tiled=True)
-    return total.reshape(parts, count, each // parts, wide)
+    return total
 
 
 def gate_grads_kernel(tiles, conv_ref, decay_pre_ref, input_pre_ref, gates_ref, dense, pairs):
@@ -784,18 +843,24 @@
         [((n_blk, shard, 3 * wide), bf16)],
     )
     columns = swap_blk(column_parts).reshape(n_blk * shard, 3 * wide)
-    columns, token_own = tie(columns, own_tokens)
+    weights = local_kernel(
+        dense_kernel, "dense_gates", (decay_gate, input_gate), [((wide, wide), bf16)] * 4
+    )
+    down_units = lax.all_gather(hidden_down, "rows", axis=0, tiled=True)
+    columns, token_own, grad_own, first_own, *weights = tie(
+        columns,
+        own_tokens,
+        for_all(own_grad, n_blk),
+        jnp.concatenate([hidden_gate, hidden_up], axis=0),
+        *weights,
+    )
     both_columns = lax.all_gather(columns[:, : 2 * wide], "rows", axis=0, tiled=True)
     output_columns = lax.all_gather(columns[:, 2 * wide :], "rows", axis=0, tiled=True)
-    tokens_all = ring_blk(token_own, n_blk)
-    tokens_all, grad_own, hidden_gate, hidden_up, hidden_down = tie(
-        tokens_all, for_all(own_grad, n_blk), hidden_gate, hidden_up, hidden_down
-    )
+    tokens_all, down_units = ring_blk(token_own, n_blk, down_units)
+    tokens_all, grad_own, first_own = tie(tokens_all, grad_own, first_own)
     out_grad = swap_blk(grad_own).reshape(n_blk * tok_count, model_width)
-    down_units = lax.all_gather(hidden_down, "rows", axis=0, tiled=True)
-    first_units = lax.all_gather(
-        jnp.concatenate([hidden_gate, hidden_up], axis=0), "rows", axis=0, tiled=True
-    ).reshape(n_rows, 2, units, model_width)
+    first_units = lax.all_gather(first_own, "rows", axis=0, tiled=True)
+    first_units = first_units.reshape(n_rows, 2, units, model_width)
 
     masks = [jnp.ones_like(segments, dtype=f32)]
     for tap in range(1, 4):
@@ -817,35 +882,29 @@
         axis=0,
     )
     vectors = jnp.pad(vectors, ((0, 0), (0, wide - width)), constant_values=1.0)
-    weights = local_kernel(
-        dense_kernel, "dense_gates", (decay_gate, input_gate), [((wide, wide), bf16)] * 4
-    )
-    mixer_normed, both_pre, gains = local_kernel(
+    mixer_normed, signal, branch_pre, gains = local_kernel(
         functools.partial(mixer_in_kernel, width),
         "mixer_in",
         (tokens_all, both_columns),
         [
             (tokens_all.shape, bf16),
-            ((n_blk * tok_count, 2 * wide), f32),
+            ((n_blk * tok_count, wide), bf16),
+            ((n_blk * tok_count, wide), f32),
             ((2, model_width), f32),
         ],
     )
     mixer_gains, mlp_gains = gains[0:1], gains[1:2]
-    signal, branch_pre = both_pre[:, :wide].astype(bf16), both_pre[:, wide:]
     states, state_values, conv_out, decay_rate, input_rate = recur_forward(
         signal, masks, vectors, weights, tiles
     )
     mixed = (gelu_tanh(branch_pre) * state_values.astype(f32)).astype(bf16)
-    mixed, out_grad = tie(mixed, out_grad)
-
-    def scatter_blk(partial):
-        return swap_blk(partial.astype(bf16).reshape(n_blk, tok_count, model_width))
-
-    mid_parts = scatter_blk(mm(mixed, output_columns, ((1,), (1,))))
+    mid_partial = mm(mixed, output_columns, ((1,), (1,))).astype(bf16)
+    mid_partial, out_grad = tie(mid_partial, out_grad)
+    mid_parts = ring_sum(mid_partial, n_blk)
     residual_mid, own_normed = local_kernel(
         mid_norm_kernel,
         "mid_norm",
-        (mlp_gains, own_tokens, mid_parts),
+        (mlp_gains, own_tokens, *mid_parts),
         [(square, f32), (square, bf16)],
     )
 
@@ -854,7 +913,7 @@
     normed_partial, out_partial, unit_sums = mlp(
         mlp_normed, out_grad, hidden_grad, first_units, down_units
     )
-    normed_parts = scatter_blk(normed_partial)
+    normed_parts = ring_sum(normed_partial, n_blk)
     unit_sums = lax.psum_scatter(
         unit_sums.reshape(n_rows * 3 * units, model_width),
         "rows",
@@ -865,19 +924,23 @@
     mid_grad, own_sent, mlp_gain_part = local_kernel(
         mid_grad_kernel,
         "mid_grad",
-        (mlp_gains, residual_mid, own_grad, normed_parts),
+        (mlp_gains, residual_mid, own_grad, *normed_parts),
         [(square, f32), (square, bf16), ((8, model_width), f32)],
     )
     mid_sent = ring_blk(own_sent, n_blk)
 
     mid_sent, out_partial = tie(mid_sent, out_partial)
-    out_parts = scatter_blk(out_partial)
+    out_parts = swap_blk(out_partial.reshape(n_blk, tok_count, model_width))
     mixed_grad = mm(mid_sent, output_columns, ((1,), (0,)))
     branch_act, branch_slope = gelu_parts(branch_pre)
     state_grad = (mixed_grad * branch_act).astype(bf16)
     branch_grad = (mixed_grad * state_values.astype(f32) * branch_slope).astype(bf16)
     early_sum = column_grads((mid_sent, mixer_normed), (mixed, branch_grad), n_rows, n_blk)
-    both_grad, decay_pre_grad, input_pre_grad, sums, token_sent = mixer_backward(
+    early_shape = early_sum.shape[1:]
+    early_sum = lax.psum_scatter(
+        early_sum.reshape(-1, wide), "rows", scatter_dimension=0, tiled=True
+    ).reshape(early_shape)
+    late_sum, decay_pre_grad, input_pre_grad, sums, token_sent = mixer_backward(
         (state_grad, branch_grad, masks, vectors, mlp_gain_part),
         (
             signal,
@@ -887,16 +950,18 @@
             input_rate,
             *weights,
             both_columns,
+            mixer_normed,
             tokens_all,
         ),
+        n_rows,
         n_blk,
         tiles,
     )
-    token_sent, out_parts, unit_sums, both_grad, decay_pre_grad, input_pre_grad, sums = tie(
-        token_sent, out_parts, unit_sums, both_grad, decay_pre_grad, input_pre_grad, sums
+    token_sent, out_parts, unit_sums, late_sum, decay_pre_grad, input_pre_grad, sums = tie(
+        token_sent, out_parts, unit_sums, late_sum, decay_pre_grad, input_pre_grad, sums
     )
     token_parts = swap_blk(token_sent)
-    late_sum = column_grads((mixer_normed,), (both_grad[:, :wide],), n_rows, n_blk)
+    late_sum = sum_columns(late_sum, n_rows)
     (gate_sums,) = local_kernel(
         functools.partial(gate_grads_kernel, tiles),
         "gate_grads",
@@ -914,7 +979,7 @@
             gate_sums[number] = add_from(gate_sums[number], n_rows, order[at], bf16)
         vector_sums = add_from(vector_sums, n_rows, bit)
         vector_sums, *gate_sums = tie(vector_sums, *gate_sums)
-    token_parts, early_sum = tie(token_parts, early_sum)
+    token_parts, early_sum, late_sum = tie(token_parts, early_sum, late_sum)
     vector_sums = vector_sums[:, :width]
     token_grad, gain_sums = local_kernel(
         token_grad_kernel,

time: 588 us -> 542 us (0.922)
  blocking collectives: 88.2 us -> 0 us
  waiting for transfers between devices: 242 us -> 281 us
    ppermute x0 -> x11, waiting for transfers between devices: none -> 105 us  [the longest x6 80.2 us: ring_sum(): lax.ppermute(total, 'blk', [(place, (place + 1) % size) for place in rang...]
    all_to_all x2 -> x0, blocking collectives: 88.2 us -> none  [swap_blk(): return lax.all_to_all(parts, 'blk', split_axis=0, concat_axis=0, tiled=True)]
    all_to_all x5, waiting for transfers between devices: 107 us -> 34.8 us  [swap_blk(): return lax.all_to_all(parts, 'blk', split_axis=0, concat_axis=0, tiled=True)]
    all_gather x1, waiting for transfers between devices: 0.01 us -> 9.25 us  [body(): lax.all_gather(columns[:, 2 * wide:], 'rows', axis=0, tiled=True)]
    pallas_call x2 -> x1, Pallas kernels: 17.4 us -> 9.6 us  [column_grads(): pl.pallas_call(functools.partial(column_grads_kernel, count), grid=(size,...]
    ppermute x0 -> x11, starting transfers between devices: none -> 6.06 us  [the longest x5 4.12 us: halve(): got = lax.ppermute(away, 'rows', flip(size, bit))]
    unnamed x68 -> x74, local copies, waits for them, and re-layouts: 10.2 us -> 12.5 us
  transfers between devices with their start and end apart: 33 -> 43, of which waited for: 19 -> 28; matrix products, arithmetic and copies ran while one was open for 10% -> 11% of each run, Pallas kernels for 16% -> 17%
where the time goes in v3:
time: 542 us; the launch traced here: 533 us
  waiting for transfers between devices  281 us (52%)
  Pallas kernels  132 us (24%)
  starting transfers between devices  38.7 us (7%)
  local copies, waits for them, and re-layouts  33.5 us (6%)
  other arithmetic  16.6 us (3%)
  matrix products  16 us (3%)
  between operations  15.5 us (3%)
    ppermute x9, waiting for transfers between devices, ring_blk(): lax.ppermute(part, 'blk', [(place, (place + 1) % size) for place in range...  111 us
    ppermute x6, waiting for transfers between devices, ring_sum(): lax.ppermute(total, 'blk', [(place, (place + 1) % size) for place in rang...  80.2 us
    pallas_call x9, Pallas kernels, local_kernel(): pl.pallas_call(kernel, out_shape=[jax.ShapeDtypeStruct(shape, kind) for s...  51 us
    pallas_call x1, Pallas kernels, mlp(): pl.pallas_call(mlp_kernel, grid=(total // tile,), out_shape=[whole, whole...  37.9 us
    all_to_all x5, waiting for transfers between devices, swap_blk(): return lax.all_to_all(parts, 'blk', split_axis=0, concat_axis=0, tiled=True)  34.8 us
    pallas_call x1, Pallas kernels, mixer_backward(): pl.pallas_call(functools.partial(mixer_backward_kernel, tiles), out_shape...  33 us
    ppermute x5, waiting for transfers between devices, halve(): got = lax.ppermute(away, 'rows', flip(size, bit))  25.2 us
    all_to_all x5, starting transfers between devices, swap_blk(): return lax.all_to_all(parts, 'blk', split_axis=0, concat_axis=0, tiled=True)  22.1 us
  transfers between devices with their start and end apart: 43, of which 28 were waited for; matrix products, arithmetic and copies ran while one was open for 11% of the time, Pallas kernels for 17%

profile of v3, /device:TPU:0, one launch (start us, length us, event | category | flops | bytes accessed | tf_op | source)
XLA Modules:
  0.0 532.9 jit_solution(8292095379090432578)
XLA Ops:
  13.3 6.3 %all-to-all-start = ((bf16[4,64,2304]{2,1,0:T(8,128)(2,1)}), bf16[4,64,2304]{2,1,0:T(8,128)(2,1)S(1)}, u32[]{:S(2)}, u32[]{:S(2)}) async-start(bf16[4,64,2304]{2,1,0:T(8,128)(2,1)} %split_columns.1), calls=%async_computation | async-start | bytes 2359296 | tf_op jit(solution)/shard_map/all_to_all | solution.py:62
  22.8 4.3 dense_gates.1
  28.4 19.8 %all-to-all-done = bf16[4,64,2304]{2,1,0:T(8,128)(2,1)S(1)} async-done(((bf16[4,64,2304]{2,1,0:T(8,128)(2,1)}), bf16[4,64,2304]{2,1,0:T(8,128)(2,1)S(1)}, u32[]{:S(2)}, u32[]{:S(2)}) %all-to-all-start) | async-done | bytes 1179680 | tf_op jit(solution)/shard_map/all_to_all | solution.py:62
  51.7 14.7 %collective-permute-done = bf16[128,2048]{1,0:T(8,128)(2,1)S(1)} collective-permute-done((bf16[128,2048]{1,0:T(8,128)(2,1)S(1)}, bf16[128,2048]{1,0:T(8,128)(2,1)S(1)}, u32[]{:S(2)}, u32[]{:S(2)}) %collective-permute-start) | collective-permute-done | bytes 524320 | tf_op jit(solution)/shard_map/ppermute | solution.py:70
  66.4 13.9 %collective-permute-done.1 = bf16[128,2048]{1,0:T(8,128)(2,1)} collective-permute-done((bf16[128,2048]{1,0:T(8,128)(2,1)S(1)}, bf16[128,2048]{1,0:T(8,128)(2,1)}, u32[]{:S(2)}, u32[]{:S(2)}) %collective-permute-start.1) | collective-permute-done | bytes 524320 | tf_op jit(solution)/shard_map/ppermute | solution.py:70
  81.7 11.6 %collective-permute-done.2 = bf16[128,2048]{1,0:T(8,128)(2,1)S(1)} collective-permute-done((bf16[128,2048]{1,0:T(8,128)(2,1)}, bf16[128,2048]{1,0:T(8,128)(2,1)S(1)}, u32[]{:S(2)}, u32[]{:S(2)}) %collective-permute-start.2) | collective-permute-done | bytes 524320 | tf_op jit(solution)/shard_map/ppermute | solution.py:70
  94.7 4.5 all-to-all-start.1
  101.6 4.6 all-gather.7.cloned.1.call-done.columns_ref.both_any
  106.2 8.9 %mixer_in.1 = (bf16[512,2048]{1,0:T(8,128)(2,1)}, bf16[512,768]{1,0:T(8,128)(2,1)}, f32[512,768]{1,0:T(8,128)}, f32[2,2048]{1,0:T(2,128)}) custom-call(bf16[512,2048]{1,0:T(8,128)(2,1)} %copy-done, bf16[2048,1536]{1,0:T(8,128)(2,1)} %all-gather.7.cloned.1.call-done.columns_ref.both_any), custom_call_target="tpu_custom_call" | custom-call | tf_op jit(solution)/shard_map/mixer_in/pallas_call | solution.py:245
  115.1 14.9 %recur_forward.1 = (f32[512,768]{1,0:T(8,128)}, bf16[512,768]{1,0:T(8,128)(2,1)}, f32[512,768]{1,0:T(8,128)}, f32[512,768]{1,0:T(8,128)}, f32[512,768]{1,0:T(8,128)}) custom-call(bf16[512,768]{1,0:T(8,128)(2,1)} %get-tuple-element.102.signal_ref.signal_any, f32[520,8]{1,0:T(8,128)} %pad.12.masks_ref, f32[8,768]{1,0:T(8,128)} %pad.13.vectors_ref, ...), custom_call_target="tpu_custom_call" | custom-call | tf_op jit(solution)/shard_map/recur_forward/pallas_call | solution.py:245
  131.8 9.2 %all-gather.9.cloned.1.call-done = bf16[2048,768]{1,0:T(8,128)(2,1)} async-done(((bf16[256,768]{1,0:T(8,128)(2,1)}), bf16[2048,768]{1,0:T(8,128)(2,1)}) %all-gather.9.cloned.1.call-update) | async-done | bytes 3145744 | tf_op jit(solution)/shard_map/all_gather | solution.py:858
  147.1 14.4 %collective-permute-done.3 = bf16[128,2048]{1,0:T(8,128)(2,1)S(1)} collective-permute-done((bf16[128,2048]{1,0:T(8,128)(2,1)S(1)}, bf16[128,2048]{1,0:T(8,128)(2,1)S(1)}, u32[]{:S(2)}, u32[]{:S(2)}) %collective-permute-start.3) | collective-permute-done | bytes 524320 | tf_op jit(solution)/shard_map/ppermute | solution.py:83
  161.7 15.0 %collective-permute-done.4 = bf16[128,2048]{1,0:T(8,128)(2,1)S(1)} collective-permute-done((bf16[128,2048]{1,0:T(8,128)(2,1)S(1)}, bf16[128,2048]{1,0:T(8,128)(2,1)S(1)}, u32[]{:S(2)}, u32[]{:S(2)}) %collective-permute-start.4) | collective-permute-done | bytes 524320 | tf_op jit(solution)/shard_map/ppermute | solution.py:83
  177.6 13.5 %collective-permute-done.5.one_ref = bf16[128,2048]{1,0:T(8,128)(2,1)S(1)} collective-permute-done((bf16[128,2048]{1,0:T(8,128)(2,1)S(1)}, bf16[128,2048]{1,0:T(8,128)(2,1)S(1)}, u32[]{:S(2)}, u32[]{:S(2)}) %collective-permute-start.5) | collective-permute-done | bytes 524320 | tf_op jit(solution)/shard_map/ppermute | solution.py:83
  195.1 13.4 %collective-permute-done.6 = bf16[128,2048]{1,0:T(8,128)(2,1)S(1)} collective-permute-done((bf16[128,2048]{1,0:T(8,128)(2,1)}, bf16[128,2048]{1,0:T(8,128)(2,1)S(1)}, u32[]{:S(2)}, u32[]{:S(2)}) %collective-permute-start.6) | collective-permute-done | bytes 524320 | tf_op jit(solution)/shard_map/ppermute | solution.py:70
  208.6 8.6 %fusion.27.hidden_grad_ref = f32[512,1536]{1,0:T(8,128)} fusion(bf16[512,2048]{1,0:T(8,128)(2,1)} %bitcast.10.cotangent_ref, bf16[1536,2048]{1,0:T(8,128)(2,1)} %all-gather.5.cloned.1.call-done.down_ref), kind=kOutput, calls=%fused_computation.99 | convolution fusion | flops 3221225472 | bytes 11534336 | tf_op jit(solution)/shard_map/dot_general | solution.py:37
  221.3 10.9 %collective-permute-done.8 = bf16[128,2048]{1,0:T(8,128)(2,1)S(1)} collective-permute-done((bf16[128,2048]{1,0:T(8,128)(2,1)S(1)}, bf16[128,2048]{1,0:T(8,128)(2,1)S(1)}, u32[]{:S(2)}, u32[]{:S(2)}) %collective-permute-start.8) | collective-permute-done | bytes 524320 | tf_op jit(solution)/shard_map/ppermute | solution.py:70
  233.5 37.9 %mlp.1 = (bf16[512,2048]{1,0:T(8,128)(2,1)}, bf16[512,2048]{1,0:T(8,128)(2,1)}, bf16[8,3,192,2048]{3,2,1,0:T(8,128)(2,1)}) custom-call(bf16[512,2048]{1,0:T(8,128)(2,1)} %copy-done.3, bf16[512,2048]{1,0:T(8,128)(2,1)} %bitcast.10.cotangent_ref, f32[512,1536]{1,0:T(8,128)} %fusion.27.hidden_grad_ref, bf16[8,2,192,2048]{3,2,1,0:T(8,128)(2,1)} %bitcast.67, ...), custom_call_target="tpu_custom_call" | custom-call | tf_op jit(solution)/shard_map/mlp/pallas_call | solution.py:787
  273.9 12.5 %collective-permute-done.9 = bf16[128,2048]{1,0:T(8,128)(2,1)S(1)} collective-permute-done((bf16[128,2048]{1,0:T(8,128)(2,1)S(1)}, bf16[128,2048]{1,0:T(8,128)(2,1)S(1)}, u32[]{:S(2)}, u32[]{:S(2)}) %collective-permute-start.9) | collective-permute-done | bytes 524320 | tf_op jit(solution)/shard_map/ppermute | solution.py:83
  286.8 13.8 %collective-permute-done.10 = bf16[128,2048]{1,0:T(8,128)(2,1)S(1)} collective-permute-done((bf16[128,2048]{1,0:T(8,128)(2,1)S(1)}, bf16[128,2048]{1,0:T(8,128)(2,1)S(1)}, u32[]{:S(2)}, u32[]{:S(2)}) %collective-permute-start.10) | collective-permute-done | bytes 524320 | tf_op jit(solution)/shard_map/ppermute | solution.py:83
  300.8 11.0 %collective-permute-done.11.one_ref = bf16[128,2048]{1,0:T(8,128)(2,1)S(1)} collective-permute-done((bf16[128,2048]{1,0:T(8,128)(2,1)S(1)}, bf16[128,2048]{1,0:T(8,128)(2,1)S(1)}, u32[]{:S(2)}, u32[]{:S(2)}) %collective-permute-start.11) | collective-permute-done | bytes 524320 | tf_op jit(solution)/shard_map/ppermute | solution.py:83
  316.5 16.8 %collective-permute-done.12 = bf16[128,2048]{1,0:T(8,128)(2,1)S(1)} collective-permute-done((bf16[128,2048]{1,0:T(8,128)(2,1)}, bf16[128,2048]{1,0:T(8,128)(2,1)S(1)}, u32[]{:S(2)}, u32[]{:S(2)}) %collective-permute-start.12) | collective-permute-done | bytes 524320 | tf_op jit(solution)/shard_map/ppermute | solution.py:70
  333.3 15.7 %collective-permute-done.13 = bf16[128,2048]{1,0:T(8,128)(2,1)S(1)} collective-permute-done((bf16[128,2048]{1,0:T(8,128)(2,1)S(1)}, bf16[128,2048]{1,0:T(8,128)(2,1)S(1)}, u32[]{:S(2)}, u32[]{:S(2)}) %collective-permute-start.13) | collective-permute-done | bytes 524320 | tf_op jit(solution)/shard_map/ppermute | solution.py:70
  349.5 10.5 %collective-permute-done.14 = bf16[128,2048]{1,0:T(8,128)(2,1)S(1)} collective-permute-done((bf16[128,2048]{1,0:T(8,128)(2,1)S(1)}, bf16[128,2048]{1,0:T(8,128)(2,1)S(1)}, u32[]{:S(2)}, u32[]{:S(2)}) %collective-permute-start.14) | collective-permute-done | bytes 524320 | tf_op jit(solution)/shard_map/ppermute | solution.py:70
  363.8 9.6 %column_grads.1 = bf16[8,4,2,64,768]{4,3,2,1,0:T(8,128)(2,1)} custom-call(bf16[512,2048]{1,0:T(8,128)(2,1)} %copy-done.6, bf16[512,2048]{1,0:T(8,128)(2,1)} %get-tuple-element.124.normed_any.refs_1_, bf16[512,768]{1,0:T(8,128)(2,1)} %copy-done.11, bf16[512,768]{1,0:T(8,128)(2,1)} %get-tuple-element.218.branch_grad_ref.refs_3_), custom_call_target="tpu_custom_call" | custom-call | tf_op jit(solution)/shard_map/column_grads/pallas_call | solution.py:662
  377.1 33.0 %mixer_backward.1 = (bf16[8,4,1,64,768]{4,3,2,1,0:T(8,128)(2,1)}, f32[512,768]{1,0:T(8,128)}, f32[512,768]{1,0:T(8,128)}, f32[64,768]{1,0:T(8,128)}, bf16[4,144,2048]{2,1,0:T(8,128)(2,1)}) custom-call(bf16[512,768]{1,0:T(8,128)(2,1)} %get-tuple-element.219.state_grad_ref, bf16[512,768]{1,0:T(8,128)(2,1)} %get-tuple-element.218.branch_grad_ref.refs_3_, ...), custom_call_target="tpu_custom_call" | custom-call | tf_op jit(solution)/shard_map/mixer_backward/pallas_call | solution.py:634
  417.4 4.0 all-to-all-start.3
  429.4 15.9 %collective-permute-done.17 = bf16[2,4,1,64,384]{4,3,1,2,0:T(8,128)(2,1)S(1)} collective-permute-done((bf16[2,4,1,64,384]{4,3,1,2,0:T(8,128)(2,1)S(1)}, bf16[2,4,1,64,384]{4,3,1,2,0:T(8,128)(2,1)S(1)}, u32[]{:S(2)}, u32[]{:S(2)}) %collective-permute-start.17) | collective-permute-done | bytes 393248 | tf_op jit(solution)/shard_map/ppermute | solution.py:99
  448.7 6.2 %gate_grads.1 = f32[2,4,171,171]{3,2,1,0:T(8,128)} custom-call(f32[512,768]{1,0:T(8,128)} %get-tuple-element.121.conv_any.conv_ref, f32[512,768]{1,0:T(8,128)} %get-tuple-element.134.decay_pre_ref, f32[512,768]{1,0:T(8,128)} %get-tuple-element.135.input_pre_ref), custom_call_target="tpu_custom_call" | custom-call | tf_op jit(solution)/shard_map/gate_grads/pallas_call | solution.py:245
  457.1 7.7 %collective-permute-done.18 = bf16[4,1,64,384]{3,2,0,1:T(8,128)(2,1)S(1)} collective-permute-done((bf16[4,1,64,384]{3,2,0,1:T(8,128)(2,1)S(1)}, bf16[4,1,64,384]{3,2,0,1:T(8,128)(2,1)S(1)}, u32[]{:S(2)}, u32[]{:S(2)}) %collective-permute-start.18) | collective-permute-done | bytes 196640 | tf_op jit(solution)/shard_map/ppermute | solution.py:99
  464.9 11.2 %all-to-all-done.3.parts_ref = bf16[4,144,2048]{2,1,0:T(8,128)(2,1)S(1)} async-done(((bf16[4,144,2048]{2,1,0:T(8,128)(2,1)}), bf16[4,144,2048]{2,1,0:T(8,128)(2,1)S(1)}, u32[]{:S(2)}, u32[]{:S(2)}) %all-to-all-start.3) | async-done | bytes 2359328 | tf_op jit(solution)/shard_map/all_to_all | solution.py:62
  497.8 5.4 %collective-permute-done.28 = bf16[4,171,171]{2,1,0:T(8,128)(2,1)S(1)} collective-permute-done((bf16[4,171,171]{2,1,0:T(8,128)(2,1)S(1)}, bf16[4,171,171]{2,1,0:T(8,128)(2,1)S(1)}, u32[]{:S(2)}, u32[]{:S(2)}) %collective-permute-start.28) | collective-permute-done | bytes 233960 | tf_op jit(solution)/shard_map/ppermute | solution.py:120
  (234 shorter events, 117.6 us)
Async XLA Ops:
  7.2 59.2 %all-gather.5.cloned.1.call-start = ((), (), s32[]{:S(2)}) async-start(), calls=%async_computation.7 | async-start | bytes 7077888 | tf_op jit(solution)/shard_map/all_gather | solution.py:849
  13.3 34.9 %all-to-all-start = ((bf16[4,64,2304]{2,1,0:T(8,128)(2,1)}), bf16[4,64,2304]{2,1,0:T(8,128)(2,1)S(1)}, u32[]{:S(2)}, u32[]{:S(2)}) async-start(bf16[4,64,2304]{2,1,0:T(8,128)(2,1)} %split_columns.1), calls=%async_computation | async-start | bytes 2359296 | tf_op jit(solution)/shard_map/all_to_all | solution.py:62
  19.6 86.5 %all-gather.7.cloned.1.call-start = ((), (), s32[]{:S(2)}) async-start(), calls=%async_computation.8 | async-start | bytes 7077888 | tf_op jit(solution)/shard_map/all_gather | solution.py:857
  50.7 90.3 %all-gather.9.cloned.1.call-start = ((), (), s32[]{:S(2)}) async-start(), calls=%async_computation.9 | async-start | bytes 3538944 | tf_op jit(solution)/shard_map/all_gather | solution.py:858
  51.6 180.7 %all-gather.11.cloned.1.call-start = ((), (), s32[]{:S(2)}) async-start(), calls=%async_computation.10 | async-start | bytes 14155776 | tf_op jit(solution)/shard_map/all_gather | solution.py:862
  51.6 14.7 %collective-permute-start = (bf16[128,2048]{1,0:T(8,128)(2,1)S(1)}, bf16[128,2048]{1,0:T(8,128)(2,1)S(1)}, u32[]{:S(2)}, u32[]{:S(2)}) collective-permute-start(bf16[128,2048]{1,0:T(8,128)(2,1)S(1)} %bitcast.75), channel_id=1, source_target_pairs={{0,1},{1,2},{2,3},{3,0},{4,5},{5,6},{6,7},{7,4},{8,9},{9,10},{10,1... | collective-permute-start | bytes 1572872 | tf_op jit(solution)/shard_map/ppermute | solution.py:70
  66.4 13.9 %collective-permute-start.1 = (bf16[128,2048]{1,0:T(8,128)(2,1)S(1)}, bf16[128,2048]{1,0:T(8,128)(2,1)}, u32[]{:S(2)}, u32[]{:S(2)}) collective-permute-start(bf16[128,2048]{1,0:T(8,128)(2,1)S(1)} %collective-permute-done), channel_id=1, source_target_pairs={{0,1},{1,2},{2,3},{3,0},{4,5},{5,6},{6,7},{7,4},{8,9},{9,10},{10,1... | collective-permute-start | bytes 1572872 | tf_op jit(solution)/shard_map/ppermute | solution.py:70
  80.2 13.1 %collective-permute-start.2 = (bf16[128,2048]{1,0:T(8,128)(2,1)}, bf16[128,2048]{1,0:T(8,128)(2,1)S(1)}, u32[]{:S(2)}, u32[]{:S(2)}) collective-permute-start(bf16[128,2048]{1,0:T(8,128)(2,1)} %collective-permute-done.1), channel_id=1, source_target_pairs={{0,1},{1,2},{2,3},{3,0},{4,5},{5,6},{6,7},{7,4},{8,9},{9,10},{10,1... | collective-permute-start | bytes 1572872 | tf_op jit(solution)/shard_map/ppermute | solution.py:70
  94.7 50.1 %all-to-all-start.1 = ((bf16[4,128,2048]{2,1,0:T(8,128)(2,1)}), bf16[4,128,2048]{2,1,0:T(8,128)(2,1)}, u32[]{:S(2)}, u32[]{:S(2)}) async-start(bf16[4,128,2048]{2,1,0:T(8,128)(2,1)} %broadcast_in_dim.32), calls=%async_computation.1 | async-start | bytes 4194304 | tf_op jit(solution)/shard_map/all_to_all | solution.py:62
  99.2 314.8 %reduce-scatter.3.cloned.1.call-start = ((), (), s32[]{:S(2)}) async-start(), calls=%async_computation.11 | async-start | bytes 21233664 | tf_op jit(solution)/shard_map/reduce_scatter | solution.py:917
  145.6 15.9 %collective-permute-start.3 = (bf16[128,2048]{1,0:T(8,128)(2,1)S(1)}, bf16[128,2048]{1,0:T(8,128)(2,1)S(1)}, u32[]{:S(2)}, u32[]{:S(2)}) collective-permute-start(bf16[128,2048]{1,0:T(8,128)(2,1)S(1)} %get-tuple-element.226), channel_id=1, source_target_pairs={{0,1},{1,2},{2,3},{3,0},{4,5},{5,6},{6,7},{7,4},{8,9},{9,10},{10,1... | collective-permute-start | bytes 1572872 | tf_op jit(solution)/shard_map/ppermute | solution.py:83
  161.7 15.1 %collective-permute-start.4 = (bf16[128,2048]{1,0:T(8,128)(2,1)S(1)}, bf16[128,2048]{1,0:T(8,128)(2,1)S(1)}, u32[]{:S(2)}, u32[]{:S(2)}) collective-permute-start(bf16[128,2048]{1,0:T(8,128)(2,1)S(1)} %add_convert_fusion.4), channel_id=1, source_target_pairs={{0,1},{1,2},{2,3},{3,0},{4,5},{5,6},{6,7},{7,4},{8,9},{9,10},{10,1... | collective-permute-start | bytes 1572872 | tf_op jit(solution)/shard_map/ppermute | solution.py:83
  176.9 14.2 %collective-permute-start.5 = (bf16[128,2048]{1,0:T(8,128)(2,1)S(1)}, bf16[128,2048]{1,0:T(8,128)(2,1)S(1)}, u32[]{:S(2)}, u32[]{:S(2)}) collective-permute-start(bf16[128,2048]{1,0:T(8,128)(2,1)S(1)} %add_convert_fusion.3), channel_id=1, source_target_pairs={{0,1},{1,2},{2,3},{3,0},{4,5},{5,6},{6,7},{7,4},{8,9},{9,10},{10,1... | collective-permute-start | bytes 1572872 | tf_op jit(solution)/shard_map/ppermute | solution.py:83
  195.1 13.4 %collective-permute-start.6 = (bf16[128,2048]{1,0:T(8,128)(2,1)}, bf16[128,2048]{1,0:T(8,128)(2,1)S(1)}, u32[]{:S(2)}, u32[]{:S(2)}) collective-permute-start(bf16[128,2048]{1,0:T(8,128)(2,1)} %get-tuple-element.111), channel_id=1, source_target_pairs={{0,1},{1,2},{2,3},{3,0},{4,5},{5,6},{6,7},{7,4},{8,9},{9,10},{10,1... | collective-permute-start | bytes 1572872 | tf_op jit(solution)/shard_map/ppermute | solution.py:70
  208.4 12.4 %collective-permute-start.7 = (bf16[128,2048]{1,0:T(8,128)(2,1)S(1)}, bf16[128,2048]{1,0:T(8,128)(2,1)S(1)}, u32[]{:S(2)}, u32[]{:S(2)}) collective-permute-start(bf16[128,2048]{1,0:T(8,128)(2,1)S(1)} %collective-permute-done.6), channel_id=1, source_target_pairs={{0,1},{1,2},{2,3},{3,0},{4,5},{5,6},{6,7},{7,4},{8,9},{9,10},{10,1... | collective-permute-start | bytes 1572872 | tf_op jit(solution)/shard_map/ppermute | solution.py:70
  220.8 11.3 %collective-permute-start.8 = (bf16[128,2048]{1,0:T(8,128)(2,1)S(1)}, bf16[128,2048]{1,0:T(8,128)(2,1)S(1)}, u32[]{:S(2)}, u32[]{:S(2)}) collective-permute-start(bf16[128,2048]{1,0:T(8,128)(2,1)S(1)} %collective-permute-done.7), channel_id=1, source_target_pairs={{0,1},{1,2},{2,3},{3,0},{4,5},{5,6},{6,7},{7,4},{8,9},{9,10},{10,1... | collective-permute-start | bytes 1572872 | tf_op jit(solution)/shard_map/ppermute | solution.py:70
  271.5 208.3 %reduce-scatter.5.cloned.1.call-start = ((), (), s32[]{:S(2)}) async-start(), calls=%async_computation.12 | async-start | bytes 7077888 | tf_op jit(solution)/shard_map/reduce_scatter | solution.py:940
  273.9 12.5 %collective-permute-start.9 = (bf16[128,2048]{1,0:T(8,128)(2,1)S(1)}, bf16[128,2048]{1,0:T(8,128)(2,1)S(1)}, u32[]{:S(2)}, u32[]{:S(2)}) collective-permute-start(bf16[128,2048]{1,0:T(8,128)(2,1)S(1)} %get-tuple-element.224), channel_id=1, source_target_pairs={{0,1},{1,2},{2,3},{3,0},{4,5},{5,6},{6,7},{7,4},{8,9},{9,10},{10,1... | collective-permute-start | bytes 1572872 | tf_op jit(solution)/shard_map/ppermute | solution.py:83
  286.5 14.1 %collective-permute-start.10 = (bf16[128,2048]{1,0:T(8,128)(2,1)S(1)}, bf16[128,2048]{1,0:T(8,128)(2,1)S(1)}, u32[]{:S(2)}, u32[]{:S(2)}) collective-permute-start(bf16[128,2048]{1,0:T(8,128)(2,1)S(1)} %add_convert_fusion.2), channel_id=1, source_target_pairs={{0,1},{1,2},{2,3},{3,0},{4,5},{5,6},{6,7},{7,4},{8,9},{9,10},{10,1... | collective-permute-start | bytes 1572872 | tf_op jit(solution)/shard_map/ppermute | solution.py:83
  300.7 11.0 %collective-permute-start.11 = (bf16[128,2048]{1,0:T(8,128)(2,1)S(1)}, bf16[128,2048]{1,0:T(8,128)(2,1)S(1)}, u32[]{:S(2)}, u32[]{:S(2)}) collective-permute-start(bf16[128,2048]{1,0:T(8,128)(2,1)S(1)} %add_convert_fusion.1), channel_id=1, source_target_pairs={{0,1},{1,2},{2,3},{3,0},{4,5},{5,6},{6,7},{7,4},{8,9},{9,10},{10,1... | collective-permute-start | bytes 1572872 | tf_op jit(solution)/shard_map/ppermute | solution.py:83
  316.5 16.8 %collective-permute-start.12 = (bf16[128,2048]{1,0:T(8,128)(2,1)}, bf16[128,2048]{1,0:T(8,128)(2,1)S(1)}, u32[]{:S(2)}, u32[]{:S(2)}) collective-permute-start(bf16[128,2048]{1,0:T(8,128)(2,1)} %get-tuple-element.116), channel_id=1, source_target_pairs={{0,1},{1,2},{2,3},{3,0},{4,5},{5,6},{6,7},{7,4},{8,9},{9,10},{10,1... | collective-permute-start | bytes 1572872 | tf_op jit(solution)/shard_map/ppermute | solution.py:70
  333.2 15.7 %collective-permute-start.13 = (bf16[128,2048]{1,0:T(8,128)(2,1)S(1)}, bf16[128,2048]{1,0:T(8,128)(2,1)S(1)}, u32[]{:S(2)}, u32[]{:S(2)}) collective-permute-start(bf16[128,2048]{1,0:T(8,128)(2,1)S(1)} %collective-permute-done.12), channel_id=1, source_target_pairs={{0,1},{1,2},{2,3},{3,0},{4,5},{5,6},{6,7},{7,4},{8,9},{9,10},{10,1... | collective-permute-start | bytes 1572872 | tf_op jit(solution)/shard_map/ppermute | solution.py:70
  349.0 11.0 %collective-permute-start.14 = (bf16[128,2048]{1,0:T(8,128)(2,1)S(1)}, bf16[128,2048]{1,0:T(8,128)(2,1)S(1)}, u32[]{:S(2)}, u32[]{:S(2)}) collective-permute-start(bf16[128,2048]{1,0:T(8,128)(2,1)S(1)} %collective-permute-done.13), channel_id=1, source_target_pairs={{0,1},{1,2},{2,3},{3,0},{4,5},{5,6},{6,7},{7,4},{8,9},{9,10},{10,1... | collective-permute-start | bytes 1572872 | tf_op jit(solution)/shard_map/ppermute | solution.py:70
  373.4 40.6 %all-to-all-start.2 = ((bf16[4,128,2048]{2,1,0:T(8,128)(2,1)}), bf16[4,128,2048]{2,1,0:T(8,128)(2,1)S(1)}, u32[]{:S(2)}, u32[]{:S(2)}) async-start(bf16[4,128,2048]{2,1,0:T(8,128)(2,1)} %bitcast.81), calls=%async_computation.2 | async-start | bytes 4194304 | tf_op jit(solution)/shard_map/all_to_all | solution.py:62
  417.4 58.6 %all-to-all-start.3 = ((bf16[4,144,2048]{2,1,0:T(8,128)(2,1)}), bf16[4,144,2048]{2,1,0:T(8,128)(2,1)S(1)}, u32[]{:S(2)}, u32[]{:S(2)}) async-start(bf16[4,144,2048]{2,1,0:T(8,128)(2,1)} %get-tuple-element.136), calls=%async_computation.4 | async-start | bytes 4718592 | tf_op jit(solution)/shard_map/all_to_all | solution.py:62
  421.6 33.3 %collective-permute-start.23 = (f32[8,768]{1,0:T(8,128)S(1)}, f32[8,768]{1,0:T(8,128)S(1)}, u32[]{:S(2)}, u32[]{:S(2)}) collective-permute-start(f32[8,768]{1,0:T(8,128)S(1)} %bitcast_reduce_fusion), channel_id=1, source_target_pairs={{0,4},{4,0},{8,12},{12,8},{16,20},{20,16},{24,28},{28,24},{1,5},{5... | collective-permute-start | bytes 73736 | tf_op jit(solution)/shard_map/ppermute | solution.py:120
  425.1 20.2 %collective-permute-start.17 = (bf16[2,4,1,64,384]{4,3,1,2,0:T(8,128)(2,1)S(1)}, bf16[2,4,1,64,384]{4,3,1,2,0:T(8,128)(2,1)S(1)}, u32[]{:S(2)}, u32[]{:S(2)}) collective-permute-start(bf16[2,4,1,64,384]{4,3,1,2,0:T(8,128)(2,1)S(1)} %dynamic-slice_bitcast_fusion.1), channel_id=1, source_target_pairs={{0,16},{4,20},{8,24},{12,28},{16,0},{20,4},{24,8},{28,12},{1,17},{... | collective-permute-start | bytes 1179656 | tf_op jit(solution)/shard_map/ppermute | solution.py:99
  426.9 20.1 %collective-permute-start.16 = (bf16[2,4,1,64,384]{4,3,1,0,2:T(8,128)(2,1)S(1)}, bf16[2,4,1,64,384]{4,3,1,0,2:T(8,128)(2,1)S(1)}, u32[]{:S(2)}, u32[]{:S(2)}) collective-permute-start(bf16[2,4,1,64,384]{4,3,1,0,2:T(8,128)(2,1)S(1)} %dynamic-slice_bitcast_fusion.2), channel_id=1, source_target_pairs={{0,8},{4,12},{8,0},{12,4},{16,24},{20,28},{24,16},{28,20},{1,9},{5... | collective-permute-start | bytes 1179656 | tf_op jit(solution)/shard_map/ppermute | solution.py:99
  479.2 12.1 %collective-permute-start.24 = (bf16[4,171,171]{2,1,0:T(8,128)(2,1)}, bf16[4,171,171]{2,1,0:T(8,128)(2,1)}, u32[]{:S(2)}, u32[]{:S(2)}) collective-permute-start(bf16[4,171,171]{2,1,0:T(8,128)(2,1)} %get-tuple-element.232), channel_id=1, source_target_pairs={{0,4},{4,0},{8,12},{12,8},{16,20},{20,16},{24,28},{28,24},{1,5},{5... | collective-permute-start | bytes 701792 | tf_op jit(solution)/shard_map/ppermute | solution.py:120
  479.2 12.1 %collective-permute-start.25 = (bf16[4,171,171]{2,1,0:T(8,128)(2,1)}, bf16[4,171,171]{2,1,0:T(8,128)(2,1)}, u32[]{:S(2)}, u32[]{:S(2)}) collective-permute-start(bf16[4,171,171]{2,1,0:T(8,128)(2,1)} %get-tuple-element.231), channel_id=1, source_target_pairs={{0,4},{4,0},{8,12},{12,8},{16,20},{20,16},{24,28},{28,24},{1,5},{5... | collective-permute-start | bytes 701792 | tf_op jit(solution)/shard_map/ppermute | solution.py:120
  486.1 35.6 %all-to-all-start.4 = ((bf16[4,3,64,768]{3,2,1,0:T(8,128)(2,1)}), bf16[4,3,64,768]{3,2,1,0:T(8,128)(2,1)S(1)}, u32[]{:S(2)}, u32[]{:S(2)}) async-start(bf16[4,3,64,768]{3,2,1,0:T(8,128)(2,1)} %pad_maximum_fusion.1), calls=%async_computation.6 | async-start | bytes 2359296 | tf_op jit(solution)/shard_map/all_to_all | solution.py:62
  495.3 12.2 %collective-permute-start.22 = (f32[2,2048]{1,0:T(2,128)S(1)}, f32[2,2048]{1,0:T(2,128)S(1)}, u32[]{:S(2)}, u32[]{:S(2)}) collective-permute-start(f32[2,2048]{1,0:T(2,128)S(1)} %add.288), channel_id=1, source_target_pairs={{0,16},{4,20},{8,24},{12,28},{16,0},{20,4},{24,8},{28,12},{1,17},{... | collective-permute-start | bytes 49160 | tf_op jit(solution)/shard_map/ppermute | solution.py:120
  (46 other events, 367.5 us)
Sparse Core Ops, SparseCore 0:
  9.9 48.2 all-gather.4
  60.6 45.5 all-gather.6
  108.6 32.3 all-gather.8
  142.7 72.1 all-gather.10
  271.6 123.3 reduce-scatter.2
  398.2 72.5 reduce-scatter.4

commit v4 on v3

--- a/solution.py
+++ b/solution.py
@@ -12,7 +12,6 @@
 bf16 = jnp.bfloat16
 f32 = jnp.float32
 chunk = 64
-gain_rows = 16
 vmem_limit = 60 * 1024 * 1024
 
 
@@ -100,10 +99,11 @@
     return (keep.astype(f32) + got.astype(f32)).astype(bf16)
 
 
-def sum_columns(total, size):
+def sum_columns(total, size, beside):
     left = list(reversed(bits_of(size)))
     total = total.reshape((2,) * len(left) + total.shape[1:])
     total = halve(total, size, 1, left)
+    beside = [add_from(value, size, 1) for value in beside]
     half, order = total.shape[-1] // 2, bits_of(size)[1:]
     found = []
     for cut, bits in ((total[..., :half], order), (total[..., half:], order[::-1])):
@@ -112,18 +112,13 @@
     for at in range(len(order)):
         for piece in found:
             piece[0] = halve(piece[0], size, piece[1][at], piece[2])
-        found[0][0], found[1][0] = tie(found[0][0], found[1][0])
-    return jnp.concatenate([found[0][0], found[1][0]], axis=-1)
+        beside = [add_from(value, size, order[at]) for value in beside]
+        found[0][0], found[1][0], *beside = tie(found[0][0], found[1][0], *beside)
+    return jnp.concatenate([found[0][0], found[1][0]], axis=-1), beside
 
 
 def add_from(value, size, bit, wire=f32):
     return value + lax.ppermute(value.astype(wire), "rows", flip(size, bit)).astype(f32)
-
-
-def sum_rows(value, size):
-    for bit in bits_of(size):
-        value = add_from(value, size, bit)
-    return value
 
 
 def split_columns_kernel(
@@ -220,12 +215,8 @@
     lax.fori_loop(0, mid_ref.shape[0] // step, rows_step, 0)
 
 
-def token_grad_kernel(gain_ref, tokens_ref, mid_grad_ref, parts_ref, grad_ref, gains_ref):
+def token_grad_kernel(gain_ref, tokens_ref, mid_grad_ref, parts_ref, grad_ref):
     step = 32
-    rows = tokens_ref.shape[0]
-    terms = sum_parts(parts_ref, slice(rows, rows + gain_rows))
-    gains_ref[0:1, :] = terms[0:1, :] + terms[1:2, :]
-    gains_ref[1:2, :] = terms[2:3, :] + terms[3:4, :]
 
     def rows_step(index, carry):
         here = pl.ds(pl.multiple_of(index * step, step), step)
@@ -418,9 +409,9 @@
     normed_any,
     tokens_any,
     late_ref,
-    decay_pre_ref,
-    input_pre_ref,
     sums_ref,
+    gains_ref,
+    gates_ref,
     token_ref,
     signal_ref,
     states_ref,
@@ -438,10 +429,15 @@
     padded,
     grads,
     earlier,
+    decay_pre_ref,
+    input_pre_ref,
     decay_pre_high,
     decay_pre_low,
     input_pre_high,
     input_pre_low,
+    conv_high,
+    conv_low,
+    dense,
     gain_sums,
     arrived,
 ):
@@ -529,6 +525,7 @@
         rows = pl.ds(pl.multiple_of(index * chunk, chunk), chunk)
         decay_pre_high[rows, :], decay_pre_low[rows, :] = split_bf16(decay_pre_ref[rows, :])
         input_pre_high[rows, :], input_pre_low[rows, :] = split_bf16(input_pre_ref[rows, :])
+        conv_high[rows, :], conv_low[rows, :] = split_bf16(conv_ref[rows, :])
         return carry
 
     lax.fori_loop(0, count, split_step, 0)
@@ -578,8 +575,7 @@
         return carry
 
     lax.fori_loop(0, late_ref.shape[0], late_step, 0)
-    parts, rows, model_width = token_ref.shape
-    rows = rows - gain_rows
+    parts, rows, _ = token_ref.shape
     gain_sums[...] = jnp.zeros_like(gain_sums)
 
     def token_step(index, carry):
@@ -590,17 +586,25 @@
         copy.wait()
         values = tokens_ref[...].astype(f32)
         gain_sums[...] += fold8(values * rms_scale(values) * grad)
-        token_ref[index, :rows, :] = grad.astype(bf16)
+        token_ref[index] = grad.astype(bf16)
         return carry
 
     lax.fori_loop(0, parts, token_step, 0)
-    terms = []
-    for total in (gain_sums[...], mlp_ref[...]):
-        terms += split_bf16(total.sum(axis=0, keepdims=True))
-    terms.append(jnp.zeros((gain_rows - len(terms), model_width), bf16))
-    terms = jnp.concatenate([term.astype(f32) for term in terms], axis=0).astype(bf16)
-    for part in range(parts):
-        token_ref[part, rows:, :] = terms
+    heads, block = gates_ref.shape[1:3]
+    for gate, (high, low) in enumerate(
+        ((decay_pre_high, decay_pre_low), (input_pre_high, input_pre_low))
+    ):
+        for start, stop, first, last in tiles:
+            total = None
+            for left, right in ((conv_high, high), (conv_high, low), (conv_low, high)):
+                part = mm(left[:, first:last], right[:, start:stop], ((0,), (0,)))
+                total = part if total is None else total + part
+            dense[first:last, start:stop] = total
+        for head in range(heads):
+            cut = slice(head * block, (head + 1) * block)
+            gates_ref[gate, head] = dense[cut, cut]
+    for row, total in enumerate((gain_sums, mlp_ref)):
+        gains_ref[row : row + 1, :] = total[...].sum(axis=0, keepdims=True)
 
 
 def recur_forward(signal, masks, vectors, weights, tiles):
@@ -619,16 +623,15 @@
     )
 
 
-def mixer_backward(resident, fetched, size, parts, tiles):
+def mixer_backward(resident, fetched, size, parts, tiles, gates_shape):
     length, wide = resident[0].shape
     model_width = fetched[-1].shape[1]
-    whole = ((length, wide), f32)
     outs = [
         ((size, parts, 1, model_width // size // parts, wide), bf16),
-        whole,
-        whole,
         ((64, wide), f32),
-        ((parts, length // parts + gain_rows, model_width), bf16),
+        ((2, model_width), f32),
+        (gates_shape, f32),
+        ((parts, length // parts, model_width), bf16),
     ]
     padded = pltpu.VMEM((length + 8, wide), f32)
     return pl.pallas_call(
@@ -640,8 +643,9 @@
         + [pltpu.VMEM((length // parts, model_width), bf16)]
         + [pltpu.VMEM((length, 2 * wide), bf16)]
         + [padded] * 3
-        + [pltpu.VMEM((length, wide), bf16)] * 4
-        + [pltpu.VMEM((8, model_width), f32), pltpu.SemaphoreType.DMA((len(fetched),))],
+        + [pltpu.VMEM((length, wide), f32)] * 2
+        + [pltpu.VMEM((length, wide), bf16)] * 6
+        + [pltpu.VMEM((wide, wide), f32), pltpu.VMEM((8, model_width), f32), pltpu.SemaphoreType.DMA((len(fetched),))],
         compiler_params=pltpu.CompilerParams(vmem_limit_bytes=vmem_limit),
         name="mixer_backward",
     )(*resident, *fetched)
@@ -670,22 +674,6 @@
         name="column_grads",
     )(*lefts, *rights)
     return total
-
-
-def gate_grads_kernel(tiles, conv_ref, decay_pre_ref, input_pre_ref, gates_ref, dense, pairs):
-    heads, block = gates_ref.shape[1:3]
-    pairs[0], pairs[1] = split_bf16(conv_ref[...])
-    for gate, ref in enumerate((decay_pre_ref, input_pre_ref)):
-        pairs[2], pairs[3] = split_bf16(ref[...])
-        for start, stop, low, high in tiles:
-            total = None
-            for left, right in ((0, 2), (0, 3), (1, 2)):
-                part = mm(pairs[left, :, low:high], pairs[right, :, start:stop], ((0,), (0,)))
-                total = part if total is None else total + part
-            dense[low:high, start:stop] = total
-        for head in range(heads):
-            cut = slice(head * block, (head + 1) * block)
-            gates_ref[gate, head] = dense[cut, cut]
 
 
 def dense_kernel(decay_ref, input_ref, decay_high, decay_low, input_high, input_low):
@@ -940,7 +928,7 @@
     early_sum = lax.psum_scatter(
         early_sum.reshape(-1, wide), "rows", scatter_dimension=0, tiled=True
     ).reshape(early_shape)
-    late_sum, decay_pre_grad, input_pre_grad, sums, token_sent = mixer_backward(
+    late_sum, sums, gain_sums, gate_sums, token_sent = mixer_backward(
         (state_grad, branch_grad, masks, vectors, mlp_gain_part),
         (
             signal,
@@ -956,44 +944,40 @@
         n_rows,
         n_blk,
         tiles,
-    )
-    token_sent, out_parts, unit_sums, late_sum, decay_pre_grad, input_pre_grad, sums = tie(
-        token_sent, out_parts, unit_sums, late_sum, decay_pre_grad, input_pre_grad, sums
+        (2, heads, block, block),
+    )
+    token_sent, out_parts, unit_sums, late_sum, sums, gain_sums, gate_sums = tie(
+        token_sent, out_parts, unit_sums, late_sum, sums, gain_sums, gate_sums
     )
     token_parts = swap_blk(token_sent)
-    late_sum = sum_columns(late_sum, n_rows)
-    (gate_sums,) = local_kernel(
-        functools.partial(gate_grads_kernel, tiles),
-        "gate_grads",
-        (conv_out, decay_pre_grad, input_pre_grad),
-        [((2, heads, block, block), f32)],
-        [pltpu.VMEM((wide, wide), f32), pltpu.VMEM((4,) + signal.shape, bf16)],
-    )
-    gate_sums, token_parts = tie(gate_sums, token_parts)
-    gate_sums = [gate_sums[0], gate_sums[1]]
-    one_way = bits_of(n_rows)
-    other_way = one_way[:1] + one_way[:0:-1]
     vector_sums = sums.reshape(8, 8, wide).sum(axis=1)
-    for at, bit in enumerate(bits_of(n_rows)):
-        for number, order in enumerate((one_way, other_way)):
-            gate_sums[number] = add_from(gate_sums[number], n_rows, order[at], bf16)
-        vector_sums = add_from(vector_sums, n_rows, bit)
-        vector_sums, *gate_sums = tie(vector_sums, *gate_sums)
-    token_parts, early_sum, late_sum = tie(token_parts, early_sum, late_sum)
+    late_sum, (vector_sums, gain_sums) = sum_columns(late_sum, n_rows, [vector_sums, gain_sums])
+    column_sums = jnp.concatenate([early_sum, late_sum], axis=1)
+    gate_sums = [add_from(gate_sums[number], n_rows, 1, bf16) for number in range(2)]
+    *gate_sums, token_parts, column_sums, gain_sums = tie(
+        *gate_sums, token_parts, column_sums, gain_sums
+    )
+    one_way = bits_of(n_rows)[1:]
+    over_blk = bits_of(n_blk)
+    for at in range(max(len(one_way), len(over_blk))):
+        if at < len(one_way):
+            for number, order in enumerate((one_way, one_way[::-1])):
+                gate_sums[number] = add_from(gate_sums[number], n_rows, order[at], bf16)
+        if at < len(over_blk):
+            moved = lax.ppermute(gain_sums, "blk", flip(n_blk, over_blk[at]))
+            gain_sums = gain_sums + moved
+        *gate_sums, gain_sums = tie(*gate_sums, gain_sums)
     vector_sums = vector_sums[:, :width]
-    token_grad, gain_sums = local_kernel(
+    (token_grad,) = local_kernel(
         token_grad_kernel,
         "token_grad",
         (mixer_gains, own_tokens, mid_grad, token_parts),
-        [(square, f32), ((2, model_width), f32)],
-    )
-    gain_sums = sum_rows(gain_sums, n_rows)
-
-    column_sums = swap_blk(jnp.concatenate([early_sum, late_sum], axis=1))
+        [(square, f32)],
+    )
     output_weight_grad, branch_weight_grad, input_weight_grad = local_kernel(
         functools.partial(join_columns_kernel, width),
         "join_columns",
-        (column_sums,),
+        (swap_blk(column_sums),),
         [((shard, n_blk * width), f32)] * 3,
     )
     block_out = (residual_mid + out_parts.astype(f32).sum(axis=0)).astype(bf16)

time: 542 us -> 532 us (0.982)
  waiting for transfers between devices: 281 us -> 272 us
  Pallas kernels: 132 us -> 126 us
    all_to_all x5, waiting for transfers between devices: 34.8 us -> 25.4 us  [swap_blk(): return lax.all_to_all(parts, 'blk', split_axis=0, concat_axis=0, tiled=True)]
    ppermute x5, waiting for transfers between devices: 25.2 us -> 16.5 us  [halve(): got = lax.ppermute(away, 'rows', flip(size, bit))]
    reduce_scatter x1, waiting for transfers between devices: 0.02 us -> 6.67 us  [body(): lax.psum_scatter(early_sum.reshape(-1, wide), 'rows', scatter_dimension=0...]
    pallas_call x9 -> x8, Pallas kernels: 51 us -> 44.7 us  [local_kernel(): pl.pallas_call(kernel, out_shape=[jax.ShapeDtypeStruct(shape, kind) for s...]
    ppermute x0 -> x2, waiting for transfers between devices: none -> 5.94 us  [body(): moved = lax.ppermute(gain_sums, 'blk', flip(n_blk, over_blk[at]))]
    unnamed x74 -> x68, local copies, waits for them, and re-layouts: 12.5 us -> 12.5 us
  transfers between devices with their start and end apart: 43 -> 45, of which waited for: 28 -> 32; matrix products, arithmetic and copies ran while one was open for 11% -> 12% of each run, Pallas kernels for 17% -> 16%
where the time goes in v4:
time: 532 us; the launch traced here: 523 us
  waiting for transfers between devices  272 us (51%)
  Pallas kernels  126 us (24%)
  starting transfers between devices  42.9 us (8%)
  local copies, waits for them, and re-layouts  30.7 us (6%)
  other arithmetic  20.6 us (4%)
  matrix products  16 us (3%)
  between operations  15.4 us (3%)
    ppermute x9, waiting for transfers between devices, ring_blk(): lax.ppermute(part, 'blk', [(place, (place + 1) % size) for place in range...  111 us
    ppermute x6, waiting for transfers between devices, ring_sum(): lax.ppermute(total, 'blk', [(place, (place + 1) % size) for place in rang...  80.2 us
    pallas_call x8, Pallas kernels, local_kernel(): pl.pallas_call(kernel, out_shape=[jax.ShapeDtypeStruct(shape, kind) for s...  44.7 us
    pallas_call x1, Pallas kernels, mlp(): pl.pallas_call(mlp_kernel, grid=(total // tile,), out_shape=[whole, whole...  37.9 us
    pallas_call x1, Pallas kernels, mixer_backward(): pl.pallas_call(functools.partial(mixer_backward_kernel, tiles), out_shape...  33.5 us
    all_to_all x5, waiting for transfers between devices, swap_blk(): return lax.all_to_all(parts, 'blk', split_axis=0, concat_axis=0, tiled=True)  25.4 us
    all_to_all x5, starting transfers between devices, swap_blk(): return lax.all_to_all(parts, 'blk', split_axis=0, concat_axis=0, tiled=True)  22.9 us
    ppermute x5, waiting for transfers between devices, halve(): got = lax.ppermute(away, 'rows', flip(size, bit))  16.5 us
  transfers between devices with their start and end apart: 45, of which 32 were waited for; matrix products, arithmetic and copies ran while one was open for 12% of the time, Pallas kernels for 16%

profile of v4, /device:TPU:0, one launch (start us, length us, event | category | flops | bytes accessed | tf_op | source)
XLA Modules:
  0.0 523.1 jit_solution(5603723599648612071)
XLA Ops:
  13.3 6.3 %all-to-all-start = ((bf16[4,64,2304]{2,1,0:T(8,128)(2,1)}), bf16[4,64,2304]{2,1,0:T(8,128)(2,1)S(1)}, u32[]{:S(2)}, u32[]{:S(2)}) async-start(bf16[4,64,2304]{2,1,0:T(8,128)(2,1)} %split_columns.1), calls=%async_computation | async-start | bytes 2359296 | tf_op jit(solution)/shard_map/all_to_all | solution.py:61
  22.8 4.3 dense_gates.1
  28.4 19.8 %all-to-all-done = bf16[4,64,2304]{2,1,0:T(8,128)(2,1)S(1)} async-done(((bf16[4,64,2304]{2,1,0:T(8,128)(2,1)}), bf16[4,64,2304]{2,1,0:T(8,128)(2,1)S(1)}, u32[]{:S(2)}, u32[]{:S(2)}) %all-to-all-start) | async-done | bytes 1179680 | tf_op jit(solution)/shard_map/all_to_all | solution.py:61
  51.7 14.7 %collective-permute-done = bf16[128,2048]{1,0:T(8,128)(2,1)S(1)} collective-permute-done((bf16[128,2048]{1,0:T(8,128)(2,1)S(1)}, bf16[128,2048]{1,0:T(8,128)(2,1)S(1)}, u32[]{:S(2)}, u32[]{:S(2)}) %collective-permute-start) | collective-permute-done | bytes 524320 | tf_op jit(solution)/shard_map/ppermute | solution.py:69
  66.4 13.9 %collective-permute-done.1 = bf16[128,2048]{1,0:T(8,128)(2,1)} collective-permute-done((bf16[128,2048]{1,0:T(8,128)(2,1)S(1)}, bf16[128,2048]{1,0:T(8,128)(2,1)}, u32[]{:S(2)}, u32[]{:S(2)}) %collective-permute-start.1) | collective-permute-done | bytes 524320 | tf_op jit(solution)/shard_map/ppermute | solution.py:69
  81.7 11.6 %collective-permute-done.2 = bf16[128,2048]{1,0:T(8,128)(2,1)S(1)} collective-permute-done((bf16[128,2048]{1,0:T(8,128)(2,1)}, bf16[128,2048]{1,0:T(8,128)(2,1)S(1)}, u32[]{:S(2)}, u32[]{:S(2)}) %collective-permute-start.2) | collective-permute-done | bytes 524320 | tf_op jit(solution)/shard_map/ppermute | solution.py:69
  94.7 4.5 all-to-all-start.1
  101.6 4.6 all-gather.7.cloned.1.call-done.columns_ref.both_any
  106.2 8.9 %mixer_in.1 = (bf16[512,2048]{1,0:T(8,128)(2,1)}, bf16[512,768]{1,0:T(8,128)(2,1)}, f32[512,768]{1,0:T(8,128)}, f32[2,2048]{1,0:T(2,128)}) custom-call(bf16[512,2048]{1,0:T(8,128)(2,1)} %copy-done, bf16[2048,1536]{1,0:T(8,128)(2,1)} %all-gather.7.cloned.1.call-done.columns_ref.both_any), custom_call_target="tpu_custom_call" | custom-call | tf_op jit(solution)/shard_map/mixer_in/pallas_call | solution.py:236
  115.1 14.9 %recur_forward.1 = (f32[512,768]{1,0:T(8,128)}, bf16[512,768]{1,0:T(8,128)(2,1)}, f32[512,768]{1,0:T(8,128)}, f32[512,768]{1,0:T(8,128)}, f32[512,768]{1,0:T(8,128)}) custom-call(bf16[512,768]{1,0:T(8,128)(2,1)} %get-tuple-element.101.signal_ref.signal_any, f32[520,8]{1,0:T(8,128)} %pad.12.masks_ref, f32[8,768]{1,0:T(8,128)} %pad.13.vectors_ref, ...), custom_call_target="tpu_custom_call" | custom-call | tf_op jit(solution)/shard_map/recur_forward/pallas_call | solution.py:236
  131.8 9.2 %all-gather.9.cloned.1.call-done = bf16[2048,768]{1,0:T(8,128)(2,1)} async-done(((bf16[256,768]{1,0:T(8,128)(2,1)}), bf16[2048,768]{1,0:T(8,128)(2,1)}) %all-gather.9.cloned.1.call-update) | async-done | bytes 3145744 | tf_op jit(solution)/shard_map/all_gather | solution.py:846
  147.1 14.4 %collective-permute-done.3 = bf16[128,2048]{1,0:T(8,128)(2,1)S(1)} collective-permute-done((bf16[128,2048]{1,0:T(8,128)(2,1)S(1)}, bf16[128,2048]{1,0:T(8,128)(2,1)S(1)}, u32[]{:S(2)}, u32[]{:S(2)}) %collective-permute-start.3) | collective-permute-done | bytes 524320 | tf_op jit(solution)/shard_map/ppermute | solution.py:82
  161.7 15.0 %collective-permute-done.4 = bf16[128,2048]{1,0:T(8,128)(2,1)S(1)} collective-permute-done((bf16[128,2048]{1,0:T(8,128)(2,1)S(1)}, bf16[128,2048]{1,0:T(8,128)(2,1)S(1)}, u32[]{:S(2)}, u32[]{:S(2)}) %collective-permute-start.4) | collective-permute-done | bytes 524320 | tf_op jit(solution)/shard_map/ppermute | solution.py:82
  177.6 13.5 %collective-permute-done.5.one_ref = bf16[128,2048]{1,0:T(8,128)(2,1)S(1)} collective-permute-done((bf16[128,2048]{1,0:T(8,128)(2,1)S(1)}, bf16[128,2048]{1,0:T(8,128)(2,1)S(1)}, u32[]{:S(2)}, u32[]{:S(2)}) %collective-permute-start.5) | collective-permute-done | bytes 524320 | tf_op jit(solution)/shard_map/ppermute | solution.py:82
  195.0 13.4 %collective-permute-done.6 = bf16[128,2048]{1,0:T(8,128)(2,1)S(1)} collective-permute-done((bf16[128,2048]{1,0:T(8,128)(2,1)}, bf16[128,2048]{1,0:T(8,128)(2,1)S(1)}, u32[]{:S(2)}, u32[]{:S(2)}) %collective-permute-start.6) | collective-permute-done | bytes 524320 | tf_op jit(solution)/shard_map/ppermute | solution.py:69
  208.6 8.6 %fusion.26.hidden_grad_ref = f32[512,1536]{1,0:T(8,128)} fusion(bf16[512,2048]{1,0:T(8,128)(2,1)} %bitcast.10.cotangent_ref, bf16[1536,2048]{1,0:T(8,128)(2,1)} %all-gather.5.cloned.1.call-done.down_ref), kind=kOutput, calls=%fused_computation.96 | convolution fusion | flops 3221225472 | bytes 11534336 | tf_op jit(solution)/shard_map/dot_general | solution.py:36
  221.2 10.9 %collective-permute-done.8 = bf16[128,2048]{1,0:T(8,128)(2,1)S(1)} collective-permute-done((bf16[128,2048]{1,0:T(8,128)(2,1)S(1)}, bf16[128,2048]{1,0:T(8,128)(2,1)S(1)}, u32[]{:S(2)}, u32[]{:S(2)}) %collective-permute-start.8) | collective-permute-done | bytes 524320 | tf_op jit(solution)/shard_map/ppermute | solution.py:69
  233.5 37.9 %mlp.1 = (bf16[512,2048]{1,0:T(8,128)(2,1)}, bf16[512,2048]{1,0:T(8,128)(2,1)}, bf16[8,3,192,2048]{3,2,1,0:T(8,128)(2,1)}) custom-call(bf16[512,2048]{1,0:T(8,128)(2,1)} %copy-done.1, bf16[512,2048]{1,0:T(8,128)(2,1)} %bitcast.10.cotangent_ref, f32[512,1536]{1,0:T(8,128)} %fusion.26.hidden_grad_ref, bf16[8,2,192,2048]{3,2,1,0:T(8,128)(2,1)} %bitcast.67, ...), custom_call_target="tpu_custom_call" | custom-call | tf_op jit(solution)/shard_map/mlp/pallas_call | solution.py:775
  273.9 12.5 %collective-permute-done.9 = bf16[128,2048]{1,0:T(8,128)(2,1)S(1)} collective-permute-done((bf16[128,2048]{1,0:T(8,128)(2,1)S(1)}, bf16[128,2048]{1,0:T(8,128)(2,1)S(1)}, u32[]{:S(2)}, u32[]{:S(2)}) %collective-permute-start.9) | collective-permute-done | bytes 524320 | tf_op jit(solution)/shard_map/ppermute | solution.py:82
  286.8 13.8 %collective-permute-done.10 = bf16[128,2048]{1,0:T(8,128)(2,1)S(1)} collective-permute-done((bf16[128,2048]{1,0:T(8,128)(2,1)S(1)}, bf16[128,2048]{1,0:T(8,128)(2,1)S(1)}, u32[]{:S(2)}, u32[]{:S(2)}) %collective-permute-start.10) | collective-permute-done | bytes 524320 | tf_op jit(solution)/shard_map/ppermute | solution.py:82
  300.8 11.0 %collective-permute-done.11.one_ref = bf16[128,2048]{1,0:T(8,128)(2,1)S(1)} collective-permute-done((bf16[128,2048]{1,0:T(8,128)(2,1)S(1)}, bf16[128,2048]{1,0:T(8,128)(2,1)S(1)}, u32[]{:S(2)}, u32[]{:S(2)}) %collective-permute-start.11) | collective-permute-done | bytes 524320 | tf_op jit(solution)/shard_map/ppermute | solution.py:82
  316.5 16.8 %collective-permute-done.12 = bf16[128,2048]{1,0:T(8,128)(2,1)S(1)} collective-permute-done((bf16[128,2048]{1,0:T(8,128)(2,1)}, bf16[128,2048]{1,0:T(8,128)(2,1)S(1)}, u32[]{:S(2)}, u32[]{:S(2)}) %collective-permute-start.12) | collective-permute-done | bytes 524320 | tf_op jit(solution)/shard_map/ppermute | solution.py:69
  333.3 15.7 %collective-permute-done.13 = bf16[128,2048]{1,0:T(8,128)(2,1)S(1)} collective-permute-done((bf16[128,2048]{1,0:T(8,128)(2,1)S(1)}, bf16[128,2048]{1,0:T(8,128)(2,1)S(1)}, u32[]{:S(2)}, u32[]{:S(2)}) %collective-permute-start.13) | collective-permute-done | bytes 524320 | tf_op jit(solution)/shard_map/ppermute | solution.py:69
  349.5 10.5 %collective-permute-done.14 = bf16[128,2048]{1,0:T(8,128)(2,1)S(1)} collective-permute-done((bf16[128,2048]{1,0:T(8,128)(2,1)S(1)}, bf16[128,2048]{1,0:T(8,128)(2,1)S(1)}, u32[]{:S(2)}, u32[]{:S(2)}) %collective-permute-start.14) | collective-permute-done | bytes 524320 | tf_op jit(solution)/shard_map/ppermute | solution.py:69
  363.9 9.6 %column_grads.1 = bf16[8,4,2,64,768]{4,3,2,1,0:T(8,128)(2,1)} custom-call(bf16[512,2048]{1,0:T(8,128)(2,1)} %copy-done.2, bf16[512,2048]{1,0:T(8,128)(2,1)} %get-tuple-element.123.normed_any.refs_1_, bf16[512,768]{1,0:T(8,128)(2,1)} %copy-done.7, bf16[512,768]{1,0:T(8,128)(2,1)} %get-tuple-element.216.branch_grad_ref.refs_3_), custom_call_target="tpu_custom_call" | custom-call | tf_op jit(solution)/shard_map/column_grads/pallas_call | solution.py:666
  377.2 33.5 %mixer_backward.1 = (bf16[8,4,1,64,768]{4,3,2,1,0:T(8,128)(2,1)}, f32[64,768]{1,0:T(8,128)}, f32[2,2048]{1,0:T(2,128)}, f32[2,4,171,171]{3,2,1,0:T(8,128)}, bf16[4,128,2048]{2,1,0:T(8,128)(2,1)}) custom-call(bf16[512,768]{1,0:T(8,128)(2,1)} %get-tuple-element.217.state_grad_ref, bf16[512,768]{1,0:T(8,128)(2,1)} %get-tuple-element.216.branch_grad_ref.refs_3_, ...), custom_call_target="tpu_custom_call" | custom-call | tf_op jit(solution)/shard_map/mixer_backward/pallas_call | solution.py:637
  420.3 4.9 all-to-all-start.3
  439.2 8.8 %collective-permute-done.19 = bf16[2,4,1,64,384]{4,3,1,2,0:T(8,128)(2,1)S(1)} collective-permute-done((bf16[2,4,1,64,384]{4,3,1,2,0:T(8,128)(2,1)S(1)}, bf16[2,4,1,64,384]{4,3,1,2,0:T(8,128)(2,1)S(1)}, u32[]{:S(2)}, u32[]{:S(2)}) %collective-permute-start.19) | collective-permute-done | bytes 393248 | tf_op jit(solution)/shard_map/ppermute | solution.py:98
  457.2 5.3 %collective-permute-done.24 = bf16[4,1,64,384]{3,2,0,1:T(8,128)(2,1)S(1)} collective-permute-done((bf16[4,1,64,384]{3,2,0,1:T(8,128)(2,1)S(1)}, bf16[4,1,64,384]{3,2,0,1:T(8,128)(2,1)S(1)}, u32[]{:S(2)}, u32[]{:S(2)}) %collective-permute-start.24) | collective-permute-done | bytes 196640 | tf_op jit(solution)/shard_map/ppermute | solution.py:98
  462.6 6.7 %reduce-scatter.5.cloned.1.call-done = bf16[512,768]{1,0:T(8,128)(2,1)} async-done(((bf16[4096,768]{1,0:T(8,128)(2,1)}), bf16[512,768]{1,0:T(8,128)(2,1)}) %reduce-scatter.5.cloned.1.call-update) | async-done | bytes 786448 | tf_op jit(solution)/shard_map/reduce_scatter | solution.py:928
  484.6 6.0 %collective-permute-done.28 = bf16[4,171,171]{2,1,0:T(8,128)(2,1)S(1)} collective-permute-done((bf16[4,171,171]{2,1,0:T(8,128)(2,1)S(1)}, bf16[4,171,171]{2,1,0:T(8,128)(2,1)S(1)}, u32[]{:S(2)}, u32[]{:S(2)}) %collective-permute-start.28) | collective-permute-done | bytes 233960 | tf_op jit(solution)/shard_map/ppermute | solution.py:121
  501.4 5.9 %collective-permute-done.33 = f32[2,2048]{1,0:T(2,128)S(1)} collective-permute-done((f32[2,2048]{1,0:T(2,128)S(1)}, f32[2,2048]{1,0:T(2,128)S(1)}, u32[]{:S(2)}, u32[]{:S(2)}) %collective-permute-start.33) | collective-permute-done | bytes 16416 | tf_op jit(solution)/shard_map/ppermute | solution.py:967
  (233 shorter events, 120.4 us)
Async XLA Ops:
  7.2 59.2 %all-gather.5.cloned.1.call-start = ((), (), s32[]{:S(2)}) async-start(), calls=%async_computation.7 | async-start | bytes 7077888 | tf_op jit(solution)/shard_map/all_gather | solution.py:837
  13.3 34.9 %all-to-all-start = ((bf16[4,64,2304]{2,1,0:T(8,128)(2,1)}), bf16[4,64,2304]{2,1,0:T(8,128)(2,1)S(1)}, u32[]{:S(2)}, u32[]{:S(2)}) async-start(bf16[4,64,2304]{2,1,0:T(8,128)(2,1)} %split_columns.1), calls=%async_computation | async-start | bytes 2359296 | tf_op jit(solution)/shard_map/all_to_all | solution.py:61
  19.6 86.5 %all-gather.7.cloned.1.call-start = ((), (), s32[]{:S(2)}) async-start(), calls=%async_computation.8 | async-start | bytes 7077888 | tf_op jit(solution)/shard_map/all_gather | solution.py:845
  50.7 90.3 %all-gather.9.cloned.1.call-start = ((), (), s32[]{:S(2)}) async-start(), calls=%async_computation.9 | async-start | bytes 3538944 | tf_op jit(solution)/shard_map/all_gather | solution.py:846
  51.6 180.6 %all-gather.11.cloned.1.call-start = ((), (), s32[]{:S(2)}) async-start(), calls=%async_computation.10 | async-start | bytes 14155776 | tf_op jit(solution)/shard_map/all_gather | solution.py:850
  51.6 14.7 %collective-permute-start = (bf16[128,2048]{1,0:T(8,128)(2,1)S(1)}, bf16[128,2048]{1,0:T(8,128)(2,1)S(1)}, u32[]{:S(2)}, u32[]{:S(2)}) collective-permute-start(bf16[128,2048]{1,0:T(8,128)(2,1)S(1)} %bitcast.75), channel_id=1, source_target_pairs={{0,1},{1,2},{2,3},{3,0},{4,5},{5,6},{6,7},{7,4},{8,9},{9,10},{10,1... | collective-permute-start | bytes 1572872 | tf_op jit(solution)/shard_map/ppermute | solution.py:69
  66.4 13.9 %collective-permute-start.1 = (bf16[128,2048]{1,0:T(8,128)(2,1)S(1)}, bf16[128,2048]{1,0:T(8,128)(2,1)}, u32[]{:S(2)}, u32[]{:S(2)}) collective-permute-start(bf16[128,2048]{1,0:T(8,128)(2,1)S(1)} %collective-permute-done), channel_id=1, source_target_pairs={{0,1},{1,2},{2,3},{3,0},{4,5},{5,6},{6,7},{7,4},{8,9},{9,10},{10,1... | collective-permute-start | bytes 1572872 | tf_op jit(solution)/shard_map/ppermute | solution.py:69
  80.3 13.1 %collective-permute-start.2 = (bf16[128,2048]{1,0:T(8,128)(2,1)}, bf16[128,2048]{1,0:T(8,128)(2,1)S(1)}, u32[]{:S(2)}, u32[]{:S(2)}) collective-permute-start(bf16[128,2048]{1,0:T(8,128)(2,1)} %collective-permute-done.1), channel_id=1, source_target_pairs={{0,1},{1,2},{2,3},{3,0},{4,5},{5,6},{6,7},{7,4},{8,9},{9,10},{10,1... | collective-permute-start | bytes 1572872 | tf_op jit(solution)/shard_map/ppermute | solution.py:69
  94.7 50.1 %all-to-all-start.1 = ((bf16[4,128,2048]{2,1,0:T(8,128)(2,1)}), bf16[4,128,2048]{2,1,0:T(8,128)(2,1)}, u32[]{:S(2)}, u32[]{:S(2)}) async-start(bf16[4,128,2048]{2,1,0:T(8,128)(2,1)} %broadcast_in_dim.32), calls=%async_computation.1 | async-start | bytes 4194304 | tf_op jit(solution)/shard_map/all_to_all | solution.py:61
  99.2 314.8 %reduce-scatter.3.cloned.1.call-start = ((), (), s32[]{:S(2)}) async-start(), calls=%async_computation.11 | async-start | bytes 21233664 | tf_op jit(solution)/shard_map/reduce_scatter | solution.py:905
  145.6 15.9 %collective-permute-start.3 = (bf16[128,2048]{1,0:T(8,128)(2,1)S(1)}, bf16[128,2048]{1,0:T(8,128)(2,1)S(1)}, u32[]{:S(2)}, u32[]{:S(2)}) collective-permute-start(bf16[128,2048]{1,0:T(8,128)(2,1)S(1)} %get-tuple-element.224), channel_id=1, source_target_pairs={{0,1},{1,2},{2,3},{3,0},{4,5},{5,6},{6,7},{7,4},{8,9},{9,10},{10,1... | collective-permute-start | bytes 1572872 | tf_op jit(solution)/shard_map/ppermute | solution.py:82
  161.7 15.1 %collective-permute-start.4 = (bf16[128,2048]{1,0:T(8,128)(2,1)S(1)}, bf16[128,2048]{1,0:T(8,128)(2,1)S(1)}, u32[]{:S(2)}, u32[]{:S(2)}) collective-permute-start(bf16[128,2048]{1,0:T(8,128)(2,1)S(1)} %add_convert_fusion.4), channel_id=1, source_target_pairs={{0,1},{1,2},{2,3},{3,0},{4,5},{5,6},{6,7},{7,4},{8,9},{9,10},{10,1... | collective-permute-start | bytes 1572872 | tf_op jit(solution)/shard_map/ppermute | solution.py:82
  176.9 14.2 %collective-permute-start.5 = (bf16[128,2048]{1,0:T(8,128)(2,1)S(1)}, bf16[128,2048]{1,0:T(8,128)(2,1)S(1)}, u32[]{:S(2)}, u32[]{:S(2)}) collective-permute-start(bf16[128,2048]{1,0:T(8,128)(2,1)S(1)} %add_convert_fusion.3), channel_id=1, source_target_pairs={{0,1},{1,2},{2,3},{3,0},{4,5},{5,6},{6,7},{7,4},{8,9},{9,10},{10,1... | collective-permute-start | bytes 1572872 | tf_op jit(solution)/shard_map/ppermute | solution.py:82
  195.0 13.4 %collective-permute-start.6 = (bf16[128,2048]{1,0:T(8,128)(2,1)}, bf16[128,2048]{1,0:T(8,128)(2,1)S(1)}, u32[]{:S(2)}, u32[]{:S(2)}) collective-permute-start(bf16[128,2048]{1,0:T(8,128)(2,1)} %get-tuple-element.110), channel_id=1, source_target_pairs={{0,1},{1,2},{2,3},{3,0},{4,5},{5,6},{6,7},{7,4},{8,9},{9,10},{10,1... | collective-permute-start | bytes 1572872 | tf_op jit(solution)/shard_map/ppermute | solution.py:69
  208.4 12.4 %collective-permute-start.7 = (bf16[128,2048]{1,0:T(8,128)(2,1)S(1)}, bf16[128,2048]{1,0:T(8,128)(2,1)S(1)}, u32[]{:S(2)}, u32[]{:S(2)}) collective-permute-start(bf16[128,2048]{1,0:T(8,128)(2,1)S(1)} %collective-permute-done.6), channel_id=1, source_target_pairs={{0,1},{1,2},{2,3},{3,0},{4,5},{5,6},{6,7},{7,4},{8,9},{9,10},{10,1... | collective-permute-start | bytes 1572872 | tf_op jit(solution)/shard_map/ppermute | solution.py:69
  220.8 11.3 %collective-permute-start.8 = (bf16[128,2048]{1,0:T(8,128)(2,1)S(1)}, bf16[128,2048]{1,0:T(8,128)(2,1)S(1)}, u32[]{:S(2)}, u32[]{:S(2)}) collective-permute-start(bf16[128,2048]{1,0:T(8,128)(2,1)S(1)} %collective-permute-done.7), channel_id=1, source_target_pairs={{0,1},{1,2},{2,3},{3,0},{4,5},{5,6},{6,7},{7,4},{8,9},{9,10},{10,1... | collective-permute-start | bytes 1572872 | tf_op jit(solution)/shard_map/ppermute | solution.py:69
  271.5 197.8 %reduce-scatter.5.cloned.1.call-start = ((), (), s32[]{:S(2)}) async-start(), calls=%async_computation.12 | async-start | bytes 7077888 | tf_op jit(solution)/shard_map/reduce_scatter | solution.py:928
  273.9 12.5 %collective-permute-start.9 = (bf16[128,2048]{1,0:T(8,128)(2,1)S(1)}, bf16[128,2048]{1,0:T(8,128)(2,1)S(1)}, u32[]{:S(2)}, u32[]{:S(2)}) collective-permute-start(bf16[128,2048]{1,0:T(8,128)(2,1)S(1)} %get-tuple-element.222), channel_id=1, source_target_pairs={{0,1},{1,2},{2,3},{3,0},{4,5},{5,6},{6,7},{7,4},{8,9},{9,10},{10,1... | collective-permute-start | bytes 1572872 | tf_op jit(solution)/shard_map/ppermute | solution.py:82
  286.6 14.1 %collective-permute-start.10 = (bf16[128,2048]{1,0:T(8,128)(2,1)S(1)}, bf16[128,2048]{1,0:T(8,128)(2,1)S(1)}, u32[]{:S(2)}, u32[]{:S(2)}) collective-permute-start(bf16[128,2048]{1,0:T(8,128)(2,1)S(1)} %add_convert_fusion.2), channel_id=1, source_target_pairs={{0,1},{1,2},{2,3},{3,0},{4,5},{5,6},{6,7},{7,4},{8,9},{9,10},{10,1... | collective-permute-start | bytes 1572872 | tf_op jit(solution)/shard_map/ppermute | solution.py:82
  316.5 16.8 %collective-permute-start.12 = (bf16[128,2048]{1,0:T(8,128)(2,1)}, bf16[128,2048]{1,0:T(8,128)(2,1)S(1)}, u32[]{:S(2)}, u32[]{:S(2)}) collective-permute-start(bf16[128,2048]{1,0:T(8,128)(2,1)} %get-tuple-element.115), channel_id=1, source_target_pairs={{0,1},{1,2},{2,3},{3,0},{4,5},{5,6},{6,7},{7,4},{8,9},{9,10},{10,1... | collective-permute-start | bytes 1572872 | tf_op jit(solution)/shard_map/ppermute | solution.py:69
  333.3 15.7 %collective-permute-start.13 = (bf16[128,2048]{1,0:T(8,128)(2,1)S(1)}, bf16[128,2048]{1,0:T(8,128)(2,1)S(1)}, u32[]{:S(2)}, u32[]{:S(2)}) collective-permute-start(bf16[128,2048]{1,0:T(8,128)(2,1)S(1)} %collective-permute-done.12), channel_id=1, source_target_pairs={{0,1},{1,2},{2,3},{3,0},{4,5},{5,6},{6,7},{7,4},{8,9},{9,10},{10,1... | collective-permute-start | bytes 1572872 | tf_op jit(solution)/shard_map/ppermute | solution.py:69
  373.5 40.5 %all-to-all-start.2 = ((bf16[4,128,2048]{2,1,0:T(8,128)(2,1)}), bf16[4,128,2048]{2,1,0:T(8,128)(2,1)S(1)}, u32[]{:S(2)}, u32[]{:S(2)}) async-start(bf16[4,128,2048]{2,1,0:T(8,128)(2,1)} %bitcast.81), calls=%async_computation.2 | async-start | bytes 4194304 | tf_op jit(solution)/shard_map/all_to_all | solution.py:61
  416.7 14.8 %collective-permute-start.22 = (f32[2,2048]{1,0:T(2,128)S(1)}, f32[2,2048]{1,0:T(2,128)}, u32[]{:S(2)}, u32[]{:S(2)}) collective-permute-start(f32[2,2048]{1,0:T(2,128)S(1)} %copy-done.23), channel_id=1, source_target_pairs={{0,4},{4,0},{8,12},{12,8},{16,20},{20,16},{24,28},{28,24},{1,5},{5... | collective-permute-start | bytes 49160 | tf_op jit(solution)/shard_map/ppermute | solution.py:121
  418.8 15.0 %collective-permute-start.20 = (f32[8,768]{1,0:T(8,128)}, f32[8,768]{1,0:T(8,128)}, u32[]{:S(2)}, u32[]{:S(2)}) collective-permute-start(f32[8,768]{1,0:T(8,128)} %bitcast_reduce_fusion), channel_id=1, source_target_pairs={{0,4},{4,0},{8,12},{12,8},{16,20},{20,16},{24,28},{28,24},{1,5},{5... | collective-permute-start | bytes 73736 | tf_op jit(solution)/shard_map/ppermute | solution.py:121
  419.8 31.1 %collective-permute-start.15 = (bf16[4,171,171]{2,1,0:T(8,128)(2,1)}, bf16[4,171,171]{2,1,0:T(8,128)(2,1)S(1)}, u32[]{:S(2)}, u32[]{:S(2)}) collective-permute-start(bf16[4,171,171]{2,1,0:T(8,128)(2,1)} %get-tuple-element.230), channel_id=1, source_target_pairs={{0,4},{4,0},{8,12},{12,8},{16,20},{20,16},{24,28},{28,24},{1,5},{5... | collective-permute-start | bytes 701792 | tf_op jit(solution)/shard_map/ppermute | solution.py:121
  420.3 53.6 %all-to-all-start.3 = ((bf16[4,128,2048]{2,1,0:T(8,128)(2,1)}), bf16[4,128,2048]{2,1,0:T(8,128)(2,1)}, u32[]{:S(2)}, u32[]{:S(2)}) async-start(bf16[4,128,2048]{2,1,0:T(8,128)(2,1)} %get-tuple-element.134), calls=%async_computation.4 | async-start | bytes 4194304 | tf_op jit(solution)/shard_map/all_to_all | solution.py:61
  427.9 20.1 %collective-permute-start.19 = (bf16[2,4,1,64,384]{4,3,1,2,0:T(8,128)(2,1)S(1)}, bf16[2,4,1,64,384]{4,3,1,2,0:T(8,128)(2,1)S(1)}, u32[]{:S(2)}, u32[]{:S(2)}) collective-permute-start(bf16[2,4,1,64,384]{4,3,1,2,0:T(8,128)(2,1)S(1)} %dynamic-slice_bitcast_fusion.1), channel_id=1, source_target_pairs={{0,16},{4,20},{8,24},{12,28},{16,0},{20,4},{24,8},{28,12},{1,17},{... | collective-permute-start | bytes 1179656 | tf_op jit(solution)/shard_map/ppermute | solution.py:98
  435.3 15.1 %collective-permute-start.18 = (bf16[2,4,1,64,384]{4,3,1,0,2:T(8,128)(2,1)S(1)}, bf16[2,4,1,64,384]{4,3,1,0,2:T(8,128)(2,1)S(1)}, u32[]{:S(2)}, u32[]{:S(2)}) collective-permute-start(bf16[2,4,1,64,384]{4,3,1,0,2:T(8,128)(2,1)S(1)} %dynamic-slice_bitcast_fusion.2), channel_id=1, source_target_pairs={{0,8},{4,12},{8,0},{12,4},{16,24},{20,28},{24,16},{28,20},{1,9},{5... | collective-permute-start | bytes 1179656 | tf_op jit(solution)/shard_map/ppermute | solution.py:98
  438.1 12.8 %collective-permute-start.16 = (bf16[4,171,171]{2,1,0:T(8,128)(2,1)S(1)}, bf16[4,171,171]{2,1,0:T(8,128)(2,1)S(1)}, u32[]{:S(2)}, u32[]{:S(2)}) collective-permute-start(bf16[4,171,171]{2,1,0:T(8,128)(2,1)S(1)} %copy-done.21), channel_id=1, source_target_pairs={{0,4},{4,0},{8,12},{12,8},{16,20},{20,16},{24,28},{28,24},{1,5},{5... | collective-permute-start | bytes 701792 | tf_op jit(solution)/shard_map/ppermute | solution.py:121
  475.3 36.6 %all-to-all-start.4 = ((bf16[4,3,64,768]{3,2,1,0:T(8,128)(2,1)}), bf16[4,3,64,768]{3,2,1,0:T(8,128)(2,1)S(1)}, u32[]{:S(2)}, u32[]{:S(2)}) async-start(bf16[4,3,64,768]{3,2,1,0:T(8,128)(2,1)} %maximum_maximum_fusion), calls=%async_computation.6 | async-start | bytes 2359296 | tf_op jit(solution)/shard_map/all_to_all | solution.py:61
  490.7 16.7 %collective-permute-start.32 = (bf16[4,171,171]{2,1,0:T(8,128)(2,1)S(1)}, bf16[4,171,171]{2,1,0:T(8,128)(2,1)S(1)}, u32[]{:S(2)}, u32[]{:S(2)}) collective-permute-start(bf16[4,171,171]{2,1,0:T(8,128)(2,1)S(1)} %convert_element_type.278), channel_id=1, source_target_pairs={{0,8},{4,12},{8,0},{12,4},{16,24},{20,28},{24,16},{28,20},{1,9},{5... | collective-permute-start | bytes 701792 | tf_op jit(solution)/shard_map/ppermute | solution.py:121
  492.9 14.5 %collective-permute-start.33 = (f32[2,2048]{1,0:T(2,128)S(1)}, f32[2,2048]{1,0:T(2,128)S(1)}, u32[]{:S(2)}, u32[]{:S(2)}) collective-permute-start(f32[2,2048]{1,0:T(2,128)S(1)} %add.303), channel_id=1, source_target_pairs={{0,2},{1,3},{2,0},{3,1},{4,6},{5,7},{6,4},{7,5},{8,10},{9,11},{10,... | collective-permute-start | bytes 49160 | tf_op jit(solution)/shard_map/ppermute | solution.py:967
  (45 other events, 378.6 us)
Sparse Core Ops, SparseCore 0:
  9.9 48.2 all-gather.4
  60.6 45.5 all-gather.6
  108.6 32.3 all-gather.8
  142.7 72.1 all-gather.10
  271.6 123.3 reduce-scatter.2
  398.3 70.9 reduce-scatter.4

commit v5 on v4

--- a/solution.py
+++ b/solution.py
@@ -74,10 +74,10 @@
     return whole if beside is None else (whole, beside)
 
 
-def ring_sum(partial, size):
+def ring_sum(partial, size, first=None):
     me, rows = lax.axis_index("blk"), partial.shape[0] // size
     pick = lambda place: lax.dynamic_slice_in_dim(partial, place % size * rows, rows, axis=0)
-    total = pick(me - 1 + size)
+    total = pick(me - 1 + size) if first is None else first
     for step in range(1, size):
         total = lax.ppermute(total, "blk", [(place, (place + 1) % size) for place in range(size)])
         if step < size - 1:
@@ -99,10 +99,11 @@
     return (keep.astype(f32) + got.astype(f32)).astype(bf16)
 
 
-def sum_columns(total, size, beside):
-    left = list(reversed(bits_of(size)))
+def sum_columns(away, keep, size, beside):
+    left = list(reversed(bits_of(size)))[:-1]
+    got = lax.ppermute(away, "rows", flip(size, 1))
+    total = (keep.astype(f32) + got.astype(f32)).astype(bf16)
     total = total.reshape((2,) * len(left) + total.shape[1:])
-    total = halve(total, size, 1, left)
     beside = [add_from(value, size, 1) for value in beside]
     half, order = total.shape[-1] // 2, bits_of(size)[1:]
     found = []
@@ -124,15 +125,24 @@
 def split_columns_kernel(
     width, wide, input_ref, branch_ref, output_ref, mixer_ref, mlp_ref, both_ref
 ):
-    parts = both_ref.shape[0]
+    parts, shard, _ = both_ref.shape
     both_ref[...] = jnp.zeros_like(both_ref)
+    turn = lax.broadcasted_iota(jnp.int32, (shard, shard), 0) == lax.broadcasted_iota(
+        jnp.int32, (shard, shard), 1
+    )
+
+    def column(ref):
+        value = jnp.where(turn, ref[...].astype(f32), 0.0)
+        return jnp.sum(value, axis=1, keepdims=True).astype(bf16)
+
+    mixer_column, mlp_column = column(mixer_ref), column(mlp_ref)
     for part in range(parts):
         cut = slice(part * width, (part + 1) * width)
         both_ref[part, :, :width] = input_ref[:, cut]
         both_ref[part, :, wide : wide + width] = branch_ref[:, cut]
         both_ref[part, :, 2 * wide : 2 * wide + width] = output_ref[:, cut]
-        both_ref[part, :, width : width + 1] = mixer_ref[...]
-        both_ref[part, :, width + 1 : width + 2] = mlp_ref[...]
+        both_ref[part, :, width : width + 1] = mixer_column
+        both_ref[part, :, width + 1 : width + 2] = mlp_column
 
 
 def join_columns_kernel(width, parts_ref, *out_refs):
@@ -170,7 +180,7 @@
 
 
 def mid_norm_kernel(gain_ref, tokens_ref, one_ref, two_ref, mid_ref, normed_ref):
-    step = 32
+    step = 128
 
     def rows_step(index, carry):
         here = pl.ds(pl.multiple_of(index * step, step), step)
@@ -198,7 +208,7 @@
 def mid_grad_kernel(
     gain_ref, mid_ref, cotangent_ref, one_ref, two_ref, grad_ref, sent_ref, sums_ref
 ):
-    step = 32
+    step = 128
     sums_ref[...] = jnp.zeros_like(sums_ref)
 
     def rows_step(index, carry):
@@ -391,6 +401,7 @@
 
 def mixer_backward_kernel(
     tiles,
+    core_ref,
     state_grad_ref,
     branch_grad_ref,
     masks_ref,
@@ -408,8 +419,9 @@
     both_any,
     normed_any,
     tokens_any,
-    late_ref,
-    sums_ref,
+    away_ref,
+    keep_ref,
+    totals_ref,
     gains_ref,
     gates_ref,
     token_ref,
@@ -438,6 +450,7 @@
     conv_high,
     conv_low,
     dense,
+    sums_ref,
     gain_sums,
     arrived,
 ):
@@ -566,15 +579,17 @@
     lax.fori_loop(0, count, conv_step, 0)
     copies[9].wait()
     copies[10].wait()
-    each = late_ref.shape[1] * late_ref.shape[3]
+    each = keep_ref.shape[1] * keep_ref.shape[3]
 
     def late_step(index, carry):
-        rows = pl.ds(pl.multiple_of(index * each, each), each)
-        value = mm(normed_ref[:, rows], both_grad_ref[:, :width], ((0,), (0,))).astype(bf16)
-        late_ref[index, :, 0] = value.reshape(late_ref.shape[1], *late_ref.shape[3:])
-        return carry
-
-    lax.fori_loop(0, late_ref.shape[0], late_step, 0)
+        for side, out_ref in enumerate((keep_ref, away_ref)):
+            place = 2 * index + (core_ref[0] ^ side)
+            rows = pl.ds(pl.multiple_of(place * each, each), each)
+            value = mm(normed_ref[:, rows], both_grad_ref[:, :width], ((0,), (0,))).astype(bf16)
+            out_ref[index, :, 0] = value.reshape(out_ref.shape[1], *out_ref.shape[3:])
+        return carry
+
+    lax.fori_loop(0, keep_ref.shape[0], late_step, 0)
     parts, rows, _ = token_ref.shape
     gain_sums[...] = jnp.zeros_like(gain_sums)
 
@@ -603,6 +618,9 @@
         for head in range(heads):
             cut = slice(head * block, (head + 1) * block)
             gates_ref[gate, head] = dense[cut, cut]
+    for row in range(totals_ref.shape[0]):
+        total = sums_ref[8 * row : 8 * row + 8, :].sum(axis=0, keepdims=True)
+        totals_ref[row : row + 1, :] = total
     for row, total in enumerate((gain_sums, mlp_ref)):
         gains_ref[row : row + 1, :] = total[...].sum(axis=0, keepdims=True)
 
@@ -623,12 +641,13 @@
     )
 
 
-def mixer_backward(resident, fetched, size, parts, tiles, gates_shape):
+def mixer_backward(core, resident, fetched, size, parts, tiles, gates_shape):
     length, wide = resident[0].shape
     model_width = fetched[-1].shape[1]
     outs = [
-        ((size, parts, 1, model_width // size // parts, wide), bf16),
-        ((64, wide), f32),
+        ((size // 2, parts, 1, model_width // size // parts, wide), bf16),
+        ((size // 2, parts, 1, model_width // size // parts, wide), bf16),
+        ((8, wide), f32),
         ((2, model_width), f32),
         (gates_shape, f32),
         ((parts, length // parts, model_width), bf16),
@@ -637,7 +656,9 @@
     return pl.pallas_call(
         functools.partial(mixer_backward_kernel, tiles),
         out_shape=[jax.ShapeDtypeStruct(shape, kind) for shape, kind in outs],
-        in_specs=vmem_specs(len(resident)) + [pl.BlockSpec(memory_space=pl.ANY)] * len(fetched),
+        in_specs=[pl.BlockSpec(memory_space=pltpu.SMEM)]
+        + vmem_specs(len(resident))
+        + [pl.BlockSpec(memory_space=pl.ANY)] * len(fetched),
         out_specs=vmem_specs(len(outs)),
         scratch_shapes=[pltpu.VMEM(value.shape, value.dtype) for value in fetched[:-1]]
         + [pltpu.VMEM((length // parts, model_width), bf16)]
@@ -645,28 +666,29 @@
         + [padded] * 3
         + [pltpu.VMEM((length, wide), f32)] * 2
         + [pltpu.VMEM((length, wide), bf16)] * 6
-        + [pltpu.VMEM((wide, wide), f32), pltpu.VMEM((8, model_width), f32), pltpu.SemaphoreType.DMA((len(fetched),))],
+        + [pltpu.VMEM((wide, wide), f32), pltpu.VMEM((64, wide), f32)]
+        + [pltpu.VMEM((8, model_width), f32), pltpu.SemaphoreType.DMA((len(fetched),))],
         compiler_params=pltpu.CompilerParams(vmem_limit_bytes=vmem_limit),
         name="mixer_backward",
-    )(*resident, *fetched)
+    )(core, *resident, *fetched)
 
 
 def column_grads_kernel(count, *refs):
     for number in range(count):
         value = mm(refs[number][...], refs[count + number][...], ((0,), (0,)))
-        value = value.astype(bf16)
-        refs[-1][0, :, number] = value.reshape(refs[-1].shape[1], *refs[-1].shape[3:])
+        shape = refs[-1].shape[:2] + refs[-1].shape[3:]
+        refs[-1][:, :, number] = value.astype(bf16).reshape(shape)
 
 
 def column_grads(lefts, rights, size, parts):
     length, model_width = lefts[0].shape
     wide = rights[0].shape[1]
     each, count = model_width // size, len(lefts)
-    block = (1, parts, count, each // parts, wide)
+    block = (2, parts, count, each // parts, wide)
     total = pl.pallas_call(
         functools.partial(column_grads_kernel, count),
-        grid=(size,),
-        in_specs=[pl.BlockSpec((length, each), lambda i: (0, i))] * count
+        grid=(size // 2,),
+        in_specs=[pl.BlockSpec((length, 2 * each), lambda i: (0, i))] * count
         + [pl.BlockSpec((length, wide), lambda i: (0, 0))] * count,
         out_specs=pl.BlockSpec(block, lambda i: (i, 0, 0, 0, 0)),
         out_shape=jax.ShapeDtypeStruct((size,) + block[1:], bf16),
@@ -691,11 +713,10 @@
 
 def mlp_kernel(
     normed_ref,
-    cotangent_ref,
+    cotangent_any,
     hidden_grad_ref,
-    gate_ref,
-    up_ref,
-    down_ref,
+    first_any,
+    down_any,
     normed_grad_ref,
     out_ref,
     units_any,
@@ -705,18 +726,51 @@
     up_grads,
     hidden_all,
     units,
+    gate_all,
+    up_all,
+    down_all,
+    cotangent_ref,
     sent,
+    arrived,
+    cotangent_arrived,
 ):
     step, steps = pl.program_id(0), pl.num_programs(0)
     length = normed_ref.shape[0]
     group = units.shape[1]
-    gate_units = lambda: gate_ref[...].reshape(down_ref.shape)
-    up_units = lambda: up_ref[...].reshape(down_ref.shape)
+    tile = group * units.shape[2]
+
+    def fetch(at):
+        here = pl.ds(at * group, group)
+        rows = pl.ds(pl.multiple_of(at * tile, tile), tile)
+        return [
+            pltpu.make_async_copy(source, target, arrived.at[number, at])
+            for number, (source, target) in enumerate(
+                (
+                    (first_any.at[here, 0], gate_all.at[here]),
+                    (first_any.at[here, 1], up_all.at[here]),
+                    (down_any.at[rows, :], down_all.at[rows, :]),
+                )
+            )
+        ]
+
+    cotangent_copy = pltpu.make_async_copy(cotangent_any, cotangent_ref, cotangent_arrived)
 
     @pl.when(step == 0)
     def _():
+        for at in range(gate_all.shape[0] // group):
+            for copy in fetch(at):
+                copy.start()
+            if at == 0:
+                cotangent_copy.start()
         normed_total[...] = jnp.zeros_like(normed_total)
         out_total[...] = jnp.zeros_like(out_total)
+
+    mine = pl.ds(step * group, group)
+    gate_units = lambda: gate_all[mine].reshape(tile, gate_all.shape[2])
+    up_units = lambda: up_all[mine].reshape(tile, up_all.shape[2])
+    coming = fetch(step)
+    coming[0].wait()
+    coming[1].wait()
 
     def rows_step(index, carry):
         here = pl.ds(pl.multiple_of(index * 256, 256), 256)
@@ -730,10 +784,22 @@
         normed_total[here, :] += mm(gate_grads[here, :], gate_units(), ((1,), (0,))) + mm(
             up_grads[here, :], up_units(), ((1,), (0,))
         )
-        out_total[here, :] += mm(hidden_all[here, :], down_ref[...], ((1,), (0,)))
         return carry
 
     lax.fori_loop(0, length // 256, rows_step, 0)
+    coming[2].wait()
+
+    def out_step(index, carry):
+        here = pl.ds(pl.multiple_of(index * 256, 256), 256)
+        down = down_all[pl.ds(pl.multiple_of(step * tile, tile), tile), :]
+        out_total[here, :] += mm(hidden_all[here, :], down, ((1,), (0,)))
+        return carry
+
+    lax.fori_loop(0, length // 256, out_step, 0)
+
+    @pl.when(step == 0)
+    def _():
+        cotangent_copy.wait()
 
     def copy_of(number):
         return pltpu.make_async_copy(
@@ -767,10 +833,6 @@
     while group * units % 128 or (group < parts and 2 * group * units * length <= 768 * 512):
         group *= 2
     tile = group * units
-    first = lambda which: pl.BlockSpec(
-        (group, 1, units, model_width), lambda i: (i, which, 0, 0)
-    )
-    weights = [first(0), first(1), pl.BlockSpec((tile, model_width), lambda i: (i, 0))]
     whole = jax.ShapeDtypeStruct((length, model_width), bf16)
     return pl.pallas_call(
         mlp_kernel,
@@ -780,14 +842,20 @@
             whole,
             jax.ShapeDtypeStruct((parts, 3, units, model_width), bf16),
         ],
-        in_specs=vmem_specs(2) + [pl.BlockSpec((length, tile), lambda i: (0, i))] + weights,
+        in_specs=vmem_specs(1)
+        + [pl.BlockSpec(memory_space=pl.ANY), pl.BlockSpec((length, tile), lambda i: (0, i))]
+        + [pl.BlockSpec(memory_space=pl.ANY)] * 2,
         out_specs=vmem_specs(2) + [pl.BlockSpec(memory_space=pl.ANY)],
         scratch_shapes=[pltpu.VMEM((length, model_width), f32)] * 2
         + [pltpu.VMEM((length, tile), bf16)] * 3
-        + [pltpu.VMEM((3, group, units, model_width), bf16), pltpu.SemaphoreType.DMA((3,))],
+        + [pltpu.VMEM((3, group, units, model_width), bf16)]
+        + [pltpu.VMEM((parts, units, model_width), bf16)] * 2
+        + [pltpu.VMEM((total, model_width), bf16), pltpu.VMEM((length, model_width), bf16)]
+        + [pltpu.SemaphoreType.DMA((3,)), pltpu.SemaphoreType.DMA((3, total // tile))]
+        + [pltpu.SemaphoreType.DMA],
         compiler_params=pltpu.CompilerParams(vmem_limit_bytes=vmem_limit),
         name="mlp",
-    )(normed, cotangent, hidden_grad, first_units, first_units, down_units)
+    )(normed, cotangent, hidden_grad, first_units, down_units)
 
 
 def body(
@@ -827,7 +895,7 @@
     (column_parts,) = local_kernel(
         functools.partial(split_columns_kernel, width, wide),
         "split_columns",
-        (input_weight, branch_weight, output_weight, mixer_gain[:, None], mlp_gain[:, None]),
+        (input_weight, branch_weight, output_weight, mixer_gain[None], mlp_gain[None]),
         [((n_blk, shard, 3 * wide), bf16)],
     )
     columns = swap_blk(column_parts).reshape(n_blk * shard, 3 * wide)
@@ -886,9 +954,12 @@
         signal, masks, vectors, weights, tiles
     )
     mixed = (gelu_tanh(branch_pre) * state_values.astype(f32)).astype(bf16)
-    mid_partial = mm(mixed, output_columns, ((1,), (1,))).astype(bf16)
-    mid_partial, out_grad = tie(mid_partial, out_grad)
-    mid_parts = ring_sum(mid_partial, n_blk)
+    before = (blk + n_blk - 1) % n_blk * tok_count
+    first = lax.dynamic_slice_in_dim(mixed, before, tok_count, axis=0)
+    first = mm(first, output_columns, ((1,), (1,))).astype(bf16)
+    first, mixed_all, out_grad = tie(first, mixed, out_grad)
+    mid_partial = mm(mixed_all, output_columns, ((1,), (1,))).astype(bf16)
+    mid_parts = ring_sum(mid_partial, n_blk, first)
     residual_mid, own_normed = local_kernel(
         mid_norm_kernel,
         "mid_norm",
@@ -928,7 +999,8 @@
     early_sum = lax.psum_scatter(
         early_sum.reshape(-1, wide), "rows", scatter_dimension=0, tiled=True
     ).reshape(early_shape)
-    late_sum, sums, gain_sums, gate_sums, token_sent = mixer_backward(
+    away, keep, vector_sums, gain_sums, gate_sums, token_sent = mixer_backward(
+        (row % 2).astype(jnp.int32)[None],
         (state_grad, branch_grad, masks, vectors, mlp_gain_part),
         (
             signal,
@@ -946,12 +1018,13 @@
         tiles,
         (2, heads, block, block),
     )
-    token_sent, out_parts, unit_sums, late_sum, sums, gain_sums, gate_sums = tie(
-        token_sent, out_parts, unit_sums, late_sum, sums, gain_sums, gate_sums
+    token_sent, out_parts, unit_sums, away, keep, vector_sums, gain_sums, gate_sums = tie(
+        token_sent, out_parts, unit_sums, away, keep, vector_sums, gain_sums, gate_sums
     )
     token_parts = swap_blk(token_sent)
-    vector_sums = sums.reshape(8, 8, wide).sum(axis=1)
-    late_sum, (vector_sums, gain_sums) = sum_columns(late_sum, n_rows, [vector_sums, gain_sums])
+    late_sum, (vector_sums, gain_sums) = sum_columns(
+        away, keep, n_rows, [vector_sums, gain_sums]
+    )
     column_sums = jnp.concatenate([early_sum, late_sum], axis=1)
     gate_sums = [add_from(gate_sums[number], n_rows, 1, bf16) for number in range(2)]
     *gate_sums, token_parts, column_sums, gain_sums = tie(

time: 532 us -> 533 us (level)
  waiting for transfers between devices: 272 us -> 280 us
    reduce_scatter x1, waiting for transfers between devices: 6.67 us -> 14.7 us  [body(): lax.psum_scatter(early_sum.reshape(-1, wide), 'rows', scatter_dimension=0...]
    dot_general x3 -> x4, matrix products: 16 us -> 19.9 us  [mm(): lax.dot_general(left, right, (dims, ((), ())), preferred_element_type=f32)]
    ppermute x5 -> x4, waiting for transfers between devices: 16.5 us -> 19.1 us  [halve(): got = lax.ppermute(away, 'rows', flip(size, bit))]
    unnamed x68 -> x64, local copies, waits for them, and re-layouts: 12.5 us -> 12.5 us
  transfers between devices with their start and end apart: 45 -> 45, of which waited for: 32 -> 30; matrix products, arithmetic and copies ran while one was open for 12% -> 11% of each run, Pallas kernels for 16% -> 16%
where the time goes in v5:
time: 533 us; the launch traced here: 524 us
  waiting for transfers between devices  280 us (53%)
  Pallas kernels  122 us (23%)
  starting transfers between devices  44 us (8%)
  local copies, waits for them, and re-layouts  25.8 us (5%)
  matrix products  19.9 us (4%)
  other arithmetic  17.6 us (3%)
  between operations  15.4 us (3%)
    ppermute x9, waiting for transfers between devices, ring_blk(): lax.ppermute(part, 'blk', [(place, (place + 1) % size) for place in range...  111 us
    ppermute x6, waiting for transfers between devices, ring_sum(): lax.ppermute(total, 'blk', [(place, (place + 1) % size) for place in rang...  75.7 us
    pallas_call x8, Pallas kernels, local_kernel(): pl.pallas_call(kernel, out_shape=[jax.ShapeDtypeStruct(shape, kind) for s...  44.2 us
    pallas_call x1, Pallas kernels, mlp(): pl.pallas_call(mlp_kernel, grid=(total // tile,), out_shape=[whole, whole...  37.7 us
    pallas_call x1, Pallas kernels, mixer_backward(): pl.pallas_call(functools.partial(mixer_backward_kernel, tiles), out_shape...  32.1 us
    all_to_all x5, waiting for transfers between devices, swap_blk(): return lax.all_to_all(parts, 'blk', split_axis=0, concat_axis=0, tiled=True)  24.6 us
    all_to_all x5, starting transfers between devices, swap_blk(): return lax.all_to_all(parts, 'blk', split_axis=0, concat_axis=0, tiled=True)  22.8 us
    dot_general x4, matrix products, mm(): lax.dot_general(left, right, (dims, ((), ())), preferred_element_type=f32)  19.9 us
  transfers between devices with their start and end apart: 45, of which 30 were waited for; matrix products, arithmetic and copies ran while one was open for 11% of the time, Pallas kernels for 16%

profile of v5, /device:TPU:0, one launch (start us, length us, event | category | flops | bytes accessed | tf_op | source)
XLA Modules:
  0.0 524.2 jit_solution(16466231127594581500)
XLA Ops:
  10.6 6.3 %all-to-all-start = ((bf16[4,64,2304]{2,1,0:T(8,128)(2,1)}), bf16[4,64,2304]{2,1,0:T(8,128)(2,1)S(1)}, u32[]{:S(2)}, u32[]{:S(2)}) async-start(bf16[4,64,2304]{2,1,0:T(8,128)(2,1)} %split_columns.1), calls=%async_computation | async-start | bytes 2359296 | tf_op jit(solution)/shard_map/all_to_all | solution.py:61
  25.7 19.8 %all-to-all-done = bf16[4,64,2304]{2,1,0:T(8,128)(2,1)S(1)} async-done(((bf16[4,64,2304]{2,1,0:T(8,128)(2,1)}), bf16[4,64,2304]{2,1,0:T(8,128)(2,1)S(1)}, u32[]{:S(2)}, u32[]{:S(2)}) %all-to-all-start) | async-done | bytes 1179680 | tf_op jit(solution)/shard_map/all_to_all | solution.py:61
  49.0 14.7 %collective-permute-done = bf16[128,2048]{1,0:T(8,128)(2,1)S(1)} collective-permute-done((bf16[128,2048]{1,0:T(8,128)(2,1)S(1)}, bf16[128,2048]{1,0:T(8,128)(2,1)S(1)}, u32[]{:S(2)}, u32[]{:S(2)}) %collective-permute-start) | collective-permute-done | bytes 524320 | tf_op jit(solution)/shard_map/ppermute | solution.py:69
  63.6 13.9 %collective-permute-done.1 = bf16[128,2048]{1,0:T(8,128)(2,1)} collective-permute-done((bf16[128,2048]{1,0:T(8,128)(2,1)S(1)}, bf16[128,2048]{1,0:T(8,128)(2,1)}, u32[]{:S(2)}, u32[]{:S(2)}) %collective-permute-start.1) | collective-permute-done | bytes 524320 | tf_op jit(solution)/shard_map/ppermute | solution.py:69
  79.0 11.6 %collective-permute-done.2 = bf16[128,2048]{1,0:T(8,128)(2,1)S(1)} collective-permute-done((bf16[128,2048]{1,0:T(8,128)(2,1)}, bf16[128,2048]{1,0:T(8,128)(2,1)S(1)}, u32[]{:S(2)}, u32[]{:S(2)}) %collective-permute-start.2) | collective-permute-done | bytes 524320 | tf_op jit(solution)/shard_map/ppermute | solution.py:69
  91.9 4.5 all-to-all-start.1
  98.8 7.4 %all-gather.7.cloned.1.call-done.columns_ref.both_any = bf16[2048,1536]{1,0:T(8,128)(2,1)} async-done(((bf16[256,1536]{1,0:T(8,128)(2,1)}), bf16[2048,1536]{1,0:T(8,128)(2,1)}) %all-gather.7.cloned.1.call-update) | async-done | bytes 6291472 | tf_op jit(solution)/shard_map/all_gather | solution.py:913
  106.2 8.9 %mixer_in.1 = (bf16[512,2048]{1,0:T(8,128)(2,1)}, bf16[512,768]{1,0:T(8,128)(2,1)}, f32[512,768]{1,0:T(8,128)}, f32[2,2048]{1,0:T(2,128)}) custom-call(bf16[512,2048]{1,0:T(8,128)(2,1)} %copy-done, bf16[2048,1536]{1,0:T(8,128)(2,1)} %all-gather.7.cloned.1.call-done.columns_ref.both_any), custom_call_target="tpu_custom_call" | custom-call | tf_op jit(solution)/shard_map/mixer_in/pallas_call | solution.py:246
  115.1 14.9 %recur_forward.1 = (f32[512,768]{1,0:T(8,128)}, bf16[512,768]{1,0:T(8,128)(2,1)}, f32[512,768]{1,0:T(8,128)}, f32[512,768]{1,0:T(8,128)}, f32[512,768]{1,0:T(8,128)}) custom-call(bf16[512,768]{1,0:T(8,128)(2,1)} %get-tuple-element.104.signal_ref.signal_any, f32[520,8]{1,0:T(8,128)} %pad.12.masks_ref, f32[8,768]{1,0:T(8,128)} %pad.13.vectors_ref, ...), custom_call_target="tpu_custom_call" | custom-call | tf_op jit(solution)/shard_map/recur_forward/pallas_call | solution.py:246
  131.8 9.2 %all-gather.9.cloned.1.call-done = bf16[2048,768]{1,0:T(8,128)(2,1)} async-done(((bf16[256,768]{1,0:T(8,128)(2,1)}), bf16[2048,768]{1,0:T(8,128)(2,1)}) %all-gather.9.cloned.1.call-update) | async-done | bytes 3145744 | tf_op jit(solution)/shard_map/all_gather | solution.py:914
  150.1 10.9 %collective-permute-done.3 = bf16[128,2048]{1,0:T(8,128)(2,1)S(1)} collective-permute-done((bf16[128,2048]{1,0:T(8,128)(2,1)}, bf16[128,2048]{1,0:T(8,128)(2,1)S(1)}, u32[]{:S(2)}, u32[]{:S(2)}) %collective-permute-start.3) | collective-permute-done | bytes 524320 | tf_op jit(solution)/shard_map/ppermute | solution.py:82
  161.2 15.0 %collective-permute-done.4 = bf16[128,2048]{1,0:T(8,128)(2,1)S(1)} collective-permute-done((bf16[128,2048]{1,0:T(8,128)(2,1)S(1)}, bf16[128,2048]{1,0:T(8,128)(2,1)S(1)}, u32[]{:S(2)}, u32[]{:S(2)}) %collective-permute-start.4) | collective-permute-done | bytes 524320 | tf_op jit(solution)/shard_map/ppermute | solution.py:82
  177.8 12.7 %collective-permute-done.5.one_ref = bf16[128,2048]{1,0:T(8,128)(2,1)S(1)} collective-permute-done((bf16[128,2048]{1,0:T(8,128)(2,1)S(1)}, bf16[128,2048]{1,0:T(8,128)(2,1)S(1)}, u32[]{:S(2)}, u32[]{:S(2)}) %collective-permute-start.5) | collective-permute-done | bytes 524320 | tf_op jit(solution)/shard_map/ppermute | solution.py:82
  194.1 13.4 %collective-permute-done.6 = bf16[128,2048]{1,0:T(8,128)(2,1)S(1)} collective-permute-done((bf16[128,2048]{1,0:T(8,128)(2,1)}, bf16[128,2048]{1,0:T(8,128)(2,1)S(1)}, u32[]{:S(2)}, u32[]{:S(2)}) %collective-permute-start.6) | collective-permute-done | bytes 524320 | tf_op jit(solution)/shard_map/ppermute | solution.py:69
  207.7 8.6 %fusion.27.hidden_grad_ref = f32[512,1536]{1,0:T(8,128)} fusion(bf16[512,2048]{1,0:T(8,128)(2,1)} %bitcast.10.cotangent_any, bf16[1536,2048]{1,0:T(8,128)(2,1)} %all-gather.5.cloned.1.call-done.down_any), kind=kOutput, calls=%fused_computation.95 | convolution fusion | flops 3221225472 | bytes 11534336 | tf_op jit(solution)/shard_map/dot_general | solution.py:36
  220.4 10.9 %collective-permute-done.8 = bf16[128,2048]{1,0:T(8,128)(2,1)S(1)} collective-permute-done((bf16[128,2048]{1,0:T(8,128)(2,1)S(1)}, bf16[128,2048]{1,0:T(8,128)(2,1)S(1)}, u32[]{:S(2)}, u32[]{:S(2)}) %collective-permute-start.8) | collective-permute-done | bytes 524320 | tf_op jit(solution)/shard_map/ppermute | solution.py:69
  232.8 37.7 %mlp.1 = (bf16[512,2048]{1,0:T(8,128)(2,1)}, bf16[512,2048]{1,0:T(8,128)(2,1)}, bf16[8,3,192,2048]{3,2,1,0:T(8,128)(2,1)}) custom-call(bf16[512,2048]{1,0:T(8,128)(2,1)} %copy-done.1, bf16[512,2048]{1,0:T(8,128)(2,1)} %bitcast.10.cotangent_any, f32[512,1536]{1,0:T(8,128)} %fusion.27.hidden_grad_ref, bf16[8,2,192,2048]{3,2,1,0:T(8,128)(2,1)} %bitcast.62, ...), custom_call_target="tpu_custom_call" | custom-call | tf_op jit(solution)/shard_map/mlp/pallas_call | solution.py:837
  272.9 12.4 %collective-permute-done.9 = bf16[128,2048]{1,0:T(8,128)(2,1)S(1)} collective-permute-done((bf16[128,2048]{1,0:T(8,128)(2,1)S(1)}, bf16[128,2048]{1,0:T(8,128)(2,1)S(1)}, u32[]{:S(2)}, u32[]{:S(2)}) %collective-permute-start.9) | collective-permute-done | bytes 524320 | tf_op jit(solution)/shard_map/ppermute | solution.py:82
  285.8 13.7 %collective-permute-done.10 = bf16[128,2048]{1,0:T(8,128)(2,1)S(1)} collective-permute-done((bf16[128,2048]{1,0:T(8,128)(2,1)S(1)}, bf16[128,2048]{1,0:T(8,128)(2,1)S(1)}, u32[]{:S(2)}, u32[]{:S(2)}) %collective-permute-start.10) | collective-permute-done | bytes 524320 | tf_op jit(solution)/shard_map/ppermute | solution.py:82
  299.7 11.0 %collective-permute-done.11.one_ref = bf16[128,2048]{1,0:T(8,128)(2,1)S(1)} collective-permute-done((bf16[128,2048]{1,0:T(8,128)(2,1)S(1)}, bf16[128,2048]{1,0:T(8,128)(2,1)S(1)}, u32[]{:S(2)}, u32[]{:S(2)}) %collective-permute-start.11) | collective-permute-done | bytes 524320 | tf_op jit(solution)/shard_map/ppermute | solution.py:82
  315.3 16.7 %collective-permute-done.12 = bf16[128,2048]{1,0:T(8,128)(2,1)S(1)} collective-permute-done((bf16[128,2048]{1,0:T(8,128)(2,1)}, bf16[128,2048]{1,0:T(8,128)(2,1)S(1)}, u32[]{:S(2)}, u32[]{:S(2)}) %collective-permute-start.12) | collective-permute-done | bytes 524320 | tf_op jit(solution)/shard_map/ppermute | solution.py:69
  332.0 15.7 %collective-permute-done.13 = bf16[128,2048]{1,0:T(8,128)(2,1)S(1)} collective-permute-done((bf16[128,2048]{1,0:T(8,128)(2,1)S(1)}, bf16[128,2048]{1,0:T(8,128)(2,1)S(1)}, u32[]{:S(2)}, u32[]{:S(2)}) %collective-permute-start.13) | collective-permute-done | bytes 524320 | tf_op jit(solution)/shard_map/ppermute | solution.py:69
  348.2 10.5 %collective-permute-done.14 = bf16[128,2048]{1,0:T(8,128)(2,1)S(1)} collective-permute-done((bf16[128,2048]{1,0:T(8,128)(2,1)S(1)}, bf16[128,2048]{1,0:T(8,128)(2,1)S(1)}, u32[]{:S(2)}, u32[]{:S(2)}) %collective-permute-start.14) | collective-permute-done | bytes 524320 | tf_op jit(solution)/shard_map/ppermute | solution.py:69
  362.6 7.9 %column_grads.1 = bf16[8,4,2,64,768]{4,3,2,1,0:T(8,128)(2,1)} custom-call(bf16[512,2048]{1,0:T(8,128)(2,1)} %copy-done.2, bf16[512,2048]{1,0:T(8,128)(2,1)} %get-tuple-element.127.normed_any.refs_1_, bf16[512,768]{1,0:T(8,128)(2,1)} %copy-done.5, bf16[512,768]{1,0:T(8,128)(2,1)} %get-tuple-element.222.branch_grad_ref.refs_3_), custom_call_target="tpu_custom_call" | custom-call | tf_op jit(solution)/shard_map/column_grads/pallas_call | solution.py:688
  374.2 32.1 %mixer_backward.1 = (bf16[4,4,1,64,768]{4,3,2,1,0:T(8,128)(2,1)}, bf16[4,4,1,64,768]{4,3,2,1,0:T(8,128)(2,1)}, f32[8,768]{1,0:T(8,128)}, f32[2,2048]{1,0:T(2,128...) custom-call(s32[1]{0:T(128)} %bitcast.11.core_ref, bf16[512,768]{1,0:T(8,128)(2,1)} %get-tuple-element.223.state_grad_ref, ...), custom_call_target="tpu_custom_call" | custom-call | tf_op jit(solution)/shard_map/mixer_backward/pallas_call | solution.py:656
  406.3 4.8 all-to-all-done.2
  413.6 4.7 all-to-all-start.3
  431.3 8.9 %collective-permute-done.19 = bf16[2,4,1,64,384]{4,3,1,2,0:T(8,128)(2,1)S(1)} collective-permute-done((bf16[2,4,1,64,384]{4,3,1,2,0:T(8,128)(2,1)S(1)}, bf16[2,4,1,64,384]{4,3,1,2,0:T(8,128)(2,1)S(1)}, u32[]{:S(2)}, u32[]{:S(2)}) %collective-permute-start.19) | collective-permute-done | bytes 393248 | tf_op jit(solution)/shard_map/ppermute | solution.py:98
  440.3 7.5 %collective-permute-done.18 = bf16[2,4,1,64,384]{4,3,1,0,2:T(8,128)(2,1)S(1)} collective-permute-done((bf16[2,4,1,64,384]{4,3,1,0,2:T(8,128)(2,1)S(1)}, bf16[2,4,1,64,384]{4,3,1,0,2:T(8,128)(2,1)S(1)}, u32[]{:S(2)}, u32[]{:S(2)}) %collective-permute-start.18) | collective-permute-done | bytes 393248 | tf_op jit(solution)/shard_map/ppermute | solution.py:98
  457.2 14.7 %reduce-scatter.5.cloned.1.call-done = bf16[512,768]{1,0:T(8,128)(2,1)} async-done(((bf16[4096,768]{1,0:T(8,128)(2,1)}), bf16[512,768]{1,0:T(8,128)(2,1)}) %reduce-scatter.5.cloned.1.call-update) | async-done | bytes 786448 | tf_op jit(solution)/shard_map/reduce_scatter | solution.py:999
  486.8 6.0 %collective-permute-done.28 = bf16[4,171,171]{2,1,0:T(8,128)(2,1)S(1)} collective-permute-done((bf16[4,171,171]{2,1,0:T(8,128)(2,1)S(1)}, bf16[4,171,171]{2,1,0:T(8,128)(2,1)S(1)}, u32[]{:S(2)}, u32[]{:S(2)}) %collective-permute-start.28) | collective-permute-done | bytes 233960 | tf_op jit(solution)/shard_map/ppermute | solution.py:122
  503.5 6.1 %collective-permute-done.33 = f32[2,2048]{1,0:T(2,128)S(1)} collective-permute-done((f32[2,2048]{1,0:T(2,128)S(1)}, f32[2,2048]{1,0:T(2,128)S(1)}, u32[]{:S(2)}, u32[]{:S(2)}) %collective-permute-start.33) | collective-permute-done | bytes 16416 | tf_op jit(solution)/shard_map/ppermute | solution.py:1040
  (226 shorter events, 115.7 us)
Async XLA Ops:
  7.2 56.5 %all-gather.5.cloned.1.call-start = ((), (), s32[]{:S(2)}) async-start(), calls=%async_computation.7 | async-start | bytes 7077888 | tf_op jit(solution)/shard_map/all_gather | solution.py:905
  10.6 34.9 %all-to-all-start = ((bf16[4,64,2304]{2,1,0:T(8,128)(2,1)}), bf16[4,64,2304]{2,1,0:T(8,128)(2,1)S(1)}, u32[]{:S(2)}, u32[]{:S(2)}) async-start(bf16[4,64,2304]{2,1,0:T(8,128)(2,1)} %split_columns.1), calls=%async_computation | async-start | bytes 2359296 | tf_op jit(solution)/shard_map/all_to_all | solution.py:61
  16.9 89.3 %all-gather.7.cloned.1.call-start = ((), (), s32[]{:S(2)}) async-start(), calls=%async_computation.8 | async-start | bytes 7077888 | tf_op jit(solution)/shard_map/all_gather | solution.py:913
  48.0 93.0 %all-gather.9.cloned.1.call-start = ((), (), s32[]{:S(2)}) async-start(), calls=%async_computation.9 | async-start | bytes 3538944 | tf_op jit(solution)/shard_map/all_gather | solution.py:914
  48.8 182.6 %all-gather.11.cloned.1.call-start = ((), (), s32[]{:S(2)}) async-start(), calls=%async_computation.10 | async-start | bytes 14155776 | tf_op jit(solution)/shard_map/all_gather | solution.py:918
  48.9 14.7 %collective-permute-start = (bf16[128,2048]{1,0:T(8,128)(2,1)S(1)}, bf16[128,2048]{1,0:T(8,128)(2,1)S(1)}, u32[]{:S(2)}, u32[]{:S(2)}) collective-permute-start(bf16[128,2048]{1,0:T(8,128)(2,1)S(1)} %bitcast.68), channel_id=1, source_target_pairs={{0,1},{1,2},{2,3},{3,0},{4,5},{5,6},{6,7},{7,4},{8,9},{9,10},{10,1... | collective-permute-start | bytes 1572872 | tf_op jit(solution)/shard_map/ppermute | solution.py:69
  63.6 13.9 %collective-permute-start.1 = (bf16[128,2048]{1,0:T(8,128)(2,1)S(1)}, bf16[128,2048]{1,0:T(8,128)(2,1)}, u32[]{:S(2)}, u32[]{:S(2)}) collective-permute-start(bf16[128,2048]{1,0:T(8,128)(2,1)S(1)} %collective-permute-done), channel_id=1, source_target_pairs={{0,1},{1,2},{2,3},{3,0},{4,5},{5,6},{6,7},{7,4},{8,9},{9,10},{10,1... | collective-permute-start | bytes 1572872 | tf_op jit(solution)/shard_map/ppermute | solution.py:69
  77.5 13.1 %collective-permute-start.2 = (bf16[128,2048]{1,0:T(8,128)(2,1)}, bf16[128,2048]{1,0:T(8,128)(2,1)S(1)}, u32[]{:S(2)}, u32[]{:S(2)}) collective-permute-start(bf16[128,2048]{1,0:T(8,128)(2,1)} %collective-permute-done.1), channel_id=1, source_target_pairs={{0,1},{1,2},{2,3},{3,0},{4,5},{5,6},{6,7},{7,4},{8,9},{9,10},{10,1... | collective-permute-start | bytes 1572872 | tf_op jit(solution)/shard_map/ppermute | solution.py:69
  91.9 52.9 %all-to-all-start.1 = ((bf16[4,128,2048]{2,1,0:T(8,128)(2,1)}), bf16[4,128,2048]{2,1,0:T(8,128)(2,1)}, u32[]{:S(2)}, u32[]{:S(2)}) async-start(bf16[4,128,2048]{2,1,0:T(8,128)(2,1)} %broadcast_in_dim.35), calls=%async_computation.1 | async-start | bytes 4194304 | tf_op jit(solution)/shard_map/all_to_all | solution.py:61
  96.4 314.7 %reduce-scatter.3.cloned.1.call-start = ((), (), s32[]{:S(2)}) async-start(), calls=%async_computation.11 | async-start | bytes 21233664 | tf_op jit(solution)/shard_map/reduce_scatter | solution.py:976
  144.8 16.1 %collective-permute-start.3 = (bf16[128,2048]{1,0:T(8,128)(2,1)}, bf16[128,2048]{1,0:T(8,128)(2,1)S(1)}, u32[]{:S(2)}, u32[]{:S(2)}) collective-permute-start(bf16[128,2048]{1,0:T(8,128)(2,1)} %convolution_convert_fusion.1), channel_id=1, source_target_pairs={{0,1},{1,2},{2,3},{3,0},{4,5},{5,6},{6,7},{7,4},{8,9},{9,10},{10,1... | collective-permute-start | bytes 1572872 | tf_op jit(solution)/shard_map/ppermute | solution.py:82
  161.1 15.1 %collective-permute-start.4 = (bf16[128,2048]{1,0:T(8,128)(2,1)S(1)}, bf16[128,2048]{1,0:T(8,128)(2,1)S(1)}, u32[]{:S(2)}, u32[]{:S(2)}) collective-permute-start(bf16[128,2048]{1,0:T(8,128)(2,1)S(1)} %add_convert_fusion.5), channel_id=1, source_target_pairs={{0,1},{1,2},{2,3},{3,0},{4,5},{5,6},{6,7},{7,4},{8,9},{9,10},{10,1... | collective-permute-start | bytes 1572872 | tf_op jit(solution)/shard_map/ppermute | solution.py:82
  176.3 14.2 %collective-permute-start.5 = (bf16[128,2048]{1,0:T(8,128)(2,1)S(1)}, bf16[128,2048]{1,0:T(8,128)(2,1)S(1)}, u32[]{:S(2)}, u32[]{:S(2)}) collective-permute-start(bf16[128,2048]{1,0:T(8,128)(2,1)S(1)} %add_convert_fusion.4), channel_id=1, source_target_pairs={{0,1},{1,2},{2,3},{3,0},{4,5},{5,6},{6,7},{7,4},{8,9},{9,10},{10,1... | collective-permute-start | bytes 1572872 | tf_op jit(solution)/shard_map/ppermute | solution.py:82
  194.1 13.4 %collective-permute-start.6 = (bf16[128,2048]{1,0:T(8,128)(2,1)}, bf16[128,2048]{1,0:T(8,128)(2,1)S(1)}, u32[]{:S(2)}, u32[]{:S(2)}) collective-permute-start(bf16[128,2048]{1,0:T(8,128)(2,1)} %get-tuple-element.114), channel_id=1, source_target_pairs={{0,1},{1,2},{2,3},{3,0},{4,5},{5,6},{6,7},{7,4},{8,9},{9,10},{10,1... | collective-permute-start | bytes 1572872 | tf_op jit(solution)/shard_map/ppermute | solution.py:69
  207.5 12.5 %collective-permute-start.7 = (bf16[128,2048]{1,0:T(8,128)(2,1)S(1)}, bf16[128,2048]{1,0:T(8,128)(2,1)S(1)}, u32[]{:S(2)}, u32[]{:S(2)}) collective-permute-start(bf16[128,2048]{1,0:T(8,128)(2,1)S(1)} %collective-permute-done.6), channel_id=1, source_target_pairs={{0,1},{1,2},{2,3},{3,0},{4,5},{5,6},{6,7},{7,4},{8,9},{9,10},{10,1... | collective-permute-start | bytes 1572872 | tf_op jit(solution)/shard_map/ppermute | solution.py:69
  220.0 11.4 %collective-permute-start.8 = (bf16[128,2048]{1,0:T(8,128)(2,1)S(1)}, bf16[128,2048]{1,0:T(8,128)(2,1)S(1)}, u32[]{:S(2)}, u32[]{:S(2)}) collective-permute-start(bf16[128,2048]{1,0:T(8,128)(2,1)S(1)} %collective-permute-done.7), channel_id=1, source_target_pairs={{0,1},{1,2},{2,3},{3,0},{4,5},{5,6},{6,7},{7,4},{8,9},{9,10},{10,1... | collective-permute-start | bytes 1572872 | tf_op jit(solution)/shard_map/ppermute | solution.py:69
  270.5 201.4 %reduce-scatter.5.cloned.1.call-start = ((), (), s32[]{:S(2)}) async-start(), calls=%async_computation.12 | async-start | bytes 7077888 | tf_op jit(solution)/shard_map/reduce_scatter | solution.py:999
  272.9 12.4 %collective-permute-start.9 = (bf16[128,2048]{1,0:T(8,128)(2,1)S(1)}, bf16[128,2048]{1,0:T(8,128)(2,1)S(1)}, u32[]{:S(2)}, u32[]{:S(2)}) collective-permute-start(bf16[128,2048]{1,0:T(8,128)(2,1)S(1)} %get-tuple-element.228), channel_id=1, source_target_pairs={{0,1},{1,2},{2,3},{3,0},{4,5},{5,6},{6,7},{7,4},{8,9},{9,10},{10,1... | collective-permute-start | bytes 1572872 | tf_op jit(solution)/shard_map/ppermute | solution.py:82
  285.5 14.0 %collective-permute-start.10 = (bf16[128,2048]{1,0:T(8,128)(2,1)S(1)}, bf16[128,2048]{1,0:T(8,128)(2,1)S(1)}, u32[]{:S(2)}, u32[]{:S(2)}) collective-permute-start(bf16[128,2048]{1,0:T(8,128)(2,1)S(1)} %add_convert_fusion.3), channel_id=1, source_target_pairs={{0,1},{1,2},{2,3},{3,0},{4,5},{5,6},{6,7},{7,4},{8,9},{9,10},{10,1... | collective-permute-start | bytes 1572872 | tf_op jit(solution)/shard_map/ppermute | solution.py:82
  315.3 16.7 %collective-permute-start.12 = (bf16[128,2048]{1,0:T(8,128)(2,1)}, bf16[128,2048]{1,0:T(8,128)(2,1)S(1)}, u32[]{:S(2)}, u32[]{:S(2)}) collective-permute-start(bf16[128,2048]{1,0:T(8,128)(2,1)} %get-tuple-element.119), channel_id=1, source_target_pairs={{0,1},{1,2},{2,3},{3,0},{4,5},{5,6},{6,7},{7,4},{8,9},{9,10},{10,1... | collective-permute-start | bytes 1572872 | tf_op jit(solution)/shard_map/ppermute | solution.py:69
  332.0 15.7 %collective-permute-start.13 = (bf16[128,2048]{1,0:T(8,128)(2,1)S(1)}, bf16[128,2048]{1,0:T(8,128)(2,1)S(1)}, u32[]{:S(2)}, u32[]{:S(2)}) collective-permute-start(bf16[128,2048]{1,0:T(8,128)(2,1)S(1)} %collective-permute-done.12), channel_id=1, source_target_pairs={{0,1},{1,2},{2,3},{3,0},{4,5},{5,6},{6,7},{7,4},{8,9},{9,10},{10,1... | collective-permute-start | bytes 1572872 | tf_op jit(solution)/shard_map/ppermute | solution.py:69
  370.5 40.6 %all-to-all-start.2 = ((bf16[4,128,2048]{2,1,0:T(8,128)(2,1)}), bf16[4,128,2048]{2,1,0:T(8,128)(2,1)S(1)}, u32[]{:S(2)}, u32[]{:S(2)}) async-start(bf16[4,128,2048]{2,1,0:T(8,128)(2,1)} %bitcast.72), calls=%async_computation.2 | async-start | bytes 4194304 | tf_op jit(solution)/shard_map/all_to_all | solution.py:61
  411.1 13.8 %collective-permute-start.22 = (f32[2,2048]{1,0:T(2,128)}, f32[2,2048]{1,0:T(2,128)S(1)}, u32[]{:S(2)}, u32[]{:S(2)}) collective-permute-start(f32[2,2048]{1,0:T(2,128)} %get-tuple-element.143), channel_id=1, source_target_pairs={{0,4},{4,0},{8,12},{12,8},{16,20},{20,16},{24,28},{28,24},{1,5},{5... | collective-permute-start | bytes 49160 | tf_op jit(solution)/shard_map/ppermute | solution.py:122
  411.6 15.1 %collective-permute-start.20 = (f32[8,768]{1,0:T(8,128)}, f32[8,768]{1,0:T(8,128)S(1)}, u32[]{:S(2)}, u32[]{:S(2)}) collective-permute-start(f32[8,768]{1,0:T(8,128)} %get-tuple-element.142), channel_id=1, source_target_pairs={{0,4},{4,0},{8,12},{12,8},{16,20},{20,16},{24,28},{28,24},{1,5},{5... | collective-permute-start | bytes 73736 | tf_op jit(solution)/shard_map/ppermute | solution.py:122
  413.1 36.0 %collective-permute-start.15 = (bf16[4,171,171]{2,1,0:T(8,128)(2,1)S(1)}, bf16[4,171,171]{2,1,0:T(8,128)(2,1)S(1)}, u32[]{:S(2)}, u32[]{:S(2)}) collective-permute-start(bf16[4,171,171]{2,1,0:T(8,128)(2,1)S(1)} %get-tuple-element.234), channel_id=1, source_target_pairs={{0,4},{4,0},{8,12},{12,8},{16,20},{20,16},{24,28},{28,24},{1,5},{5... | collective-permute-start | bytes 701792 | tf_op jit(solution)/shard_map/ppermute | solution.py:122
  413.6 60.5 %all-to-all-start.3 = ((bf16[4,128,2048]{2,1,0:T(8,128)(2,1)}), bf16[4,128,2048]{2,1,0:T(8,128)(2,1)}, u32[]{:S(2)}, u32[]{:S(2)}) async-start(bf16[4,128,2048]{2,1,0:T(8,128)(2,1)} %get-tuple-element.139), calls=%async_computation.4 | async-start | bytes 4194304 | tf_op jit(solution)/shard_map/all_to_all | solution.py:61
  421.1 19.1 %collective-permute-start.19 = (bf16[2,4,1,64,384]{4,3,1,2,0:T(8,128)(2,1)S(1)}, bf16[2,4,1,64,384]{4,3,1,2,0:T(8,128)(2,1)S(1)}, u32[]{:S(2)}, u32[]{:S(2)}) collective-permute-start(bf16[2,4,1,64,384]{4,3,1,2,0:T(8,128)(2,1)S(1)} %dynamic-slice_bitcast_fusion), channel_id=1, source_target_pairs={{0,16},{4,20},{8,24},{12,28},{16,0},{20,4},{24,8},{28,12},{1,17},{... | collective-permute-start | bytes 1179656 | tf_op jit(solution)/shard_map/ppermute | solution.py:98
  427.1 20.7 %collective-permute-start.18 = (bf16[2,4,1,64,384]{4,3,1,0,2:T(8,128)(2,1)S(1)}, bf16[2,4,1,64,384]{4,3,1,0,2:T(8,128)(2,1)S(1)}, u32[]{:S(2)}, u32[]{:S(2)}) collective-permute-start(bf16[2,4,1,64,384]{4,3,1,0,2:T(8,128)(2,1)S(1)} %dynamic-slice_bitcast_fusion.1), channel_id=1, source_target_pairs={{0,8},{4,12},{8,0},{12,4},{16,24},{20,28},{24,16},{28,20},{1,9},{5... | collective-permute-start | bytes 1179656 | tf_op jit(solution)/shard_map/ppermute | solution.py:98
  430.3 18.8 %collective-permute-start.16 = (bf16[4,171,171]{2,1,0:T(8,128)(2,1)S(1)}, bf16[4,171,171]{2,1,0:T(8,128)(2,1)S(1)}, u32[]{:S(2)}, u32[]{:S(2)}) collective-permute-start(bf16[4,171,171]{2,1,0:T(8,128)(2,1)S(1)} %get-tuple-element.233), channel_id=1, source_target_pairs={{0,4},{4,0},{8,12},{12,8},{16,20},{20,16},{24,28},{28,24},{1,5},{5... | collective-permute-start | bytes 701792 | tf_op jit(solution)/shard_map/ppermute | solution.py:122
  477.1 35.9 %all-to-all-start.4 = ((bf16[4,3,64,768]{3,2,1,0:T(8,128)(2,1)}), bf16[4,3,64,768]{3,2,1,0:T(8,128)(2,1)S(1)}, u32[]{:S(2)}, u32[]{:S(2)}) async-start(bf16[4,3,64,768]{3,2,1,0:T(8,128)(2,1)} %maximum_maximum_fusion), calls=%async_computation.6 | async-start | bytes 2359296 | tf_op jit(solution)/shard_map/all_to_all | solution.py:61
  493.0 16.7 %collective-permute-start.32 = (bf16[4,171,171]{2,1,0:T(8,128)(2,1)S(1)}, bf16[4,171,171]{2,1,0:T(8,128)(2,1)S(1)}, u32[]{:S(2)}, u32[]{:S(2)}) collective-permute-start(bf16[4,171,171]{2,1,0:T(8,128)(2,1)S(1)} %convert_element_type.270), channel_id=1, source_target_pairs={{0,8},{4,12},{8,0},{12,4},{16,24},{20,28},{24,16},{28,20},{1,9},{5... | collective-permute-start | bytes 701792 | tf_op jit(solution)/shard_map/ppermute | solution.py:122
  494.3 15.3 %collective-permute-start.33 = (f32[2,2048]{1,0:T(2,128)S(1)}, f32[2,2048]{1,0:T(2,128)S(1)}, u32[]{:S(2)}, u32[]{:S(2)}) collective-permute-start(f32[2,2048]{1,0:T(2,128)S(1)} %add.292), channel_id=1, source_target_pairs={{0,2},{1,3},{2,0},{3,1},{4,6},{5,7},{6,4},{7,5},{8,10},{9,11},{10,... | collective-permute-start | bytes 49160 | tf_op jit(solution)/shard_map/ppermute | solution.py:1040
  (43 other events, 357.6 us)
Sparse Core Ops, SparseCore 0:
  9.9 48.2 all-gather.4
  60.6 45.5 all-gather.6
  108.6 32.3 all-gather.8
  142.8 72.1 all-gather.10
  270.6 123.3 reduce-scatter.2
  397.2 74.6 reduce-scatter.4
